TPU v7x, 512 devices: a whole 4x8x8 slice. The times are simulated.
512 devices in a mesh: cam: 8 (over z_lo, x), frame: 64 (over z_hi, y, core).
Axes of the slice: x: 4, y: 8, z: 8 (z_hi: 4, z_lo: 2; z = z_hi * 2 + z_lo), core: 2. Of those that a mesh axis runs over, the one named last changes fastest.
Arguments:
- queries: bfloat16 [8, 64, 256, 1024], P('cam', 'frame'), may hold values from -8 to 8
- key_vectors: bfloat16 [8, 64, 256, 1024], P('cam', 'frame'), may hold values from -8 to 8
- value_vectors: bfloat16 [8, 64, 256, 1024], P('cam', 'frame'), may hold values from -6 to 6
- out_grad: bfloat16 [8, 64, 256, 1024], P('cam', 'frame'), may hold values from -6 to 6
- valid_count: int32 [8, 64], P('cam', 'frame'), may hold values from 128 to 256, as said below
Outputs:
- attended: bfloat16 [8, 64, 256, 1024], P('cam', 'frame')
- grad_queries: bfloat16 [8, 64, 256, 1024], P('cam', 'frame')
- grad_keys: bfloat16 [8, 64, 256, 1024], P('cam', 'frame')
- grad_values: bfloat16 [8, 64, 256, 1024], P('cam', 'frame')
Inputs may be any that keep to these rules, and one draw needn't show every extreme that they name: `valid_count`: every camera has a frame whose 256 tokens are all valid.
All inputs are finite; a program needn't handle non-finite values.
Results may differ from a plain program's by a relative error of at most 0.0092.
Values may be sent and summed in bfloat16 or wider, within the bound.
No kernel may reach another device: no remote copies, remote signals or barrier semaphores. Data moves between devices by JAX's collectives and lax.ppermute only.
A program may use at most 128 MiB of HBM per device.

v0:
```python
import jax
import jax.numpy as jnp
from jax import lax
from jax.sharding import PartitionSpec as P

HEAD_DIM = 64


CROSS_FORMS = ("rhe", "mhe", "hrm")
TIME_FORMS = ("fnhe", "gnhe", "nhfg")


def from_behind(shard, axis, by):
    devices = lax.axis_size(axis)
    return lax.ppermute(shard, axis, [(i, (i + by) % devices) for i in range(devices)])


def take_heads(matrix, column_start):
    sliced = lax.dynamic_slice_in_dim(matrix, column_start, 128, matrix.ndim - 1)
    return sliced.reshape(sliced.shape[:-1] + (128 // HEAD_DIM, HEAD_DIM))


def put_heads(target, sliced, column_start):
    flattened = sliced.reshape(sliced.shape[:-2] + (sliced.shape[-2] * sliced.shape[-1],))
    return lax.dynamic_update_slice_in_dim(target, flattened, column_start, target.ndim - 1)


def attend_heads(query_part, key_part, value_part, grad_part, keep_mask, subscripts):
    query_subs, key_subs, score_subs = subscripts
    score_scale = HEAD_DIM ** (-0.5)
    to_score = query_subs + "," + key_subs + "->" + score_subs
    to_query = score_subs + "," + key_subs + "->" + query_subs
    scores = (
        jnp.einsum(to_score, query_part, key_part, preferred_element_type=jnp.float32) * score_scale
    )
    scores = jnp.where(keep_mask, scores, -jnp.inf)
    row_max = jnp.max(scores, axis=-1, keepdims=True)
    shifted = jnp.exp(scores - row_max)
    row_total = jnp.sum(shifted, axis=-1, keepdims=True)
    attn_probs = shifted / row_total
    probs_low = attn_probs.astype(jnp.bfloat16)
    output = jnp.einsum(to_query, probs_low, value_part, preferred_element_type=jnp.float32)
    grad_probs = jnp.einsum(to_score, grad_part, value_part, preferred_element_type=jnp.float32)
    row_delta = jnp.sum(attn_probs * grad_probs, axis=-1, keepdims=True)
    grad_scores = (attn_probs * (grad_probs - row_delta)).astype(jnp.bfloat16)
    grad_query = (
        jnp.einsum(to_query, grad_scores, key_part, preferred_element_type=jnp.float32)
        * score_scale
    )
    to_key = score_subs + "," + query_subs + "->" + key_subs
    grad_key = (
        jnp.einsum(to_key, grad_scores, query_part, preferred_element_type=jnp.float32)
        * score_scale
    )
    grad_value = jnp.einsum(to_key, probs_low, grad_part, preferred_element_type=jnp.float32)
    return (output, grad_query, grad_key, grad_value)


def run_groups(query_rows, key_rows, value_rows, grad_rows, keep_mask, subscripts):
    groups = query_rows.shape[-1] // 128
    zeros_query = jnp.zeros(query_rows.shape, jnp.float32)
    zeros_key = jnp.zeros(key_rows.shape, jnp.float32)
    initial = (zeros_query, zeros_query, zeros_key, zeros_key)

    def visit_group(head_group, carried):
        column_start = head_group * 128
        results = attend_heads(
            take_heads(query_rows, column_start),
            take_heads(key_rows, column_start),
            take_heads(value_rows, column_start),
            take_heads(grad_rows, column_start),
            keep_mask,
            subscripts,
        )
        output = put_heads(carried[0], results[0], column_start)
        grad_query = put_heads(carried[1], results[1], column_start)
        return (
            output,
            grad_query,
            put_heads(carried[2], results[2], column_start),
            put_heads(carried[3], results[3], column_start),
        )

    return lax.fori_loop(0, groups, visit_group, initial)


def temporal_items(pieces):
    query_part = pieces[0][:, 0]
    key_part = pieces[1][:, 0]
    value_part = pieces[2][:, 0]
    grad_part = pieces[3][:, 0]
    keep_part = pieces[4][:, 0]
    keep_mask = (jnp.transpose(keep_part) > 0)[:, None, None, :]
    results = run_groups(query_part, key_part, value_part, grad_part, keep_mask, TIME_FORMS)
    return tuple((result.astype(jnp.bfloat16)[:, None] for result in results))


def on_device(queries, key_vectors, value_vectors, out_grad, valid_count):
    query_rows = queries[0, 0]
    key_rows = key_vectors[0, 0]
    value_rows = value_vectors[0, 0]
    grad_rows = out_grad[0, 0]
    length = query_rows.shape[0]
    width = query_rows.shape[1]
    frame_count = lax.axis_size("frame")
    per_frame = length // frame_count
    positions = jnp.arange(length, dtype=jnp.int32)
    own_keep = positions < valid_count[0, 0]
    keep_low = own_keep.astype(jnp.bfloat16)
    from_lower = from_behind((key_rows, value_rows, keep_low), "cam", 1)
    from_upper = from_behind((key_rows, value_rows, keep_low), "cam", -1)
    key_set = jnp.concatenate([from_lower[0], key_rows, from_upper[0]], axis=0)
    value_set = jnp.concatenate([from_lower[1], value_rows, from_upper[1]], axis=0)
    keep_set = jnp.concatenate([from_lower[2] > 0, own_keep, from_upper[2] > 0])
    cross_out, cross_query, cross_key, cross_value = run_groups(
        query_rows, key_set, value_set, grad_rows, keep_set, CROSS_FORMS
    )
    upper_grads = from_behind((cross_key[:length], cross_value[:length]), "cam", -1)
    lower_grads = from_behind((cross_key[2 * length :], cross_value[2 * length :]), "cam", 1)
    key_total = cross_key[length : 2 * length] + upper_grads[0] + lower_grads[0]
    value_total = cross_value[length : 2 * length] + upper_grads[1] + lower_grads[1]
    block_shape = (1, frame_count, per_frame, width)
    keep_blocks = keep_low.reshape(1, frame_count, per_frame)
    temporal = temporal_items(
        (
            lax.all_to_all(
                query_rows.reshape(block_shape), "frame", split_axis=1, concat_axis=0, tiled=True
            ),
            lax.all_to_all(
                key_rows.reshape(block_shape), "frame", split_axis=1, concat_axis=0, tiled=True
            ),
            lax.all_to_all(
                value_rows.reshape(block_shape), "frame", split_axis=1, concat_axis=0, tiled=True
            ),
            lax.all_to_all(
                grad_rows.reshape(block_shape), "frame", split_axis=1, concat_axis=0, tiled=True
            ),
            lax.all_to_all(keep_blocks, "frame", split_axis=1, concat_axis=0, tiled=True),
        )
    )
    returned = (
        lax.all_to_all(temporal[0], "frame", split_axis=0, concat_axis=1, tiled=True),
        lax.all_to_all(temporal[1], "frame", split_axis=0, concat_axis=1, tiled=True),
        lax.all_to_all(temporal[2], "frame", split_axis=0, concat_axis=1, tiled=True),
        lax.all_to_all(temporal[3], "frame", split_axis=0, concat_axis=1, tiled=True),
    )
    back_rows = [piece.reshape(length, width).astype(jnp.float32) for piece in returned]
    attended = (cross_out + back_rows[0]).astype(jnp.bfloat16)
    grad_queries = (cross_query + back_rows[1]).astype(jnp.bfloat16)
    grad_keys = (key_total + back_rows[2]).astype(jnp.bfloat16)
    grad_values = (value_total + back_rows[3]).astype(jnp.bfloat16)
    return (
        attended[None, None],
        grad_queries[None, None],
        grad_keys[None, None],
        grad_values[None, None],
    )


def solution(mesh):
    placed = (
        P("cam", "frame", None, None),
        P("cam", "frame", None, None),
        P("cam", "frame", None, None),
        P("cam", "frame", None, None),
        P("cam", "frame"),
    )
    return jax.shard_map(
        on_device,
        mesh=mesh,
        in_specs=placed,
        out_specs=(
            P("cam", "frame", None, None),
            P("cam", "frame", None, None),
            P("cam", "frame", None, None),
            P("cam", "frame", None, None),
        ),
        check_vma=False,
    )
```

profile of v0, /device:TPU:1, one launch (start us, length us, event | category | flops | bytes accessed | tf_op | source)
XLA Modules:
  0.0 456.8 jit_solution(15271740577122444573)
XLA Ops:
  2.1 17.6 %all-to-all-start.1 = ((bf16[1,64,4]{2,0,1:T(2,128)(2,1)}), bf16[1,64,4]{2,0,1:T(2,128)(2,1)S(1)}, u32[]{:S(2)}, u32[]{:S(2)}) async-start(bf16[1,64,4]{2,0,1:T(2,128)(2,1)} %copy.210), calls=%async_computation.1 | async-start | bytes 65536 | tf_op jit(solution)/shard_map/all_to_all | solution.py:138
  21.8 9.6 %all-to-all-done.1 = bf16[1,64,4]{2,0,1:T(2,128)(2,1)S(1)} async-done(((bf16[1,64,4]{2,0,1:T(2,128)(2,1)}), bf16[1,64,4]{2,0,1:T(2,128)(2,1)S(1)}, u32[]{:S(2)}, u32[]{:S(2)}) %all-to-all-start.1) | async-done | bytes 544 | tf_op jit(solution)/shard_map/all_to_all | solution.py:138
  31.3 5.6 %all-to-all-start = ((bf16[1,64,4,1024]{3,2,0,1:T(4,128)(2,1)}), bf16[1,64,4,1024]{3,2,0,1:T(4,128)(2,1)}, u32[]{:S(2)}, u32[]{:S(2)}) async-start(bf16[1,64,4,1024]{3,2,0,1:T(4,128)(2,1)} %bitcast.25), calls=%async_computation | async-start | bytes 1048576 | tf_op jit(solution)/shard_map/all_to_all | solution.py:132
  38.0 17.7 %all-to-all-done = bf16[1,64,4,1024]{3,2,0,1:T(4,128)(2,1)} async-done(((bf16[1,64,4,1024]{3,2,0,1:T(4,128)(2,1)}), bf16[1,64,4,1024]{3,2,0,1:T(4,128)(2,1)}, u32[]{:S(2)}, u32[]{:S(2)}) %all-to-all-start) | async-done | bytes 524320 | tf_op jit(solution)/shard_map/all_to_all | solution.py:132
  55.7 8.0 %all-to-all-start.2 = ((bf16[1,64,4,1024]{3,2,0,1:T(4,128)(2,1)}), bf16[1,64,4,1024]{3,2,0,1:T(4,128)(2,1)}, u32[]{:S(2)}, u32[]{:S(2)}) async-start(bf16[1,64,4,1024]{3,2,0,1:T(4,128)(2,1)} %bitcast.30), calls=%async_computation.2 | async-start | bytes 1048576 | tf_op jit(solution)/shard_map/all_to_all | solution.py:126
  64.7 17.5 %all-to-all-done.2 = bf16[1,64,4,1024]{3,2,0,1:T(4,128)(2,1)} async-done(((bf16[1,64,4,1024]{3,2,0,1:T(4,128)(2,1)}), bf16[1,64,4,1024]{3,2,0,1:T(4,128)(2,1)}, u32[]{:S(2)}, u32[]{:S(2)}) %all-to-all-start.2) | async-done | bytes 524320 | tf_op jit(solution)/shard_map/all_to_all | solution.py:126
  82.3 7.7 %all-to-all-start.3 = ((bf16[1,64,4,1024]{3,2,0,1:T(4,128)(2,1)}), bf16[1,64,4,1024]{3,2,0,1:T(4,128)(2,1)}, u32[]{:S(2)}, u32[]{:S(2)}) async-start(bf16[1,64,4,1024]{3,2,0,1:T(4,128)(2,1)} %bitcast.32), calls=%async_computation.3 | async-start | bytes 1048576 | tf_op jit(solution)/shard_map/all_to_all | solution.py:129
  91.0 17.5 %all-to-all-done.3 = bf16[1,64,4,1024]{3,2,0,1:T(4,128)(2,1)} async-done(((bf16[1,64,4,1024]{3,2,0,1:T(4,128)(2,1)}), bf16[1,64,4,1024]{3,2,0,1:T(4,128)(2,1)}, u32[]{:S(2)}, u32[]{:S(2)}) %all-to-all-start.3) | async-done | bytes 524320 | tf_op jit(solution)/shard_map/all_to_all | solution.py:129
  108.5 7.5 %all-to-all-start.4 = ((bf16[1,64,4,1024]{3,2,0,1:T(4,128)(2,1)}), bf16[1,64,4,1024]{3,2,0,1:T(4,128)(2,1)}, u32[]{:S(2)}, u32[]{:S(2)}) async-start(bf16[1,64,4,1024]{3,2,0,1:T(4,128)(2,1)} %bitcast.34), calls=%async_computation.4 | async-start | bytes 1048576 | tf_op jit(solution)/shard_map/all_to_all | solution.py:135
  116.1 18.4 %all-to-all-done.4 = bf16[1,64,4,1024]{3,2,0,1:T(4,128)(2,1)} async-done(((bf16[1,64,4,1024]{3,2,0,1:T(4,128)(2,1)}), bf16[1,64,4,1024]{3,2,0,1:T(4,128)(2,1)}, u32[]{:S(2)}, u32[]{:S(2)}) %all-to-all-start.4) | async-done | bytes 524320 | tf_op jit(solution)/shard_map/all_to_all | solution.py:135
  137.4 65.3 %while.39 = (s32[]{:T(128)}, bf16[64,4,1024]{2,1,0:T(4,128)(2,1)}, bf16[64,4,1024]{2,1,0:T(4,128)(2,1)}, bf16[64,4,1024]{2,1,0:T(4,128)(2,1)S(1)}, bf16[64,4,102...) while((s32[]{:T(128)}, bf16[64,4,1024]{2,1,0:T(4,128)(2,1)}, ...), condition=%wide.region_9.10_spmd, body=%wide.region_5.9_spmd.sunk | while | flops 34374340 | bytes 4275147 | solution.py:84
  202.8 26.1 %all_to_all.36 = bf16[64,1,4,1024]{3,2,1,0:T(4,128)(2,1)} all-to-all(bf16[64,1,4,1024]{3,2,1,0:T(4,128)(2,1)} %bitcast.228), channel_id=1, replica_groups=mesh['cam'=8,'frame'=64] {'frame'}, dimensions={0} | all-to-all | bytes 1048576 | tf_op jit(solution)/shard_map/all_to_all | solution.py:145
  228.9 25.8 %all_to_all.37 = bf16[64,1,4,1024]{3,2,1,0:T(4,128)(2,1)} all-to-all(bf16[64,1,4,1024]{3,2,1,0:T(4,128)(2,1)S(1)} %bitcast.227), channel_id=1, replica_groups=mesh['cam'=8,'frame'=64] {'frame'}, dimensions={0} | all-to-all | bytes 1048576 | tf_op jit(solution)/shard_map/all_to_all | solution.py:144
  254.7 7.3 %all-to-all-start.6 = ((bf16[64,1,4,1024]{3,2,1,0:T(4,128)(2,1)}), bf16[64,1,4,1024]{3,2,1,0:T(4,128)(2,1)S(1)}, u32[]{:S(2)}, u32[]{:S(2)}) async-start(bf16[64,1,4,1024]{3,2,1,0:T(4,128)(2,1)} %bitcast.76), calls=%async_computation.6 | async-start | bytes 1048576 | tf_op jit(solution)/shard_map/all_to_all | solution.py:143
  279.6 5.5 %collective-permute-start.5 = (bf16[256,1024]{0,1:T(8,128)(2,1)S(1)}, bf16[256,1024]{0,1:T(8,128)(2,1)S(1)}, u32[]{:S(2)}, u32[]{:S(2)}) collective-permute-start(bf16[256,1024]{0,1:T(8,128)(2,1)S(1)} %bitcast.230), channel_id=1, source_target_pairs={{0,448},{64,0},{128,64},{192,128},{256,192},{320,256},{384,320},{4... | collective-permute-start | bytes 1572872 | tf_op jit(solution)/shard_map/ppermute | solution.py:15
  285.1 5.8 %collective-permute-done = bf16[256,1024]{0,1:T(8,128)(2,1)} collective-permute-done((bf16[256,1024]{0,1:T(8,128)(2,1)S(1)}, bf16[256,1024]{0,1:T(8,128)(2,1)}, u32[]{:S(2)}, u32[]{:S(2)}) %collective-permute-start) | collective-permute-done | bytes 524320 | tf_op jit(solution)/shard_map/ppermute | solution.py:15
  293.3 8.8 %collective-permute-done.4 = bf16[256,1024]{0,1:T(8,128)(2,1)} collective-permute-done((bf16[256,1024]{0,1:T(8,128)(2,1)S(1)}, bf16[256,1024]{0,1:T(8,128)(2,1)}, u32[]{:S(2)}, u32[]{:S(2)}) %collective-permute-start.4) | collective-permute-done | bytes 524320 | tf_op jit(solution)/shard_map/ppermute | solution.py:15
  304.5 10.9 %all-to-all-start.5 = ((bf16[64,1,4,1024]{3,2,1,0:T(4,128)(2,1)}), bf16[64,1,4,1024]{3,2,1,0:T(4,128)(2,1)}, u32[]{:S(2)}, u32[]{:S(2)}) async-start(bf16[64,1,4,1024]{3,2,1,0:T(4,128)(2,1)} %bitcast.77), calls=%async_computation.5 | async-start | bytes 1048576 | tf_op jit(solution)/shard_map/all_to_all | solution.py:142
  321.7 73.2 %while.38 = (s32[]{:T(128)}, f32[256,1024]{1,0:T(8,128)}, f32[256,1024]{1,0:T(8,128)}, f32[768,1024]{1,0:T(8,128)}, f32[768,1024]{1,0:T(8,128)}, /*index=5*/bf16...) while((s32[]{:T(128)}, f32[256,1024]{1,0:T(8,128)}, ...), condition=%wide.region_4.5_spmd, body=%wide.region_0.4_spmd.sunk | while | flops 411044608 | bytes 22299140 | solution.py:84
  398.1 5.3 %collective-permute-start.8 = (f32[256,1024]{1,0:T(8,128)}, f32[256,1024]{1,0:T(8,128)}, u32[]{:S(2)}, u32[]{:S(2)}) collective-permute-start(f32[256,1024]{1,0:T(8,128)} %get-tuple-element.472), channel_id=1, source_target_pairs={{0,448},{64,0},{128,64},{192,128},{256,192},{320,256},{384,320},{4... | collective-permute-start | bytes 3145736 | tf_op jit(solution)/shard_map/ppermute | solution.py:15
  406.9 5.5 %collective-permute-start.6 = (f32[256,1024]{1,0:T(8,128)}, f32[256,1024]{1,0:T(8,128)}, u32[]{:S(2)}, u32[]{:S(2)}) collective-permute-start(f32[256,1024]{1,0:T(8,128)} %get-tuple-element.474), channel_id=1, source_target_pairs={{0,448},{64,0},{128,64},{192,128},{256,192},{320,256},{384,320},{4... | collective-permute-start | bytes 3145736 | tf_op jit(solution)/shard_map/ppermute | solution.py:15
  426.3 5.3 %collective-permute-done.9 = f32[256,1024]{1,0:T(8,128)} collective-permute-done((f32[256,1024]{1,0:T(8,128)}, f32[256,1024]{1,0:T(8,128)}, u32[]{:S(2)}, u32[]{:S(2)}) %collective-permute-start.9) | collective-permute-done | bytes 1048608 | tf_op jit(solution)/shard_map/ppermute | solution.py:15
  434.6 13.6 %collective-permute-done.6 = f32[256,1024]{1,0:T(8,128)} collective-permute-done((f32[256,1024]{1,0:T(8,128)}, f32[256,1024]{1,0:T(8,128)}, u32[]{:S(2)}, u32[]{:S(2)}) %collective-permute-start.6) | collective-permute-done | bytes 1048608 | tf_op jit(solution)/shard_map/ppermute | solution.py:15
  448.2 5.9 %collective-permute-done.7 = f32[256,1024]{1,0:T(8,128)} collective-permute-done((f32[256,1024]{1,0:T(8,128)}, f32[256,1024]{1,0:T(8,128)}, u32[]{:S(2)}, u32[]{:S(2)}) %collective-permute-start.7) | collective-permute-done | bytes 1048608 | tf_op jit(solution)/shard_map/ppermute | solution.py:15
  (423 shorter events, 200.6 us)
Async XLA Ops:
  0.6 36.4 %copy-start.8 = (bf16[1,1,256,1024]{3,2,1,0:T(8,128)(2,1)S(1)}, bf16[1,1,256,1024]{3,2,1,0:T(8,128)(2,1)}, u32[]{:S(2)}) copy-start(bf16[1,1,256,1024]{3,2,1,0:T(8,128)(2,1)} %param.9) | copy-start | bytes 1572868
  2.1 29.2 %all-to-all-start.1 = ((bf16[1,64,4]{2,0,1:T(2,128)(2,1)}), bf16[1,64,4]{2,0,1:T(2,128)(2,1)S(1)}, u32[]{:S(2)}, u32[]{:S(2)}) async-start(bf16[1,64,4]{2,0,1:T(2,128)(2,1)} %copy.210), calls=%async_computation.1 | async-start | bytes 65536 | tf_op jit(solution)/shard_map/all_to_all | solution.py:138
  31.3 32.4 %copy-start.7 = (bf16[1,1,256,1024]{3,2,1,0:T(8,128)(2,1)S(1)}, bf16[1,1,256,1024]{3,2,1,0:T(8,128)(2,1)}, u32[]{:S(2)}) copy-start(bf16[1,1,256,1024]{3,2,1,0:T(8,128)(2,1)} %param.10) | copy-start | bytes 1572868
  31.3 24.4 %all-to-all-start = ((bf16[1,64,4,1024]{3,2,0,1:T(4,128)(2,1)}), bf16[1,64,4,1024]{3,2,0,1:T(4,128)(2,1)}, u32[]{:S(2)}, u32[]{:S(2)}) async-start(bf16[1,64,4,1024]{3,2,0,1:T(4,128)(2,1)} %bitcast.25), calls=%async_computation | async-start | bytes 1048576 | tf_op jit(solution)/shard_map/all_to_all | solution.py:132
  55.7 34.3 %copy-start.9 = (bf16[1,1,256,1024]{3,2,1,0:T(8,128)(2,1)S(1)}, bf16[1,1,256,1024]{3,2,1,0:T(8,128)(2,1)}, u32[]{:S(2)}) copy-start(bf16[1,1,256,1024]{3,2,1,0:T(8,128)(2,1)} %param.12) | copy-start | bytes 1572868
  55.7 26.5 %all-to-all-start.2 = ((bf16[1,64,4,1024]{3,2,0,1:T(4,128)(2,1)}), bf16[1,64,4,1024]{3,2,0,1:T(4,128)(2,1)}, u32[]{:S(2)}, u32[]{:S(2)}) async-start(bf16[1,64,4,1024]{3,2,0,1:T(4,128)(2,1)} %bitcast.30), calls=%async_computation.2 | async-start | bytes 1048576 | tf_op jit(solution)/shard_map/all_to_all | solution.py:126
  82.3 26.2 %all-to-all-start.3 = ((bf16[1,64,4,1024]{3,2,0,1:T(4,128)(2,1)}), bf16[1,64,4,1024]{3,2,0,1:T(4,128)(2,1)}, u32[]{:S(2)}, u32[]{:S(2)}) async-start(bf16[1,64,4,1024]{3,2,0,1:T(4,128)(2,1)} %bitcast.32), calls=%async_computation.3 | async-start | bytes 1048576 | tf_op jit(solution)/shard_map/all_to_all | solution.py:129
  108.5 26.0 %all-to-all-start.4 = ((bf16[1,64,4,1024]{3,2,0,1:T(4,128)(2,1)}), bf16[1,64,4,1024]{3,2,0,1:T(4,128)(2,1)}, u32[]{:S(2)}, u32[]{:S(2)}) async-start(bf16[1,64,4,1024]{3,2,0,1:T(4,128)(2,1)} %bitcast.34), calls=%async_computation.4 | async-start | bytes 1048576 | tf_op jit(solution)/shard_map/all_to_all | solution.py:135
  202.8 65.8 %copy-start.6 = (bf16[1,1,256,1024]{3,2,1,0:T(8,128)(2,1)S(1)}, bf16[1,1,256,1024]{3,2,1,0:T(8,128)(2,1)}, u32[]{:S(2)}) copy-start(bf16[1,1,256,1024]{3,2,1,0:T(8,128)(2,1)} %param.11) | copy-start | bytes 1572868
  254.7 49.7 %all-to-all-start.6 = ((bf16[64,1,4,1024]{3,2,1,0:T(4,128)(2,1)}), bf16[64,1,4,1024]{3,2,1,0:T(4,128)(2,1)S(1)}, u32[]{:S(2)}, u32[]{:S(2)}) async-start(bf16[64,1,4,1024]{3,2,1,0:T(4,128)(2,1)} %bitcast.76), calls=%async_computation.6 | async-start | bytes 1048576 | tf_op jit(solution)/shard_map/all_to_all | solution.py:143
  262.1 17.5 %collective-permute-start.3 = (bf16[256]{0:T(256)(128)(2,1)S(1)}, bf16[256]{0:T(256)(128)(2,1)S(1)}, u32[]{:S(2)}, u32[]{:S(2)}) collective-permute-start(bf16[256]{0:T(256)(128)(2,1)S(1)} %fusion.25), channel_id=1, source_target_pairs={{0,448},{64,0},{128,64},{192,128},{256,192},{320,256},{384,320},{4... | collective-permute-start | bytes 1544 | tf_op jit(solution)/shard_map/ppermute | solution.py:15
  266.5 18.6 %collective-permute-start.2 = (bf16[256]{0:T(256)(128)(2,1)S(1)}, bf16[256]{0:T(256)(128)(2,1)S(1)}, u32[]{:S(2)}, u32[]{:S(2)}) collective-permute-start(bf16[256]{0:T(256)(128)(2,1)S(1)} %fusion.25), channel_id=1, source_target_pairs={{0,64},{64,128},{128,192},{192,256},{256,320},{320,384},{384,448},... | collective-permute-start | bytes 1544 | tf_op jit(solution)/shard_map/ppermute | solution.py:15
  268.8 22.1 %collective-permute-start = (bf16[256,1024]{0,1:T(8,128)(2,1)S(1)}, bf16[256,1024]{0,1:T(8,128)(2,1)}, u32[]{:S(2)}, u32[]{:S(2)}) collective-permute-start(bf16[256,1024]{0,1:T(8,128)(2,1)S(1)} %bitcast.232), channel_id=1, source_target_pairs={{0,64},{64,128},{128,192},{192,256},{256,320},{320,384},{384,448},... | collective-permute-start | bytes 1572872 | tf_op jit(solution)/shard_map/ppermute | solution.py:15
  270.9 19.9 %collective-permute-start.1 = (bf16[256,1024]{0,1:T(8,128)(2,1)S(1)}, bf16[256,1024]{0,1:T(8,128)(2,1)}, u32[]{:S(2)}, u32[]{:S(2)}) collective-permute-start(bf16[256,1024]{0,1:T(8,128)(2,1)S(1)} %bitcast.233), channel_id=1, source_target_pairs={{0,448},{64,0},{128,64},{192,128},{256,192},{320,256},{384,320},{4... | collective-permute-start | bytes 1572872 | tf_op jit(solution)/shard_map/ppermute | solution.py:15
  276.4 25.7 %collective-permute-start.4 = (bf16[256,1024]{0,1:T(8,128)(2,1)S(1)}, bf16[256,1024]{0,1:T(8,128)(2,1)}, u32[]{:S(2)}, u32[]{:S(2)}) collective-permute-start(bf16[256,1024]{0,1:T(8,128)(2,1)S(1)} %bitcast.229), channel_id=1, source_target_pairs={{0,64},{64,128},{128,192},{192,256},{256,320},{320,384},{384,448},... | collective-permute-start | bytes 1572872 | tf_op jit(solution)/shard_map/ppermute | solution.py:15
  279.6 22.5 %collective-permute-start.5 = (bf16[256,1024]{0,1:T(8,128)(2,1)S(1)}, bf16[256,1024]{0,1:T(8,128)(2,1)S(1)}, u32[]{:S(2)}, u32[]{:S(2)}) collective-permute-start(bf16[256,1024]{0,1:T(8,128)(2,1)S(1)} %bitcast.230), channel_id=1, source_target_pairs={{0,448},{64,0},{128,64},{192,128},{256,192},{320,256},{384,320},{4... | collective-permute-start | bytes 1572872 | tf_op jit(solution)/shard_map/ppermute | solution.py:15
  304.5 12.9 %copy-start.5 = (bf16[64,1,4,1024]{3,2,1,0:T(4,128)(2,1)}, bf16[64,1,4,1024]{3,2,1,0:T(4,128)(2,1)S(1)}, u32[]{:S(2)}) copy-start(bf16[64,1,4,1024]{3,2,1,0:T(4,128)(2,1)S(1)} %all-to-all-done.6) | copy-start | bytes 1572868
  304.5 116.2 %all-to-all-start.5 = ((bf16[64,1,4,1024]{3,2,1,0:T(4,128)(2,1)}), bf16[64,1,4,1024]{3,2,1,0:T(4,128)(2,1)}, u32[]{:S(2)}, u32[]{:S(2)}) async-start(bf16[64,1,4,1024]{3,2,1,0:T(4,128)(2,1)} %bitcast.77), calls=%async_computation.5 | async-start | bytes 1048576 | tf_op jit(solution)/shard_map/all_to_all | solution.py:142
  394.9 10.5 %copy-start = (f32[768,1024]{1,0:T(8,128)S(1)}, f32[768,1024]{1,0:T(8,128)}, u32[]{:S(2)}) copy-start(f32[768,1024]{1,0:T(8,128)} %get-tuple-element.352) | copy-start | bytes 9437188
  398.1 28.2 %collective-permute-start.8 = (f32[256,1024]{1,0:T(8,128)}, f32[256,1024]{1,0:T(8,128)}, u32[]{:S(2)}, u32[]{:S(2)}) collective-permute-start(f32[256,1024]{1,0:T(8,128)} %get-tuple-element.472), channel_id=1, source_target_pairs={{0,448},{64,0},{128,64},{192,128},{256,192},{320,256},{384,320},{4... | collective-permute-start | bytes 3145736 | tf_op jit(solution)/shard_map/ppermute | solution.py:15
  403.4 28.2 %collective-permute-start.9 = (f32[256,1024]{1,0:T(8,128)}, f32[256,1024]{1,0:T(8,128)}, u32[]{:S(2)}, u32[]{:S(2)}) collective-permute-start(f32[256,1024]{1,0:T(8,128)} %get-tuple-element.473), channel_id=1, source_target_pairs={{0,64},{64,128},{128,192},{192,256},{256,320},{320,384},{384,448},... | collective-permute-start | bytes 3145736 | tf_op jit(solution)/shard_map/ppermute | solution.py:15
  406.9 41.3 %collective-permute-start.6 = (f32[256,1024]{1,0:T(8,128)}, f32[256,1024]{1,0:T(8,128)}, u32[]{:S(2)}, u32[]{:S(2)}) collective-permute-start(f32[256,1024]{1,0:T(8,128)} %get-tuple-element.474), channel_id=1, source_target_pairs={{0,448},{64,0},{128,64},{192,128},{256,192},{320,256},{384,320},{4... | collective-permute-start | bytes 3145736 | tf_op jit(solution)/shard_map/ppermute | solution.py:15
  412.4 41.7 %collective-permute-start.7 = (f32[256,1024]{1,0:T(8,128)}, f32[256,1024]{1,0:T(8,128)}, u32[]{:S(2)}, u32[]{:S(2)}) collective-permute-start(f32[256,1024]{1,0:T(8,128)} %get-tuple-element.475), channel_id=1, source_target_pairs={{0,64},{64,128},{128,192},{192,256},{256,320},{320,384},{384,448},... | collective-permute-start | bytes 3145736 | tf_op jit(solution)/shard_map/ppermute | solution.py:15
  426.3 27.8 %copy-start.3 = (f32[256,1024]{1,0:T(8,128)S(1)}, f32[256,1024]{1,0:T(8,128)}, u32[]{:S(2)}) copy-start(f32[256,1024]{1,0:T(8,128)} %reshape.198) | copy-start | bytes 3145732
  (19 other events, 34.9 us)
where the time goes:
time: 461 us; the launch traced here: 457 us
  local copies, waits for them, and re-layouts  121 us (26%)
  waiting for transfers between devices  120 us (26%)
  starting transfers between devices  101 us (22%)
  blocking collectives  51.9 us (11%)
  matrix products  43 us (9%)
  other arithmetic  17 us (4%)
    dynamic_slice x72, local copies, waits for them, and re-layouts, take_heads(): lax.dynamic_slice_in_dim(matrix, column_start, 128, matrix.ndim - 1)  52.4 us
    ppermute x10, waiting for transfers between devices, from_behind(): lax.ppermute(shard, axis, [(i, (i + by) % devices) for i in range(devices)])  39.4 us
    ppermute x10, starting transfers between devices, from_behind(): lax.ppermute(shard, axis, [(i, (i + by) % devices) for i in range(devices)])  35.8 us
    dynamic_update_slice x112, local copies, waits for them, and re-layouts, put_heads(): lax.dynamic_update_slice_in_dim(target, flattened, column_start, target.n...  35.3 us
    all_to_all x1, blocking collectives, on_device(): lax.all_to_all(temporal[3], 'frame', split_axis=0, concat_axis=1, tiled=T...  26.1 us
    all_to_all x1, blocking collectives, on_device(): lax.all_to_all(temporal[2], 'frame', split_axis=0, concat_axis=1, tiled=T...  25.8 us
    all_to_all x1, waiting for transfers between devices, on_device(): lax.all_to_all(grad_rows.reshape(block_shape), 'frame', split_axis=1, con...  18.4 us
    all_to_all x1, waiting for transfers between devices, on_device(): lax.all_to_all(value_rows.reshape(block_shape), 'frame', split_axis=1, co...  17.7 us
  transfers between devices with their start and end apart: 17, of which 10 were waited for; matrix products, arithmetic and copies ran while one was open for 24% of the time, Pallas kernels for 0%

commit v1 on v0

v1 whole, which is shorter than its diff:
```python
import jax
import jax.numpy as jnp
from jax import lax
from jax.experimental import pallas as pl
from jax.experimental.pallas import tpu as pltpu
from jax.sharding import PartitionSpec as P

HEAD_DIM = 64
PAIR = 128
MARK = 1024.0
MARK_CUT = 512.0
MASKED = -1e30
SCALE = HEAD_DIM ** (-0.5)
ROW_T = (((1,), (1,)), ((), ()))
VMEM_BYTES = 60 * 1024 * 1024


def contract(left, right, dims):
    return lax.dot_general(left, right, dims, preferred_element_type=jnp.float32)


def multiply(left, right):
    return jnp.dot(left, right, preferred_element_type=jnp.float32)


def params():
    return pltpu.CompilerParams(vmem_limit_bytes=VMEM_BYTES)


def mark_kernel(count_ref, k_ref, v_ref, kv_ref):
    positions = lax.broadcasted_iota(jnp.int32, k_ref.shape, 0)
    wide = k_ref[...].astype(jnp.float32)
    marked = jnp.where(positions < count_ref[0, 0], wide, MARK).astype(jnp.bfloat16)
    values = v_ref[...]
    for pair in range(kv_ref.shape[0]):
        columns = slice(pair * PAIR, (pair + 1) * PAIR)
        kv_ref[pair, 0] = marked[:, columns]
        kv_ref[pair, 1] = values[:, columns]


def mark(count, keys, values):
    length, width = keys.shape
    pairs = width // PAIR
    per_step = 2
    column_spec = pl.BlockSpec((length, per_step * PAIR), lambda j: (0, j))
    return pl.pallas_call(
        mark_kernel,
        grid=(pairs // per_step,),
        in_specs=[pl.BlockSpec(memory_space=pltpu.SMEM)] + [column_spec] * 2,
        out_specs=pl.BlockSpec((per_step, 2, length, PAIR), lambda j: (j, 0, 0, 0)),
        out_shape=jax.ShapeDtypeStruct((pairs, 2, length, PAIR), jnp.bfloat16),
        compiler_params=params(),
        cost_estimate=pl.CostEstimate(
            flops=length * width, bytes_accessed=8 * length * width, transcendentals=0
        ),
        name="mark",
    )(count, keys, values)


def pack_kernel(q_ref, kv_ref, g_ref, x_ref):
    blocks, pairs, _, rows, _ = x_ref.shape
    queries = q_ref[...]
    cotangents = g_ref[...]
    for pair in range(pairs):
        columns = slice(pair * PAIR, (pair + 1) * PAIR)
        parts = (queries[:, columns], kv_ref[pair, 0], kv_ref[pair, 1], cotangents[:, columns])
        for index, part in enumerate(parts):
            x_ref[:, pair, index] = part.reshape(blocks, rows, PAIR)


def pack(queries, marked, cotangents, frames):
    length, width = queries.shape
    pairs = width // PAIR
    blocks = frames // pairs
    rows = length // blocks
    per_step = 2
    column_spec = pl.BlockSpec((length, per_step * PAIR), lambda j: (0, j))
    return pl.pallas_call(
        pack_kernel,
        grid=(pairs // per_step,),
        in_specs=[
            column_spec,
            pl.BlockSpec((per_step, 2, length, PAIR), lambda j: (j, 0, 0, 0)),
            column_spec,
        ],
        out_specs=pl.BlockSpec((blocks, per_step, 4, rows, PAIR), lambda j: (0, j, 0, 0, 0)),
        out_shape=jax.ShapeDtypeStruct((blocks, pairs, 4, rows, PAIR), jnp.bfloat16),
        compiler_params=params(),
        cost_estimate=pl.CostEstimate(
            flops=length * width, bytes_accessed=16 * length * width, transcendentals=0
        ),
        name="pack",
    )(queries, marked, cotangents)


def cross_kernel(q_ref, g_ref, own_ref, low_ref, up_ref, o_ref, dq_ref, own_out, low_out, up_out):
    length = q_ref.shape[0]
    first = lax.broadcasted_iota(jnp.int32, (length, PAIR), 1) < HEAD_DIM
    marked = jnp.concatenate([low_ref[0, 0], own_ref[0, 0], up_ref[0, 0]], axis=0)
    values = jnp.concatenate([low_ref[0, 1], own_ref[0, 1], up_ref[0, 1]], axis=0)
    wide = marked.astype(jnp.float32)
    invalid = wide > MARK_CUT
    keys_wide = jnp.where(invalid, 0.0, wide)
    keys = keys_wide.astype(jnp.bfloat16)
    bias = jnp.where(invalid, MASKED, 0.0)
    bias = jnp.concatenate([bias] * (length // PAIR), axis=1)
    keys_t = keys_wide.T.astype(jnp.bfloat16)
    values_t = values.astype(jnp.float32).T.astype(jnp.bfloat16)
    queries = q_ref[...].astype(jnp.float32) * SCALE
    cotangents = g_ref[...].astype(jnp.float32)
    outputs = []
    query_grads = []
    key_grad = None
    value_grad = None
    for head in range(PAIR // HEAD_DIM):
        mine = first if head == 0 else jnp.logical_not(first)
        query = jnp.where(mine, queries, 0.0).astype(jnp.bfloat16)
        cotangent = jnp.where(mine, cotangents, 0.0).astype(jnp.bfloat16)
        scores = contract(keys, query, ROW_T) + bias
        shifted = jnp.exp(scores - jnp.max(scores, axis=0, keepdims=True))
        probs = shifted * (1.0 / jnp.sum(shifted, axis=0, keepdims=True))
        probs_low = probs.astype(jnp.bfloat16)
        grad_probs = contract(values, cotangent, ROW_T)
        row_delta = jnp.sum(probs * grad_probs, axis=0, keepdims=True)
        grad_scores = (probs * (grad_probs - row_delta)).astype(jnp.bfloat16)
        rows = slice(head * HEAD_DIM, (head + 1) * HEAD_DIM)
        outputs.append(multiply(values_t[rows], probs_low))
        query_grads.append(multiply(keys_t[rows], grad_scores))
        value_part = multiply(probs_low, cotangent)
        key_part = multiply(grad_scores, query)
        key_grad = key_part if head == 0 else key_grad + key_part
        value_grad = value_part if head == 0 else value_grad + value_part
    o_ref[...] = jnp.concatenate(outputs, axis=0).T
    dq_ref[...] = jnp.concatenate(query_grads, axis=0).T * SCALE
    for index, grad in enumerate((key_grad, value_grad)):
        low_out[0, index] = grad[:length].astype(jnp.bfloat16)
        own_out[0, index] = grad[length : 2 * length]
        up_out[0, index] = grad[2 * length :].astype(jnp.bfloat16)


def cross(queries, cotangents, own, lower, upper):
    length, width = queries.shape
    pairs = width // PAIR
    column_spec = pl.BlockSpec((length, PAIR), lambda j: (0, j))
    pair_spec = pl.BlockSpec((1, 2, length, PAIR), lambda j: (j, 0, 0, 0))
    flat = jax.ShapeDtypeStruct((length, width), jnp.float32)
    paired = jax.ShapeDtypeStruct((pairs, 2, length, PAIR), jnp.float32)
    paired_low = jax.ShapeDtypeStruct((pairs, 2, length, PAIR), jnp.bfloat16)
    return pl.pallas_call(
        cross_kernel,
        grid=(pairs,),
        in_specs=[column_spec] * 2 + [pair_spec] * 3,
        out_specs=[column_spec] * 2 + [pair_spec] * 3,
        out_shape=[flat, flat, paired, paired_low, paired_low],
        compiler_params=params(),
        cost_estimate=pl.CostEstimate(
            flops=10000 * length * length * width,
            bytes_accessed=24 * length * width * 2,
            transcendentals=48 * length * length,
        ),
        name="cross_view",
    )(queries, cotangents, own, lower, upper)


def temporal_kernel(y_ref, z_ref, rows_in, rows_out):
    frames, _, positions, _ = y_ref.shape
    first = lax.broadcasted_iota(jnp.int32, (frames, PAIR), 1) < HEAD_DIM
    for index in range(4):
        rows_in[index] = y_ref[:, index].astype(jnp.float32).reshape(frames * positions, PAIR)

    def stacked(rows):
        return jnp.concatenate(
            [jnp.where(first, rows, 0.0), jnp.where(first, 0.0, rows)], axis=0
        ).astype(jnp.bfloat16)

    def diagonal(full):
        return jnp.where(first, full[:frames], full[frames:])

    group = 8
    for start in range(0, positions, group):
        held = []
        for position in range(start, start + group):
            at = pl.ds(position, frames, stride=positions)
            marked = rows_in[1, at, :]
            invalid = marked > MARK_CUT
            keys = jnp.where(invalid, 0.0, marked).astype(jnp.bfloat16)
            values = rows_in[2, at, :].astype(jnp.bfloat16)
            queries = stacked(rows_in[0, at, :] * SCALE)
            cotangents = stacked(rows_in[3, at, :])
            scores = jnp.where(invalid, MASKED, contract(keys, queries, ROW_T))
            grad_probs = contract(values, cotangents, ROW_T)
            held.append((at, keys, values, queries, cotangents, scores, grad_probs))
        for at, keys, values, queries, cotangents, scores, grad_probs in held:
            shifted = jnp.exp(scores - jnp.max(scores, axis=0, keepdims=True))
            probs = shifted * (1.0 / jnp.sum(shifted, axis=0, keepdims=True))
            row_delta = jnp.sum(probs * grad_probs, axis=0, keepdims=True)
            grad_scores = probs * (grad_probs - row_delta)
            rows_out[0, at, :] = diagonal(multiply(probs.T.astype(jnp.bfloat16), values))
            rows_out[1, at, :] = (
                diagonal(multiply(grad_scores.T.astype(jnp.bfloat16), keys)) * SCALE
            )
            rows_out[2, at, :] = multiply(grad_scores.astype(jnp.bfloat16), queries)
            rows_out[3, at, :] = multiply(probs.astype(jnp.bfloat16), cotangents)
    for index in range(4):
        z_ref[:, index] = rows_out[index].reshape(frames, positions, PAIR).astype(jnp.bfloat16)


def temporal(blocks):
    frames, _, positions, _ = blocks.shape
    per_step = 16
    spec = pl.BlockSpec((frames, 4, per_step, PAIR), lambda i: (0, 0, i, 0))
    scratch = pltpu.VMEM((4, frames * per_step, PAIR), jnp.float32)
    return pl.pallas_call(
        temporal_kernel,
        grid=(positions // per_step,),
        in_specs=[spec],
        out_specs=spec,
        out_shape=jax.ShapeDtypeStruct(blocks.shape, jnp.bfloat16),
        scratch_shapes=[scratch, scratch],
        compiler_params=params(),
        cost_estimate=pl.CostEstimate(
            flops=12 * positions * frames * frames * PAIR,
            bytes_accessed=4 * blocks.size,
            transcendentals=2 * positions * frames * frames,
        ),
        name="temporal",
    )(blocks)


def total_kernel(own_ref, low_ref, up_ref, key_ref, value_ref):
    for pair in range(own_ref.shape[0]):
        columns = slice(pair * PAIR, (pair + 1) * PAIR)
        for index, total_ref in enumerate((key_ref, value_ref)):
            total_ref[:, columns] = (
                own_ref[pair, index]
                + low_ref[pair, index].astype(jnp.float32)
                + up_ref[pair, index].astype(jnp.float32)
            )


def total(own, lower, upper):
    pairs, _, length, _ = own.shape
    per_step = 2
    pair_spec = pl.BlockSpec((per_step, 2, length, PAIR), lambda j: (j, 0, 0, 0))
    return pl.pallas_call(
        total_kernel,
        grid=(pairs // per_step,),
        in_specs=[pair_spec] * 3,
        out_specs=[pl.BlockSpec((length, per_step * PAIR), lambda j: (0, j))] * 2,
        out_shape=[jax.ShapeDtypeStruct((length, pairs * PAIR), jnp.float32)] * 2,
        compiler_params=params(),
        cost_estimate=pl.CostEstimate(
            flops=2 * own.size, bytes_accessed=12 * own.size, transcendentals=0
        ),
        name="total",
    )(own, lower, upper)


def finish_kernel(w_ref, *refs):
    cross_refs, out_refs = refs[:4], refs[4:]
    length = cross_refs[0].shape[0]
    for pair in range(w_ref.shape[1]):
        columns = slice(pair * PAIR, (pair + 1) * PAIR)
        for index, (cross_ref, out_ref) in enumerate(zip(cross_refs, out_refs)):
            returned = w_ref[:, pair, index].reshape(length, PAIR).astype(jnp.float32)
            out_ref[:, columns] = (cross_ref[:, columns] + returned).astype(jnp.bfloat16)


def finish(returned, *cross_parts):
    length, width = cross_parts[0].shape
    blocks, pairs, _, rows, _ = returned.shape
    per_step = 2
    column_spec = pl.BlockSpec((length, per_step * PAIR), lambda j: (0, j))
    return pl.pallas_call(
        finish_kernel,
        grid=(pairs // per_step,),
        in_specs=[pl.BlockSpec((blocks, per_step, 4, rows, PAIR), lambda j: (0, j, 0, 0, 0))]
        + [column_spec] * 4,
        out_specs=[column_spec] * 4,
        out_shape=[jax.ShapeDtypeStruct((length, width), jnp.bfloat16)] * 4,
        compiler_params=params(),
        cost_estimate=pl.CostEstimate(
            flops=4 * length * width, bytes_accessed=32 * length * width, transcendentals=0
        ),
        name="finish",
    )(returned, *cross_parts)


def from_behind(shard, axis, by):
    devices = lax.axis_size(axis)
    return lax.ppermute(shard, axis, [(i, (i + by) % devices) for i in range(devices)])


def exchange(blocks):
    return lax.all_to_all(blocks, "frame", split_axis=0, concat_axis=0, tiled=True)


def on_device(queries, key_vectors, value_vectors, out_grad, valid_count):
    query_rows = queries[0, 0]
    key_rows = key_vectors[0, 0]
    value_rows = value_vectors[0, 0]
    grad_rows = out_grad[0, 0]
    frames = lax.axis_size("frame")
    marked = mark(valid_count, key_rows, value_rows)
    lower = from_behind(marked, "cam", 1)
    upper = from_behind(marked, "cam", -1)
    packed = pack(query_rows, marked, grad_rows, frames)
    rows = packed.shape[3]
    arrived = exchange(packed.reshape(frames, 4 * rows, PAIR))
    cross_out, cross_query, own_grads, lower_grads, upper_grads = cross(
        query_rows, grad_rows, marked, lower, upper
    )
    from_upper = from_behind(lower_grads, "cam", -1)
    from_lower = from_behind(upper_grads, "cam", 1)
    arrived, cross_out = lax.optimization_barrier((arrived, cross_out))
    answered = temporal(arrived.reshape(frames, 4, rows, PAIR))
    answered, from_upper, from_lower = lax.optimization_barrier(
        (answered, from_upper, from_lower)
    )
    returned = exchange(answered.reshape(frames, 4 * rows, PAIR)).reshape(packed.shape)
    key_total, value_total = total(own_grads, from_upper, from_lower)
    results = finish(returned, cross_out, cross_query, key_total, value_total)
    return tuple(result[None, None] for result in results)


def solution(mesh):
    placed = (
        P("cam", "frame", None, None),
        P("cam", "frame", None, None),
        P("cam", "frame", None, None),
        P("cam", "frame", None, None),
        P("cam", "frame"),
    )
    return jax.shard_map(
        on_device,
        mesh=mesh,
        in_specs=placed,
        out_specs=(
            P("cam", "frame", None, None),
            P("cam", "frame", None, None),
            P("cam", "frame", None, None),
            P("cam", "frame", None, None),
        ),
        check_vma=False,
    )
```

time: 461 us -> 208 us (0.45)
  local copies, waits for them, and re-layouts: 121 us -> 4.74 us
  blocking collectives: 51.9 us -> 0 us
  matrix products: 43 us -> 0 us
  Pallas kernels: 0 us -> 42.8 us
  waiting for transfers between devices: 120 us -> 85.4 us
  starting transfers between devices: 101 us -> 70.2 us
  other arithmetic: 17 us -> 0 us
    dynamic_slice x72 -> x0, local copies, waits for them, and re-layouts: 52.4 us -> none  [take_heads(): lax.dynamic_slice_in_dim(matrix, column_start, 128, matrix.ndim - 1)]
    all_to_all x2 -> x0, blocking collectives: 51.9 us -> none  [the longest x1 26.1 us: on_device(): lax.all_to_all(temporal[3], 'frame', split_axis=0, concat_axis=1, tiled=T...]
    pallas_call x0 -> x6, Pallas kernels: none -> 42.8 us  [the longest x1 19.4 us: cross(): pl.pallas_call(cross_kernel, grid=(pairs,), in_specs=[column_spec] * 2 +...]
    dynamic_update_slice x112 -> x0, local copies, waits for them, and re-layouts: 35.3 us -> none  [put_heads(): lax.dynamic_update_slice_in_dim(target, flattened, column_start, target.n...]
    dot_general x80 -> x0, matrix products: 34.9 us -> none  [the longest x16 10.2 us: attend_heads(): jnp.einsum(to_query, probs_low, value_part, preferred_element_type=jnp.fl...]
    ppermute x10 -> x4, waiting for transfers between devices: 39.4 us -> 8.05 us  [from_behind(): lax.ppermute(shard, axis, [(i, (i + by) % devices) for i in range(devices)])]
    ppermute x10 -> x4, starting transfers between devices: 35.8 us -> 14.3 us  [from_behind(): lax.ppermute(shard, axis, [(i, (i + by) % devices) for i in range(devices)])]
    broadcast_in_dim x5 -> x0, other arithmetic: 9.22 us -> none  [the longest x1 2.99 us: on_device(): grad_values[None, None]]
  transfers between devices with their start and end apart: 17 -> 6, of which waited for: 10 -> 3; matrix products, arithmetic and copies ran while one was open for 24% -> 0% of each run, Pallas kernels for 0% -> 17%
where the time goes in v1:
time: 208 us; the launch traced here: 205 us
  waiting for transfers between devices  85.4 us (41%)
  starting transfers between devices  70.2 us (34%)
  Pallas kernels  42.8 us (21%)
  local copies, waits for them, and re-layouts  4.74 us (2%)
    all_to_all x2, waiting for transfers between devices, exchange(): lax.all_to_all(blocks, 'frame', split_axis=0, concat_axis=0, tiled=True)  77.4 us
    all_to_all x2, starting transfers between devices, exchange(): lax.all_to_all(blocks, 'frame', split_axis=0, concat_axis=0, tiled=True)  55.9 us
    pallas_call x1, Pallas kernels, cross(): pl.pallas_call(cross_kernel, grid=(pairs,), in_specs=[column_spec] * 2 +...  19.4 us
    ppermute x4, starting transfers between devices, from_behind(): lax.ppermute(shard, axis, [(i, (i + by) % devices) for i in range(devices)])  14.3 us
    ppermute x4, waiting for transfers between devices, from_behind(): lax.ppermute(shard, axis, [(i, (i + by) % devices) for i in range(devices)])  8.05 us
    pallas_call x1, Pallas kernels, temporal(): pl.pallas_call(temporal_kernel, grid=(positions // per_step,), in_specs=[...  7.26 us
    unnamed x10, local copies, waits for them, and re-layouts  4.74 us
    pallas_call x1, Pallas kernels, finish(): pl.pallas_call(finish_kernel, grid=(pairs // per_step,), in_specs=[pl.Blo...  4.57 us
  transfers between devices with their start and end apart: 6, of which 3 were waited for; matrix products, arithmetic and copies ran while one was open for 0% of the time, Pallas kernels for 17%

profile of v1, /device:TPU:1, one launch (start us, length us, event | category | flops | bytes accessed | tf_op | source)
XLA Modules:
  0.0 204.6 jit_solution(4758591799677845283)
XLA Ops:
  1.3 3.5 %mark.1.kv_ref.own_ref = bf16[8,2,256,128]{3,2,1,0:T(8,128)(2,1)} custom-call(s32[1,1]{1,0:T(1,128)S(6)} %copy.9.count_ref, bf16[256,1024]{1,0:T(8,128)(2,1)} %bitcast.15, bf16[256,1024]{1,0:T(8,128)(2,1)} %bitcast.16), custom_call_target="tpu_custom_call" | custom-call | flops 262144 | bytes 2097152 | tf_op jit(solution)/shard_map/mark/pallas_call | solution.py:46
  4.8 3.9 %collective-permute-start = (bf16[8,2,256,128]{3,2,1,0:T(8,128)(2,1)}, bf16[8,2,256,128]{3,2,1,0:T(8,128)(2,1)S(1)}, u32[]{:S(2)}, u32[]{:S(2)}) collective-permute-start(bf16[8,2,256,128]{3,2,1,0:T(8,128)(2,1)} %mark.1.kv_ref.own_ref), channel_id=1, source_target_pairs={{0,64},{64,128},{128,192},{192,256},{256,320},{320,384},{384,448},... | collective-permute-start | bytes 3145736 | tf_op jit(solution)/shard_map/ppermute | solution.py:291
  8.7 5.0 %collective-permute-start.1 = (bf16[8,2,256,128]{3,2,1,0:T(8,128)(2,1)}, bf16[8,2,256,128]{3,2,1,0:T(8,128)(2,1)S(1)}, u32[]{:S(2)}, u32[]{:S(2)}) collective-permute-start(bf16[8,2,256,128]{3,2,1,0:T(8,128)(2,1)} %mark.1.kv_ref.own_ref), channel_id=1, source_target_pairs={{0,448},{64,0},{128,64},{192,128},{256,192},{320,256},{384,320},{4... | collective-permute-start | bytes 3145736 | tf_op jit(solution)/shard_map/ppermute | solution.py:291
  13.7 3.9 %pack.1 = bf16[8,8,4,32,128]{4,3,2,1,0:T(8,128)(2,1)} custom-call(bf16[256,1024]{1,0:T(8,128)(2,1)} %bitcast.17, bf16[8,2,256,128]{3,2,1,0:T(8,128)(2,1)} %mark.1.kv_ref.own_ref, bf16[256,1024]{1,0:T(8,128)(2,1)} %bitcast.19), custom_call_target="tpu_custom_call" | custom-call | flops 262144 | bytes 4194304 | tf_op jit(solution)/shard_map/pack/pallas_call | solution.py:78
  17.6 16.8 %all-to-all-start = ((bf16[64,128,128]{2,1,0:T(8,128)(2,1)}), bf16[64,128,128]{2,1,0:T(8,128)(2,1)}, u32[]{:S(2)}, u32[]{:S(2)}) async-start(bf16[64,128,128]{2,1,0:T(8,128)(2,1)} %bitcast.13), calls=%async_computation | async-start | bytes 4194304 | tf_op jit(solution)/shard_map/all_to_all | solution.py:295
  34.4 0.0 collective-permute-done.low_ref
  34.4 0.0 copy-start.3
  34.4 0.0 collective-permute-done.1.up_ref
  34.5 1.0 copy-done.3
  35.4 1.0 copy-done.4
  36.5 19.4 %cross_view.1 = (f32[256,1024]{1,0:T(8,128)}, f32[256,1024]{1,0:T(8,128)}, f32[8,2,256,128]{3,2,1,0:T(8,128)}, bf16[8,2,256,128]{3,2,1,0:T(8,128)(2,1)}, bf16[8,2,256,128]{3,2,1,0:T(8,128)(2,1)}) custom-call(bf16[256,1024]{1,0:T(8,128)(2,1)} %bitcast.18, bf16[256,1024]{1,0:T(8,128)(2,1)} %bitcast.20, bf16[8,2,256,128]{3,2,1,0:T(8,128)(2,1)} %mark.1.kv_ref.own_ref, ...), custom_call_target="tpu_custom_call" | custom-call | flops 671088640000 | bytes 12582912 | tf_op jit(solution)/shard_map/cross_view/pallas_call | solution.py:149
  55.9 3.5 %collective-permute-start.2 = (bf16[8,2,256,128]{3,2,1,0:T(8,128)(2,1)}, bf16[8,2,256,128]{3,2,1,0:T(8,128)(2,1)S(1)}, u32[]{:S(2)}, u32[]{:S(2)}) collective-permute-start(bf16[8,2,256,128]{3,2,1,0:T(8,128)(2,1)} %get-tuple-element.22), channel_id=1, source_target_pairs={{0,448},{64,0},{128,64},{192,128},{256,192},{320,256},{384,320},{4... | collective-permute-start | bytes 3145736 | tf_op jit(solution)/shard_map/ppermute | solution.py:291
  59.3 1.9 collective-permute-start.3
  61.3 29.1 %all-to-all-done = bf16[64,128,128]{2,1,0:T(8,128)(2,1)} async-done(((bf16[64,128,128]{2,1,0:T(8,128)(2,1)}), bf16[64,128,128]{2,1,0:T(8,128)(2,1)}, u32[]{:S(2)}, u32[]{:S(2)}) %all-to-all-start) | async-done | bytes 2097184 | tf_op jit(solution)/shard_map/all_to_all | solution.py:295
  90.3 7.3 %temporal.1 = bf16[64,4,32,128]{3,2,1,0:T(8,128)(2,1)} custom-call(bf16[64,4,32,128]{3,2,1,0:T(8,128)(2,1)} %bitcast.5.y_ref), custom_call_target="tpu_custom_call" | custom-call | flops 201326592 | bytes 4194304 | tf_op jit(solution)/shard_map/temporal/pallas_call | solution.py:213
  97.6 8.0 %collective-permute-done.2.low_ref = bf16[8,2,256,128]{3,2,1,0:T(8,128)(2,1)S(1)} collective-permute-done((bf16[8,2,256,128]{3,2,1,0:T(8,128)(2,1)}, bf16[8,2,256,128]{3,2,1,0:T(8,128)(2,1)S(1)}, u32[]{:S(2)}, u32[]{:S(2)}) %collective-permute-start.2) | collective-permute-done | bytes 1048608 | tf_op jit(solution)/shard_map/ppermute | solution.py:291
  105.6 0.0 collective-permute-done.3.up_ref
  105.6 1.1 copy-done.2
  106.7 0.3 copy-done.1
  107.0 39.1 %all-to-all-start.1 = ((bf16[64,128,128]{2,1,0:T(8,128)(2,1)}), bf16[64,128,128]{2,1,0:T(8,128)(2,1)S(1)}, u32[]{:S(2)}, u32[]{:S(2)}) async-start(bf16[64,128,128]{2,1,0:T(8,128)(2,1)} %bitcast.14), calls=%async_computation.1 | async-start | bytes 4194304 | tf_op jit(solution)/shard_map/all_to_all | solution.py:295
  146.1 4.3 %total.1 = (f32[256,1024]{1,0:T(8,128)}, f32[256,1024]{1,0:T(8,128)}) custom-call(f32[8,2,256,128]{3,2,1,0:T(8,128)} %get-tuple-element.27.own_ref, bf16[8,2,256,128]{3,2,1,0:T(8,128)(2,1)} %copy-done.1, bf16[8,2,256,128]{3,2,1,0:T(8,128)(2,1)} %copy-done.2), custom_call_target="tpu_custom_call" | custom-call | flops 1048576 | bytes 6291456 | tf_op jit(solution)/shard_map/total/pallas_call | solution.py:245
  150.4 48.3 %all-to-all-done.1 = bf16[64,128,128]{2,1,0:T(8,128)(2,1)S(1)} async-done(((bf16[64,128,128]{2,1,0:T(8,128)(2,1)}), bf16[64,128,128]{2,1,0:T(8,128)(2,1)S(1)}, u32[]{:S(2)}, u32[]{:S(2)}) %all-to-all-start.1) | async-done | bytes 2097184 | tf_op jit(solution)/shard_map/all_to_all | solution.py:295
  198.7 1.3 copy-done
  200.0 4.6 %finish.1 = (bf16[256,1024]{1,0:T(8,128)(2,1)}, bf16[256,1024]{1,0:T(8,128)(2,1)}, bf16[256,1024]{1,0:T(8,128)(2,1)}, bf16[256,1024]{1,0:T(8,128)(2,1)}) custom-call(bf16[8,8,4,32,128]{4,3,2,1,0:T(8,128)(2,1)} %bitcast.12, f32[256,1024]{1,0:T(8,128)} %get-tuple-element.25.refs_0_, f32[256,1024]{1,0:T(8,128)} %get-tuple-element.26.refs_1_, ...), custom_call_target="tpu_custom_call" | custom-call | flops 1048576 | bytes 8388608 | tf_op jit(solution)/shard_map/finish/pallas_call | solution.py:274
  (4 shorter events, 0.0 us)
Async XLA Ops:
  4.8 29.7 %collective-permute-start = (bf16[8,2,256,128]{3,2,1,0:T(8,128)(2,1)}, bf16[8,2,256,128]{3,2,1,0:T(8,128)(2,1)S(1)}, u32[]{:S(2)}, u32[]{:S(2)}) collective-permute-start(bf16[8,2,256,128]{3,2,1,0:T(8,128)(2,1)} %mark.1.kv_ref.own_ref), channel_id=1, source_target_pairs={{0,64},{64,128},{128,192},{192,256},{256,320},{320,384},{384,448},... | collective-permute-start | bytes 3145736 | tf_op jit(solution)/shard_map/ppermute | solution.py:291
  8.7 25.7 %collective-permute-start.1 = (bf16[8,2,256,128]{3,2,1,0:T(8,128)(2,1)}, bf16[8,2,256,128]{3,2,1,0:T(8,128)(2,1)S(1)}, u32[]{:S(2)}, u32[]{:S(2)}) collective-permute-start(bf16[8,2,256,128]{3,2,1,0:T(8,128)(2,1)} %mark.1.kv_ref.own_ref), channel_id=1, source_target_pairs={{0,448},{64,0},{128,64},{192,128},{256,192},{320,256},{384,320},{4... | collective-permute-start | bytes 3145736 | tf_op jit(solution)/shard_map/ppermute | solution.py:291
  17.6 72.7 %all-to-all-start = ((bf16[64,128,128]{2,1,0:T(8,128)(2,1)}), bf16[64,128,128]{2,1,0:T(8,128)(2,1)}, u32[]{:S(2)}, u32[]{:S(2)}) async-start(bf16[64,128,128]{2,1,0:T(8,128)(2,1)} %bitcast.13), calls=%async_computation | async-start | bytes 4194304 | tf_op jit(solution)/shard_map/all_to_all | solution.py:295
  34.4 1.0 copy-start.3
  35.4 1.0 copy-start.4
  55.9 49.8 %collective-permute-start.2 = (bf16[8,2,256,128]{3,2,1,0:T(8,128)(2,1)}, bf16[8,2,256,128]{3,2,1,0:T(8,128)(2,1)S(1)}, u32[]{:S(2)}, u32[]{:S(2)}) collective-permute-start(bf16[8,2,256,128]{3,2,1,0:T(8,128)(2,1)} %get-tuple-element.22), channel_id=1, source_target_pairs={{0,448},{64,0},{128,64},{192,128},{256,192},{320,256},{384,320},{4... | collective-permute-start | bytes 3145736 | tf_op jit(solution)/shard_map/ppermute | solution.py:291
  59.3 46.3 %collective-permute-start.3 = (bf16[8,2,256,128]{3,2,1,0:T(8,128)(2,1)}, bf16[8,2,256,128]{3,2,1,0:T(8,128)(2,1)S(1)}, u32[]{:S(2)}, u32[]{:S(2)}) collective-permute-start(bf16[8,2,256,128]{3,2,1,0:T(8,128)(2,1)} %get-tuple-element.23), channel_id=1, source_target_pairs={{0,64},{64,128},{128,192},{192,256},{256,320},{320,384},{384,448},... | collective-permute-start | bytes 3145736 | tf_op jit(solution)/shard_map/ppermute | solution.py:291
  105.6 1.4 copy-start.1
  105.6 1.1 copy-start.2
  107.0 91.7 %all-to-all-start.1 = ((bf16[64,128,128]{2,1,0:T(8,128)(2,1)}), bf16[64,128,128]{2,1,0:T(8,128)(2,1)S(1)}, u32[]{:S(2)}, u32[]{:S(2)}) async-start(bf16[64,128,128]{2,1,0:T(8,128)(2,1)} %bitcast.14), calls=%async_computation.1 | async-start | bytes 4194304 | tf_op jit(solution)/shard_map/all_to_all | solution.py:295
  198.7 1.3 copy-start

commit v2 on v1

--- a/solution.py
+++ b/solution.py
@@ -13,6 +13,7 @@
 SCALE = HEAD_DIM ** (-0.5)
 ROW_T = (((1,), (1,)), ((), ()))
 VMEM_BYTES = 60 * 1024 * 1024
+ROOMY_BYTES = 24 * 1024 * 1024
 
 
 def contract(left, right, dims):
@@ -23,74 +24,52 @@
     return jnp.dot(left, right, preferred_element_type=jnp.float32)
 
 
-def params():
-    return pltpu.CompilerParams(vmem_limit_bytes=VMEM_BYTES)
-
-
-def mark_kernel(count_ref, k_ref, v_ref, kv_ref):
-    positions = lax.broadcasted_iota(jnp.int32, k_ref.shape, 0)
+def params(limit=VMEM_BYTES):
+    return pltpu.CompilerParams(vmem_limit_bytes=limit)
+
+
+def pack_kernel(count_ref, q_ref, k_ref, v_ref, g_ref, x_ref, kv_ref):
+    blocks, pairs, _, rows, _ = x_ref.shape
+    height = k_ref.shape[0]
+    positions = lax.broadcasted_iota(jnp.int32, k_ref.shape, 0) + pl.program_id(0) * height
     wide = k_ref[...].astype(jnp.float32)
     marked = jnp.where(positions < count_ref[0, 0], wide, MARK).astype(jnp.bfloat16)
     values = v_ref[...]
-    for pair in range(kv_ref.shape[0]):
-        columns = slice(pair * PAIR, (pair + 1) * PAIR)
-        kv_ref[pair, 0] = marked[:, columns]
-        kv_ref[pair, 1] = values[:, columns]
-
-
-def mark(count, keys, values):
-    length, width = keys.shape
-    pairs = width // PAIR
-    per_step = 2
-    column_spec = pl.BlockSpec((length, per_step * PAIR), lambda j: (0, j))
-    return pl.pallas_call(
-        mark_kernel,
-        grid=(pairs // per_step,),
-        in_specs=[pl.BlockSpec(memory_space=pltpu.SMEM)] + [column_spec] * 2,
-        out_specs=pl.BlockSpec((per_step, 2, length, PAIR), lambda j: (j, 0, 0, 0)),
-        out_shape=jax.ShapeDtypeStruct((pairs, 2, length, PAIR), jnp.bfloat16),
-        compiler_params=params(),
-        cost_estimate=pl.CostEstimate(
-            flops=length * width, bytes_accessed=8 * length * width, transcendentals=0
-        ),
-        name="mark",
-    )(count, keys, values)
-
-
-def pack_kernel(q_ref, kv_ref, g_ref, x_ref):
-    blocks, pairs, _, rows, _ = x_ref.shape
     queries = q_ref[...]
     cotangents = g_ref[...]
     for pair in range(pairs):
         columns = slice(pair * PAIR, (pair + 1) * PAIR)
-        parts = (queries[:, columns], kv_ref[pair, 0], kv_ref[pair, 1], cotangents[:, columns])
-        for index, part in enumerate(parts):
-            x_ref[:, pair, index] = part.reshape(blocks, rows, PAIR)
-
-
-def pack(queries, marked, cotangents, frames):
+        kv_ref[pair, 0] = marked[:, columns]
+        kv_ref[pair, 1] = values[:, columns]
+        for index, whole in enumerate((queries, marked, values, cotangents)):
+            x_ref[:, pair, index] = whole[:, columns].reshape(blocks, rows, PAIR)
+
+
+def pack(count, queries, keys, values, cotangents, frames):
     length, width = queries.shape
     pairs = width // PAIR
     blocks = frames // pairs
     rows = length // blocks
     per_step = 2
-    column_spec = pl.BlockSpec((length, per_step * PAIR), lambda j: (0, j))
+    row_spec = pl.BlockSpec((per_step * rows, width), lambda i: (i, 0))
     return pl.pallas_call(
         pack_kernel,
-        grid=(pairs // per_step,),
-        in_specs=[
-            column_spec,
-            pl.BlockSpec((per_step, 2, length, PAIR), lambda j: (j, 0, 0, 0)),
-            column_spec,
+        grid=(blocks // per_step,),
+        in_specs=[pl.BlockSpec(memory_space=pltpu.SMEM)] + [row_spec] * 4,
+        out_specs=[
+            pl.BlockSpec((per_step, pairs, 4, rows, PAIR), lambda i: (i, 0, 0, 0, 0)),
+            pl.BlockSpec((pairs, 2, per_step * rows, PAIR), lambda i: (0, 0, i, 0)),
         ],
-        out_specs=pl.BlockSpec((blocks, per_step, 4, rows, PAIR), lambda j: (0, j, 0, 0, 0)),
-        out_shape=jax.ShapeDtypeStruct((blocks, pairs, 4, rows, PAIR), jnp.bfloat16),
+        out_shape=[
+            jax.ShapeDtypeStruct((blocks, pairs, 4, rows, PAIR), jnp.bfloat16),
+            jax.ShapeDtypeStruct((pairs, 2, length, PAIR), jnp.bfloat16),
+        ],
         compiler_params=params(),
         cost_estimate=pl.CostEstimate(
-            flops=length * width, bytes_accessed=16 * length * width, transcendentals=0
+            flops=length * width, bytes_accessed=20 * length * width, transcendentals=0
         ),
         name="pack",
-    )(queries, marked, cotangents)
+    )(count, queries, keys, values, cotangents)
 
 
 def cross_kernel(q_ref, g_ref, own_ref, low_ref, up_ref, o_ref, dq_ref, own_out, low_out, up_out):
@@ -130,8 +109,8 @@
         key_part = multiply(grad_scores, query)
         key_grad = key_part if head == 0 else key_grad + key_part
         value_grad = value_part if head == 0 else value_grad + value_part
-    o_ref[...] = jnp.concatenate(outputs, axis=0).T
-    dq_ref[...] = jnp.concatenate(query_grads, axis=0).T * SCALE
+    o_ref[...] = jnp.concatenate(outputs, axis=0).T.astype(jnp.bfloat16)
+    dq_ref[...] = (jnp.concatenate(query_grads, axis=0).T * SCALE).astype(jnp.bfloat16)
     for index, grad in enumerate((key_grad, value_grad)):
         low_out[0, index] = grad[:length].astype(jnp.bfloat16)
         own_out[0, index] = grad[length : 2 * length]
@@ -143,7 +122,7 @@
     pairs = width // PAIR
     column_spec = pl.BlockSpec((length, PAIR), lambda j: (0, j))
     pair_spec = pl.BlockSpec((1, 2, length, PAIR), lambda j: (j, 0, 0, 0))
-    flat = jax.ShapeDtypeStruct((length, width), jnp.float32)
+    flat = jax.ShapeDtypeStruct((length, width), jnp.bfloat16)
     paired = jax.ShapeDtypeStruct((pairs, 2, length, PAIR), jnp.float32)
     paired_low = jax.ShapeDtypeStruct((pairs, 2, length, PAIR), jnp.bfloat16)
     return pl.pallas_call(
@@ -215,9 +194,9 @@
         grid=(positions // per_step,),
         in_specs=[spec],
         out_specs=spec,
-        out_shape=jax.ShapeDtypeStruct(blocks.shape, jnp.bfloat16),
+        out_shape=pltpu.HBM(blocks.shape, jnp.bfloat16),
         scratch_shapes=[scratch, scratch],
-        compiler_params=params(),
+        compiler_params=params(ROOMY_BYTES),
         cost_estimate=pl.CostEstimate(
             flops=12 * positions * frames * frames * PAIR,
             bytes_accessed=4 * blocks.size,
@@ -227,63 +206,39 @@
     )(blocks)
 
 
-def total_kernel(own_ref, low_ref, up_ref, key_ref, value_ref):
-    for pair in range(own_ref.shape[0]):
-        columns = slice(pair * PAIR, (pair + 1) * PAIR)
-        for index, total_ref in enumerate((key_ref, value_ref)):
-            total_ref[:, columns] = (
-                own_ref[pair, index]
-                + low_ref[pair, index].astype(jnp.float32)
-                + up_ref[pair, index].astype(jnp.float32)
-            )
-
-
-def total(own, lower, upper):
-    pairs, _, length, _ = own.shape
-    per_step = 2
-    pair_spec = pl.BlockSpec((per_step, 2, length, PAIR), lambda j: (j, 0, 0, 0))
-    return pl.pallas_call(
-        total_kernel,
-        grid=(pairs // per_step,),
-        in_specs=[pair_spec] * 3,
-        out_specs=[pl.BlockSpec((length, per_step * PAIR), lambda j: (0, j))] * 2,
-        out_shape=[jax.ShapeDtypeStruct((length, pairs * PAIR), jnp.float32)] * 2,
-        compiler_params=params(),
-        cost_estimate=pl.CostEstimate(
-            flops=2 * own.size, bytes_accessed=12 * own.size, transcendentals=0
-        ),
-        name="total",
-    )(own, lower, upper)
-
-
-def finish_kernel(w_ref, *refs):
-    cross_refs, out_refs = refs[:4], refs[4:]
-    length = cross_refs[0].shape[0]
+def finish_kernel(w_ref, o_ref, dq_ref, own_ref, low_ref, up_ref, *out_refs):
+    height = o_ref.shape[0]
     for pair in range(w_ref.shape[1]):
         columns = slice(pair * PAIR, (pair + 1) * PAIR)
-        for index, (cross_ref, out_ref) in enumerate(zip(cross_refs, out_refs)):
-            returned = w_ref[:, pair, index].reshape(length, PAIR).astype(jnp.float32)
-            out_ref[:, columns] = (cross_ref[:, columns] + returned).astype(jnp.bfloat16)
+        crossed = [ref[:, columns].astype(jnp.float32) for ref in (o_ref, dq_ref)]
+        for index in range(2):
+            parts = [ref[pair, index].astype(jnp.float32) for ref in (own_ref, low_ref, up_ref)]
+            crossed.append(parts[0] + parts[1] + parts[2])
+        for index, out_ref in enumerate(out_refs):
+            returned = w_ref[:, pair, index].reshape(height, PAIR).astype(jnp.float32)
+            out_ref[:, columns] = (crossed[index] + returned).astype(jnp.bfloat16)
 
 
 def finish(returned, *cross_parts):
     length, width = cross_parts[0].shape
     blocks, pairs, _, rows, _ = returned.shape
     per_step = 2
-    column_spec = pl.BlockSpec((length, per_step * PAIR), lambda j: (0, j))
+    row_spec = pl.BlockSpec((per_step * rows, width), lambda i: (i, 0))
+    pair_spec = pl.BlockSpec((pairs, 2, per_step * rows, PAIR), lambda i: (0, 0, i, 0))
     return pl.pallas_call(
         finish_kernel,
-        grid=(pairs // per_step,),
-        in_specs=[pl.BlockSpec((blocks, per_step, 4, rows, PAIR), lambda j: (0, j, 0, 0, 0))]
-        + [column_spec] * 4,
-        out_specs=[column_spec] * 4,
+        grid=(blocks // per_step,),
+        in_specs=[pl.BlockSpec((per_step, pairs, 4, rows, PAIR), lambda i: (i, 0, 0, 0, 0))]
+        + [row_spec] * 2
+        + [pair_spec] * 3,
+        out_specs=[row_spec] * 4,
         out_shape=[jax.ShapeDtypeStruct((length, width), jnp.bfloat16)] * 4,
-        compiler_params=params(),
-        cost_estimate=pl.CostEstimate(
-            flops=4 * length * width, bytes_accessed=32 * length * width, transcendentals=0
+        compiler_params=params(ROOMY_BYTES),
+        cost_estimate=pl.CostEstimate(
+            flops=8 * length * width, bytes_accessed=32 * length * width, transcendentals=0
         ),
         name="finish",
-    )(returned, *cross_parts)
+    )(returned, *(pltpu.with_memory_space_constraint(part, pltpu.HBM) for part in cross_parts))
 
 
 def from_behind(shard, axis, by):
@@ -301,25 +256,19 @@
     value_rows = value_vectors[0, 0]
     grad_rows = out_grad[0, 0]
     frames = lax.axis_size("frame")
-    marked = mark(valid_count, key_rows, value_rows)
+    packed, marked = pack(valid_count, query_rows, key_rows, value_rows, grad_rows, frames)
+    rows = packed.shape[3]
+    arrived = exchange(packed.reshape(frames, 4 * rows, PAIR))
     lower = from_behind(marked, "cam", 1)
     upper = from_behind(marked, "cam", -1)
-    packed = pack(query_rows, marked, grad_rows, frames)
-    rows = packed.shape[3]
-    arrived = exchange(packed.reshape(frames, 4 * rows, PAIR))
+    answered = temporal(arrived.reshape(frames, 4, rows, PAIR))
+    returned = exchange(answered.reshape(frames, 4 * rows, PAIR)).reshape(packed.shape)
     cross_out, cross_query, own_grads, lower_grads, upper_grads = cross(
         query_rows, grad_rows, marked, lower, upper
     )
     from_upper = from_behind(lower_grads, "cam", -1)
     from_lower = from_behind(upper_grads, "cam", 1)
-    arrived, cross_out = lax.optimization_barrier((arrived, cross_out))
-    answered = temporal(arrived.reshape(frames, 4, rows, PAIR))
-    answered, from_upper, from_lower = lax.optimization_barrier(
-        (answered, from_upper, from_lower)
-    )
-    returned = exchange(answered.reshape(frames, 4 * rows, PAIR)).reshape(packed.shape)
-    key_total, value_total = total(own_grads, from_upper, from_lower)
-    results = finish(returned, cross_out, cross_query, key_total, value_total)
+    results = finish(returned, cross_out, cross_query, own_grads, from_upper, from_lower)
     return tuple(result[None, None] for result in results)
 
 

time: 208 us -> 177 us (0.85)
  starting transfers between devices: 70.2 us -> 45.8 us
  Pallas kernels: 42.8 us -> 34.7 us
  waiting for transfers between devices: 85.4 us -> 90.5 us
  local copies, waits for them, and re-layouts: 4.74 us -> 1.01 us
    ppermute x4, waiting for transfers between devices: 8.05 us -> 45 us  [from_behind(): lax.ppermute(shard, axis, [(i, (i + by) % devices) for i in range(devices)])]
    all_to_all x2, waiting for transfers between devices: 77.4 us -> 45.5 us  [exchange(): lax.all_to_all(blocks, 'frame', split_axis=0, concat_axis=0, tiled=True)]
    all_to_all x2, starting transfers between devices: 55.9 us -> 33.3 us  [exchange(): lax.all_to_all(blocks, 'frame', split_axis=0, concat_axis=0, tiled=True)]
    pallas_call x4 -> x2, Pallas kernels: 16.2 us -> 9.17 us  [the longest x1 4.98 us: finish(): pl.pallas_call(finish_kernel, grid=(blocks // per_step,), in_specs=[pl.Bl...]
    unnamed x10 -> x6, local copies, waits for them, and re-layouts: 4.74 us -> 1.01 us
  transfers between devices with their start and end apart: 6 -> 6, of which waited for: 3 -> 3; matrix products, arithmetic and copies ran while one was open for 0% -> 0% of each run, Pallas kernels for 17% -> 15%
where the time goes in v2:
time: 177 us; the launch traced here: 173 us
  waiting for transfers between devices  90.5 us (51%)
  starting transfers between devices  45.8 us (26%)
  Pallas kernels  34.7 us (20%)
    all_to_all x2, waiting for transfers between devices, exchange(): lax.all_to_all(blocks, 'frame', split_axis=0, concat_axis=0, tiled=True)  45.5 us
    ppermute x4, waiting for transfers between devices, from_behind(): lax.ppermute(shard, axis, [(i, (i + by) % devices) for i in range(devices)])  45 us
    all_to_all x2, starting transfers between devices, exchange(): lax.all_to_all(blocks, 'frame', split_axis=0, concat_axis=0, tiled=True)  33.3 us
    pallas_call x1, Pallas kernels, cross(): pl.pallas_call(cross_kernel, grid=(pairs,), in_specs=[column_spec] * 2 +...  19.4 us
    ppermute x4, starting transfers between devices, from_behind(): lax.ppermute(shard, axis, [(i, (i + by) % devices) for i in range(devices)])  12.5 us
    pallas_call x1, Pallas kernels, temporal(): pl.pallas_call(temporal_kernel, grid=(positions // per_step,), in_specs=[...  6.18 us
    pallas_call x1, Pallas kernels, finish(): pl.pallas_call(finish_kernel, grid=(blocks // per_step,), in_specs=[pl.Bl...  4.98 us
    pallas_call x1, Pallas kernels, pack(): pl.pallas_call(pack_kernel, grid=(blocks // per_step,), in_specs=[pl.Bloc...  4.19 us
  transfers between devices with their start and end apart: 6, of which 3 were waited for; matrix products, arithmetic and copies ran while one was open for 0% of the time, Pallas kernels for 15%

profile of v2, /device:TPU:1, one launch (start us, length us, event | category | flops | bytes accessed | tf_op | source)
XLA Modules:
  0.0 173.4 jit_solution(7018379725892221304)
XLA Ops:
  1.3 4.2 %pack.1 = (bf16[8,8,4,32,128]{4,3,2,1,0:T(8,128)(2,1)}, bf16[8,2,256,128]{3,2,1,0:T(8,128)(2,1)}) custom-call(s32[1,1]{1,0:T(1,128)S(6)} %copy.9.count_ref, bf16[256,1024]{1,0:T(8,128)(2,1)} %bitcast.17, bf16[256,1024]{1,0:T(8,128)(2,1)} %bitcast.15, bf16[256,1024]{1,0:T(8,128)(2,1)} %bitcast.16, bf16[256,1024]{1,0:T(8,128)(2,1)} %bitcast.19), custom_call_target="tpu_custom_call" | custom-call | flops 262144 | bytes 5242880 | tf_op jit(solution)/shard_map/pack/pallas_call | solution.py:55
  5.5 0.0 copy-start.2
  5.5 17.8 %all-to-all-start = ((bf16[64,128,128]{2,1,0:T(8,128)(2,1)}), bf16[64,128,128]{2,1,0:T(8,128)(2,1)S(1)}, u32[]{:S(2)}, u32[]{:S(2)}) async-start(bf16[64,128,128]{2,1,0:T(8,128)(2,1)} %bitcast.14), calls=%async_computation | async-start | bytes 4194304 | tf_op jit(solution)/shard_map/all_to_all | solution.py:250
  23.2 0.0 copy-done.2
  23.2 5.3 %collective-permute-start.1 = (bf16[8,2,256,128]{3,2,1,0:T(8,128)(2,1)S(1)}, bf16[8,2,256,128]{3,2,1,0:T(8,128)(2,1)}, u32[]{:S(2)}, u32[]{:S(2)}) collective-permute-start(bf16[8,2,256,128]{3,2,1,0:T(8,128)(2,1)S(1)} %copy-done.2), channel_id=1, source_target_pairs={{0,448},{64,0},{128,64},{192,128},{256,192},{320,256},{384,320},{4... | collective-permute-start | bytes 3145736 | tf_op jit(solution)/shard_map/ppermute | solution.py:246
  28.6 1.9 %collective-permute-start = (bf16[8,2,256,128]{3,2,1,0:T(8,128)(2,1)S(1)}, bf16[8,2,256,128]{3,2,1,0:T(8,128)(2,1)}, u32[]{:S(2)}, u32[]{:S(2)}) collective-permute-start(bf16[8,2,256,128]{3,2,1,0:T(8,128)(2,1)S(1)} %copy-done.2), channel_id=1, source_target_pairs={{0,64},{64,128},{128,192},{192,256},{256,320},{320,384},{384,448},... | collective-permute-start | bytes 3145736 | tf_op jit(solution)/shard_map/ppermute | solution.py:246
  30.5 45.5 %all-to-all-done = bf16[64,128,128]{2,1,0:T(8,128)(2,1)S(1)} async-done(((bf16[64,128,128]{2,1,0:T(8,128)(2,1)}), bf16[64,128,128]{2,1,0:T(8,128)(2,1)S(1)}, u32[]{:S(2)}, u32[]{:S(2)}) %all-to-all-start) | async-done | bytes 2097184 | tf_op jit(solution)/shard_map/all_to_all | solution.py:250
  76.0 6.2 %temporal.1 = bf16[64,4,32,128]{3,2,1,0:T(8,128)(2,1)} custom-call(bf16[64,4,32,128]{3,2,1,0:T(8,128)(2,1)S(1)} %bitcast.12), custom_call_target="tpu_custom_call" | custom-call | flops 201326592 | bytes 4194304 | tf_op jit(solution)/shard_map/temporal/pallas_call | solution.py:192
  82.2 15.6 %all-to-all-start.1 = ((bf16[64,128,128]{2,1,0:T(8,128)(2,1)}), bf16[64,128,128]{2,1,0:T(8,128)(2,1)}, u32[]{:S(2)}, u32[]{:S(2)}) async-start(bf16[64,128,128]{2,1,0:T(8,128)(2,1)} %bitcast.13), calls=%async_computation.1 | async-start | bytes 4194304 | tf_op jit(solution)/shard_map/all_to_all | solution.py:250
  97.7 0.0 collective-permute-done.1.up_ref
  97.7 0.0 collective-permute-done.low_ref
  97.8 19.4 %cross_view.1 = (bf16[256,1024]{1,0:T(8,128)(2,1)}, bf16[256,1024]{1,0:T(8,128)(2,1)}, f32[8,2,256,128]{3,2,1,0:T(8,128)}, bf16[8,2,256,128]{3,2,1,0:T(8,128)(2,1)}, bf16[8,2,256,128]{3,2,1,0:T(8,128)(2,1)}) custom-call(bf16[256,1024]{1,0:T(8,128)(2,1)} %bitcast.18, bf16[256,1024]{1,0:T(8,128)(2,1)} %bitcast.20, ...), custom_call_target="tpu_custom_call" | custom-call | flops 671088640000 | bytes 12582912 | tf_op jit(solution)/shard_map/cross_view/pallas_call | solution.py:128
  117.1 1.9 %collective-permute-start.2 = (bf16[8,2,256,128]{3,2,1,0:T(8,128)(2,1)}, bf16[8,2,256,128]{3,2,1,0:T(8,128)(2,1)S(1)}, u32[]{:S(2)}, u32[]{:S(2)}) collective-permute-start(bf16[8,2,256,128]{3,2,1,0:T(8,128)(2,1)} %get-tuple-element.20), channel_id=1, source_target_pairs={{0,448},{64,0},{128,64},{192,128},{256,192},{320,256},{384,320},{4... | collective-permute-start | bytes 3145736 | tf_op jit(solution)/shard_map/ppermute | solution.py:246
  119.0 3.4 %collective-permute-start.3 = (bf16[8,2,256,128]{3,2,1,0:T(8,128)(2,1)}, bf16[8,2,256,128]{3,2,1,0:T(8,128)(2,1)S(1)}, u32[]{:S(2)}, u32[]{:S(2)}) collective-permute-start(bf16[8,2,256,128]{3,2,1,0:T(8,128)(2,1)} %get-tuple-element.21), channel_id=1, source_target_pairs={{0,64},{64,128},{128,192},{192,256},{256,320},{320,384},{384,448},... | collective-permute-start | bytes 3145736 | tf_op jit(solution)/shard_map/ppermute | solution.py:246
  122.4 44.4 %collective-permute-done.2.low_ref = bf16[8,2,256,128]{3,2,1,0:T(8,128)(2,1)S(1)} collective-permute-done((bf16[8,2,256,128]{3,2,1,0:T(8,128)(2,1)}, bf16[8,2,256,128]{3,2,1,0:T(8,128)(2,1)S(1)}, u32[]{:S(2)}, u32[]{:S(2)}) %collective-permute-start.2) | collective-permute-done | bytes 1048608 | tf_op jit(solution)/shard_map/ppermute | solution.py:246
  166.8 0.0 copy-start
  166.8 0.6 collective-permute-done.3.up_ref
  167.4 0.0 copy-start.1
  167.4 0.0 all-to-all-done.1
  167.4 0.4 copy-done
  167.8 0.6 copy-done.1
  168.4 5.0 %finish.1 = (bf16[256,1024]{1,0:T(8,128)(2,1)}, bf16[256,1024]{1,0:T(8,128)(2,1)}, bf16[256,1024]{1,0:T(8,128)(2,1)}, bf16[256,1024]{1,0:T(8,128)(2,1)}) custom-call(bf16[8,8,4,32,128]{4,3,2,1,0:T(8,128)(2,1)} %bitcast.7.w_ref, bf16[256,1024]{1,0:T(8,128)(2,1)} %get-tuple-element.17.o_ref, bf16[256,1024]{1,0:T(8,128)(2,1)} %get-tuple-element.18.dq_ref, ...), custom_call_target="tpu_custom_call" | custom-call | flops 2097152 | bytes 8388608 | tf_op jit(solution)/shard_map/finish/pallas_call | solution.py:228
Async XLA Ops:
  5.5 17.8 %copy-start.2 = (bf16[8,2,256,128]{3,2,1,0:T(8,128)(2,1)S(1)}, bf16[8,2,256,128]{3,2,1,0:T(8,128)(2,1)}, u32[]{:S(2)}) copy-start(bf16[8,2,256,128]{3,2,1,0:T(8,128)(2,1)} %get-tuple-element.16.own_ref) | copy-start | bytes 3145732
  5.5 70.5 %all-to-all-start = ((bf16[64,128,128]{2,1,0:T(8,128)(2,1)}), bf16[64,128,128]{2,1,0:T(8,128)(2,1)S(1)}, u32[]{:S(2)}, u32[]{:S(2)}) async-start(bf16[64,128,128]{2,1,0:T(8,128)(2,1)} %bitcast.14), calls=%async_computation | async-start | bytes 4194304 | tf_op jit(solution)/shard_map/all_to_all | solution.py:250
  23.2 74.5 %collective-permute-start.1 = (bf16[8,2,256,128]{3,2,1,0:T(8,128)(2,1)S(1)}, bf16[8,2,256,128]{3,2,1,0:T(8,128)(2,1)}, u32[]{:S(2)}, u32[]{:S(2)}) collective-permute-start(bf16[8,2,256,128]{3,2,1,0:T(8,128)(2,1)S(1)} %copy-done.2), channel_id=1, source_target_pairs={{0,448},{64,0},{128,64},{192,128},{256,192},{320,256},{384,320},{4... | collective-permute-start | bytes 3145736 | tf_op jit(solution)/shard_map/ppermute | solution.py:246
  28.6 69.2 %collective-permute-start = (bf16[8,2,256,128]{3,2,1,0:T(8,128)(2,1)S(1)}, bf16[8,2,256,128]{3,2,1,0:T(8,128)(2,1)}, u32[]{:S(2)}, u32[]{:S(2)}) collective-permute-start(bf16[8,2,256,128]{3,2,1,0:T(8,128)(2,1)S(1)} %copy-done.2), channel_id=1, source_target_pairs={{0,64},{64,128},{128,192},{192,256},{256,320},{320,384},{384,448},... | collective-permute-start | bytes 3145736 | tf_op jit(solution)/shard_map/ppermute | solution.py:246
  82.2 85.2 %all-to-all-start.1 = ((bf16[64,128,128]{2,1,0:T(8,128)(2,1)}), bf16[64,128,128]{2,1,0:T(8,128)(2,1)}, u32[]{:S(2)}, u32[]{:S(2)}) async-start(bf16[64,128,128]{2,1,0:T(8,128)(2,1)} %bitcast.13), calls=%async_computation.1 | async-start | bytes 4194304 | tf_op jit(solution)/shard_map/all_to_all | solution.py:250
  117.1 49.7 %collective-permute-start.2 = (bf16[8,2,256,128]{3,2,1,0:T(8,128)(2,1)}, bf16[8,2,256,128]{3,2,1,0:T(8,128)(2,1)S(1)}, u32[]{:S(2)}, u32[]{:S(2)}) collective-permute-start(bf16[8,2,256,128]{3,2,1,0:T(8,128)(2,1)} %get-tuple-element.20), channel_id=1, source_target_pairs={{0,448},{64,0},{128,64},{192,128},{256,192},{320,256},{384,320},{4... | collective-permute-start | bytes 3145736 | tf_op jit(solution)/shard_map/ppermute | solution.py:246
  119.0 48.4 %collective-permute-start.3 = (bf16[8,2,256,128]{3,2,1,0:T(8,128)(2,1)}, bf16[8,2,256,128]{3,2,1,0:T(8,128)(2,1)S(1)}, u32[]{:S(2)}, u32[]{:S(2)}) collective-permute-start(bf16[8,2,256,128]{3,2,1,0:T(8,128)(2,1)} %get-tuple-element.21), channel_id=1, source_target_pairs={{0,64},{64,128},{128,192},{192,256},{256,320},{320,384},{384,448},... | collective-permute-start | bytes 3145736 | tf_op jit(solution)/shard_map/ppermute | solution.py:246
  166.8 1.0 copy-start
  167.4 1.0 copy-start.1

commit v3 on v1

--- a/solution.py
+++ b/solution.py
@@ -13,6 +13,7 @@
 SCALE = HEAD_DIM ** (-0.5)
 ROW_T = (((1,), (1,)), ((), ()))
 VMEM_BYTES = 60 * 1024 * 1024
+ROOMY_BYTES = 24 * 1024 * 1024
 
 
 def contract(left, right, dims):
@@ -23,81 +24,70 @@
     return jnp.dot(left, right, preferred_element_type=jnp.float32)
 
 
-def params():
-    return pltpu.CompilerParams(vmem_limit_bytes=VMEM_BYTES)
-
-
-def mark_kernel(count_ref, k_ref, v_ref, kv_ref):
-    positions = lax.broadcasted_iota(jnp.int32, k_ref.shape, 0)
+def params(limit=VMEM_BYTES):
+    return pltpu.CompilerParams(vmem_limit_bytes=limit)
+
+
+def mark_kernel(count_ref, k_ref, marked_ref):
+    positions = lax.broadcasted_iota(jnp.int32, k_ref.shape, 0) + pl.program_id(0) * k_ref.shape[0]
     wide = k_ref[...].astype(jnp.float32)
-    marked = jnp.where(positions < count_ref[0, 0], wide, MARK).astype(jnp.bfloat16)
-    values = v_ref[...]
-    for pair in range(kv_ref.shape[0]):
-        columns = slice(pair * PAIR, (pair + 1) * PAIR)
-        kv_ref[pair, 0] = marked[:, columns]
-        kv_ref[pair, 1] = values[:, columns]
-
-
-def mark(count, keys, values):
+    marked_ref[...] = jnp.where(positions < count_ref[0, 0], wide, MARK).astype(jnp.bfloat16)
+
+
+def mark(count, keys):
     length, width = keys.shape
-    pairs = width // PAIR
-    per_step = 2
-    column_spec = pl.BlockSpec((length, per_step * PAIR), lambda j: (0, j))
+    row_spec = pl.BlockSpec((length // 2, width), lambda i: (i, 0))
     return pl.pallas_call(
         mark_kernel,
-        grid=(pairs // per_step,),
-        in_specs=[pl.BlockSpec(memory_space=pltpu.SMEM)] + [column_spec] * 2,
-        out_specs=pl.BlockSpec((per_step, 2, length, PAIR), lambda j: (j, 0, 0, 0)),
-        out_shape=jax.ShapeDtypeStruct((pairs, 2, length, PAIR), jnp.bfloat16),
+        grid=(2,),
+        in_specs=[pl.BlockSpec(memory_space=pltpu.SMEM), row_spec],
+        out_specs=row_spec,
+        out_shape=jax.ShapeDtypeStruct(keys.shape, jnp.bfloat16),
         compiler_params=params(),
         cost_estimate=pl.CostEstimate(
-            flops=length * width, bytes_accessed=8 * length * width, transcendentals=0
+            flops=length * width, bytes_accessed=4 * length * width, transcendentals=0
         ),
         name="mark",
-    )(count, keys, values)
-
-
-def pack_kernel(q_ref, kv_ref, g_ref, x_ref):
+    )(count, keys)
+
+
+def pack_kernel(*refs):
+    x_ref = refs[-1]
     blocks, pairs, _, rows, _ = x_ref.shape
-    queries = q_ref[...]
-    cotangents = g_ref[...]
-    for pair in range(pairs):
-        columns = slice(pair * PAIR, (pair + 1) * PAIR)
-        parts = (queries[:, columns], kv_ref[pair, 0], kv_ref[pair, 1], cotangents[:, columns])
-        for index, part in enumerate(parts):
+    for index, ref in enumerate(refs[:-1]):
+        for pair in range(pairs):
+            part = ref[:, pair * PAIR : (pair + 1) * PAIR]
             x_ref[:, pair, index] = part.reshape(blocks, rows, PAIR)
 
 
-def pack(queries, marked, cotangents, frames):
+def pack(queries, keys, values, cotangents, frames):
     length, width = queries.shape
     pairs = width // PAIR
     blocks = frames // pairs
     rows = length // blocks
     per_step = 2
-    column_spec = pl.BlockSpec((length, per_step * PAIR), lambda j: (0, j))
+    row_spec = pl.BlockSpec((per_step * rows, width), lambda i: (i, 0))
     return pl.pallas_call(
         pack_kernel,
-        grid=(pairs // per_step,),
-        in_specs=[
-            column_spec,
-            pl.BlockSpec((per_step, 2, length, PAIR), lambda j: (j, 0, 0, 0)),
-            column_spec,
-        ],
-        out_specs=pl.BlockSpec((blocks, per_step, 4, rows, PAIR), lambda j: (0, j, 0, 0, 0)),
+        grid=(blocks // per_step,),
+        in_specs=[row_spec] * 4,
+        out_specs=pl.BlockSpec((per_step, pairs, 4, rows, PAIR), lambda i: (i, 0, 0, 0, 0)),
         out_shape=jax.ShapeDtypeStruct((blocks, pairs, 4, rows, PAIR), jnp.bfloat16),
         compiler_params=params(),
         cost_estimate=pl.CostEstimate(
             flops=length * width, bytes_accessed=16 * length * width, transcendentals=0
         ),
         name="pack",
-    )(queries, marked, cotangents)
-
-
-def cross_kernel(q_ref, g_ref, own_ref, low_ref, up_ref, o_ref, dq_ref, own_out, low_out, up_out):
+    )(queries, keys, values, cotangents)
+
+
+def cross_kernel(q_ref, g_ref, *refs):
+    key_refs, value_refs = refs[:3], refs[3:6]
+    o_ref, dq_ref, own_out, low_out, up_out = refs[6:]
     length = q_ref.shape[0]
     first = lax.broadcasted_iota(jnp.int32, (length, PAIR), 1) < HEAD_DIM
-    marked = jnp.concatenate([low_ref[0, 0], own_ref[0, 0], up_ref[0, 0]], axis=0)
-    values = jnp.concatenate([low_ref[0, 1], own_ref[0, 1], up_ref[0, 1]], axis=0)
+    marked = jnp.concatenate([ref[...] for ref in key_refs], axis=0)
+    values = jnp.concatenate([ref[...] for ref in value_refs], axis=0)
     wide = marked.astype(jnp.float32)
     invalid = wide > MARK_CUT
     keys_wide = jnp.where(invalid, 0.0, wide)
@@ -130,26 +120,26 @@
         key_part = multiply(grad_scores, query)
         key_grad = key_part if head == 0 else key_grad + key_part
         value_grad = value_part if head == 0 else value_grad + value_part
-    o_ref[...] = jnp.concatenate(outputs, axis=0).T
-    dq_ref[...] = jnp.concatenate(query_grads, axis=0).T * SCALE
+    o_ref[...] = jnp.concatenate(outputs, axis=0).T.astype(jnp.bfloat16)
+    dq_ref[...] = (jnp.concatenate(query_grads, axis=0).T * SCALE).astype(jnp.bfloat16)
     for index, grad in enumerate((key_grad, value_grad)):
         low_out[0, index] = grad[:length].astype(jnp.bfloat16)
         own_out[0, index] = grad[length : 2 * length]
         up_out[0, index] = grad[2 * length :].astype(jnp.bfloat16)
 
 
-def cross(queries, cotangents, own, lower, upper):
+def cross(queries, cotangents, keys, values):
     length, width = queries.shape
     pairs = width // PAIR
     column_spec = pl.BlockSpec((length, PAIR), lambda j: (0, j))
     pair_spec = pl.BlockSpec((1, 2, length, PAIR), lambda j: (j, 0, 0, 0))
-    flat = jax.ShapeDtypeStruct((length, width), jnp.float32)
+    flat = jax.ShapeDtypeStruct((length, width), jnp.bfloat16)
     paired = jax.ShapeDtypeStruct((pairs, 2, length, PAIR), jnp.float32)
     paired_low = jax.ShapeDtypeStruct((pairs, 2, length, PAIR), jnp.bfloat16)
     return pl.pallas_call(
         cross_kernel,
         grid=(pairs,),
-        in_specs=[column_spec] * 2 + [pair_spec] * 3,
+        in_specs=[column_spec] * 8,
         out_specs=[column_spec] * 2 + [pair_spec] * 3,
         out_shape=[flat, flat, paired, paired_low, paired_low],
         compiler_params=params(),
@@ -159,7 +149,7 @@
             transcendentals=48 * length * length,
         ),
         name="cross_view",
-    )(queries, cotangents, own, lower, upper)
+    )(queries, cotangents, *keys, *values)
 
 
 def temporal_kernel(y_ref, z_ref, rows_in, rows_out):
@@ -215,9 +205,9 @@
         grid=(positions // per_step,),
         in_specs=[spec],
         out_specs=spec,
-        out_shape=jax.ShapeDtypeStruct(blocks.shape, jnp.bfloat16),
+        out_shape=pltpu.HBM(blocks.shape, jnp.bfloat16),
         scratch_shapes=[scratch, scratch],
-        compiler_params=params(),
+        compiler_params=params(ROOMY_BYTES),
         cost_estimate=pl.CostEstimate(
             flops=12 * positions * frames * frames * PAIR,
             bytes_accessed=4 * blocks.size,
@@ -235,7 +225,7 @@
                 own_ref[pair, index]
                 + low_ref[pair, index].astype(jnp.float32)
                 + up_ref[pair, index].astype(jnp.float32)
-            )
+            ).astype(jnp.bfloat16)
 
 
 def total(own, lower, upper):
@@ -247,10 +237,12 @@
         grid=(pairs // per_step,),
         in_specs=[pair_spec] * 3,
         out_specs=[pl.BlockSpec((length, per_step * PAIR), lambda j: (0, j))] * 2,
-        out_shape=[jax.ShapeDtypeStruct((length, pairs * PAIR), jnp.float32)] * 2,
+        out_shape=[jax.ShapeDtypeStruct((length, pairs * PAIR), jnp.bfloat16)] * 2,
         compiler_params=params(),
         cost_estimate=pl.CostEstimate(
-            flops=2 * own.size, bytes_accessed=12 * own.size, transcendentals=0
+            flops=10**12,
+            bytes_accessed=12 * own.size,
+            transcendentals=0,
         ),
         name="total",
     )(own, lower, upper)
@@ -258,32 +250,33 @@
 
 def finish_kernel(w_ref, *refs):
     cross_refs, out_refs = refs[:4], refs[4:]
-    length = cross_refs[0].shape[0]
+    height = cross_refs[0].shape[0]
     for pair in range(w_ref.shape[1]):
         columns = slice(pair * PAIR, (pair + 1) * PAIR)
         for index, (cross_ref, out_ref) in enumerate(zip(cross_refs, out_refs)):
-            returned = w_ref[:, pair, index].reshape(length, PAIR).astype(jnp.float32)
-            out_ref[:, columns] = (cross_ref[:, columns] + returned).astype(jnp.bfloat16)
+            returned = w_ref[:, pair, index].reshape(height, PAIR).astype(jnp.float32)
+            crossed = cross_ref[:, columns].astype(jnp.float32)
+            out_ref[:, columns] = (crossed + returned).astype(jnp.bfloat16)
 
 
 def finish(returned, *cross_parts):
     length, width = cross_parts[0].shape
     blocks, pairs, _, rows, _ = returned.shape
     per_step = 2
-    column_spec = pl.BlockSpec((length, per_step * PAIR), lambda j: (0, j))
+    row_spec = pl.BlockSpec((per_step * rows, width), lambda i: (i, 0))
     return pl.pallas_call(
         finish_kernel,
-        grid=(pairs // per_step,),
-        in_specs=[pl.BlockSpec((blocks, per_step, 4, rows, PAIR), lambda j: (0, j, 0, 0, 0))]
-        + [column_spec] * 4,
-        out_specs=[column_spec] * 4,
+        grid=(blocks // per_step,),
+        in_specs=[pl.BlockSpec((per_step, pairs, 4, rows, PAIR), lambda i: (i, 0, 0, 0, 0))]
+        + [row_spec] * 4,
+        out_specs=[row_spec] * 4,
         out_shape=[jax.ShapeDtypeStruct((length, width), jnp.bfloat16)] * 4,
-        compiler_params=params(),
+        compiler_params=params(ROOMY_BYTES),
         cost_estimate=pl.CostEstimate(
             flops=4 * length * width, bytes_accessed=32 * length * width, transcendentals=0
         ),
         name="finish",
-    )(returned, *cross_parts)
+    )(returned, *(pltpu.with_memory_space_constraint(part, pltpu.HBM) for part in cross_parts))
 
 
 def from_behind(shard, axis, by):
@@ -301,22 +294,24 @@
     value_rows = value_vectors[0, 0]
     grad_rows = out_grad[0, 0]
     frames = lax.axis_size("frame")
-    marked = mark(valid_count, key_rows, value_rows)
-    lower = from_behind(marked, "cam", 1)
-    upper = from_behind(marked, "cam", -1)
-    packed = pack(query_rows, marked, grad_rows, frames)
+    lower_values = from_behind(value_rows, "cam", 1)
+    upper_values = from_behind(value_rows, "cam", -1)
+    marked = mark(valid_count, key_rows)
+    lower_keys = from_behind(marked, "cam", 1)
+    upper_keys = from_behind(marked, "cam", -1)
+    packed = pack(query_rows, marked, value_rows, grad_rows, frames)
     rows = packed.shape[3]
     arrived = exchange(packed.reshape(frames, 4 * rows, PAIR))
     cross_out, cross_query, own_grads, lower_grads, upper_grads = cross(
-        query_rows, grad_rows, marked, lower, upper
+        query_rows,
+        grad_rows,
+        (lower_keys, marked, upper_keys),
+        (lower_values, value_rows, upper_values),
     )
     from_upper = from_behind(lower_grads, "cam", -1)
     from_lower = from_behind(upper_grads, "cam", 1)
     arrived, cross_out = lax.optimization_barrier((arrived, cross_out))
     answered = temporal(arrived.reshape(frames, 4, rows, PAIR))
-    answered, from_upper, from_lower = lax.optimization_barrier(
-        (answered, from_upper, from_lower)
-    )
     returned = exchange(answered.reshape(frames, 4 * rows, PAIR)).reshape(packed.shape)
     key_total, value_total = total(own_grads, from_upper, from_lower)
     results = finish(returned, cross_out, cross_query, key_total, value_total)

time: 208 us -> 175 us (0.84); the launches traced: 205 us -> 174 us
  starting transfers between devices: 70.2 us -> 55.3 us
  waiting for transfers between devices: 85.4 us -> 73.2 us
    all_to_all x2, starting transfers between devices: 55.9 us -> 33.7 us  [exchange(): lax.all_to_all(blocks, 'frame', split_axis=0, concat_axis=0, tiled=True)]
    ppermute x4 -> x6, waiting for transfers between devices: 8.05 us -> 0.02 us  [from_behind(): lax.ppermute(shard, axis, [(i, (i + by) % devices) for i in range(devices)])]
    ppermute x4 -> x6, starting transfers between devices: 14.3 us -> 21.6 us  [from_behind(): lax.ppermute(shard, axis, [(i, (i + by) % devices) for i in range(devices)])]
    all_to_all x2, waiting for transfers between devices: 77.4 us -> 73.2 us  [exchange(): lax.all_to_all(blocks, 'frame', split_axis=0, concat_axis=0, tiled=True)]
    unnamed x10 -> x12, local copies, waits for them, and re-layouts: 4.74 us -> 3.21 us
  transfers between devices with their start and end apart: 6 -> 8, of which waited for: 3 -> 2; matrix products, arithmetic and copies ran while one was open for 0% -> 0% of each run, Pallas kernels for 17% -> 20%
where the time goes in v3:
time: 175 us; the launch traced here: 174 us
  waiting for transfers between devices  73.2 us (42%)
  starting transfers between devices  55.3 us (32%)
  Pallas kernels  40.8 us (23%)
  local copies, waits for them, and re-layouts  3.21 us (2%)
    all_to_all x2, waiting for transfers between devices, exchange(): lax.all_to_all(blocks, 'frame', split_axis=0, concat_axis=0, tiled=True)  73.2 us
    all_to_all x2, starting transfers between devices, exchange(): lax.all_to_all(blocks, 'frame', split_axis=0, concat_axis=0, tiled=True)  33.7 us
    ppermute x6, starting transfers between devices, from_behind(): lax.ppermute(shard, axis, [(i, (i + by) % devices) for i in range(devices)])  21.6 us
    pallas_call x1, Pallas kernels, cross(): pl.pallas_call(cross_kernel, grid=(pairs,), in_specs=[column_spec] * 8, o...  19.5 us
    pallas_call x1, Pallas kernels, temporal(): pl.pallas_call(temporal_kernel, grid=(positions // per_step,), in_specs=[...  7.25 us
    pallas_call x1, Pallas kernels, finish(): pl.pallas_call(finish_kernel, grid=(blocks // per_step,), in_specs=[pl.Bl...  4.26 us
    pallas_call x1, Pallas kernels, total(): pl.pallas_call(total_kernel, grid=(pairs // per_step,), in_specs=[pair_sp...  4.04 us
    pallas_call x1, Pallas kernels, pack(): pl.pallas_call(pack_kernel, grid=(blocks // per_step,), in_specs=[row_spe...  3.97 us
  transfers between devices with their start and end apart: 8, of which 2 were waited for; matrix products, arithmetic and copies ran while one was open for 0% of the time, Pallas kernels for 20%

profile of v3, /device:TPU:1, one launch (start us, length us, event | category | flops | bytes accessed | tf_op | source)
XLA Modules:
  0.0 173.9 jit_solution(15143378667014944945)
XLA Ops:
  1.3 1.8 %mark.1.refs_1_ = bf16[256,1024]{1,0:T(8,128)(2,1)} custom-call(s32[1,1]{1,0:T(1,128)S(6)} %copy.9.count_ref, bf16[256,1024]{1,0:T(8,128)(2,1)} %bitcast.14), custom_call_target="tpu_custom_call" | custom-call | flops 262144 | bytes 1048576 | tf_op jit(solution)/shard_map/mark/pallas_call | solution.py:40
  3.1 3.9 %collective-permute-start = (bf16[256,1024]{1,0:T(8,128)(2,1)}, bf16[256,1024]{1,0:T(8,128)(2,1)S(1)}, u32[]{:S(2)}, u32[]{:S(2)}) collective-permute-start(bf16[256,1024]{1,0:T(8,128)(2,1)} %mark.1.refs_1_), channel_id=1, source_target_pairs={{0,64},{64,128},{128,192},{192,256},{256,320},{320,384},{384,448},... | collective-permute-start | bytes 1572872 | tf_op jit(solution)/shard_map/ppermute | solution.py:284
  7.0 5.0 %collective-permute-start.1 = (bf16[256,1024]{1,0:T(8,128)(2,1)}, bf16[256,1024]{1,0:T(8,128)(2,1)S(1)}, u32[]{:S(2)}, u32[]{:S(2)}) collective-permute-start(bf16[256,1024]{1,0:T(8,128)(2,1)} %mark.1.refs_1_), channel_id=1, source_target_pairs={{0,448},{64,0},{128,64},{192,128},{256,192},{320,256},{384,320},{4... | collective-permute-start | bytes 1572872 | tf_op jit(solution)/shard_map/ppermute | solution.py:284
  12.0 1.9 %collective-permute-start.2 = (bf16[256,1024]{1,0:T(8,128)(2,1)}, bf16[256,1024]{1,0:T(8,128)(2,1)S(1)}, u32[]{:S(2)}, u32[]{:S(2)}) collective-permute-start(bf16[256,1024]{1,0:T(8,128)(2,1)} %bitcast.17), channel_id=1, source_target_pairs={{0,64},{64,128},{128,192},{192,256},{256,320},{320,384},{384,448},... | collective-permute-start | bytes 1572872 | tf_op jit(solution)/shard_map/ppermute | solution.py:284
  14.0 5.5 %collective-permute-start.3 = (bf16[256,1024]{1,0:T(8,128)(2,1)}, bf16[256,1024]{1,0:T(8,128)(2,1)S(1)}, u32[]{:S(2)}, u32[]{:S(2)}) collective-permute-start(bf16[256,1024]{1,0:T(8,128)(2,1)} %bitcast.18), channel_id=1, source_target_pairs={{0,448},{64,0},{128,64},{192,128},{256,192},{320,256},{384,320},{4... | collective-permute-start | bytes 1572872 | tf_op jit(solution)/shard_map/ppermute | solution.py:284
  19.4 4.0 %pack.1 = bf16[8,8,4,32,128]{4,3,2,1,0:T(8,128)(2,1)} custom-call(bf16[256,1024]{1,0:T(8,128)(2,1)} %bitcast.15, bf16[256,1024]{1,0:T(8,128)(2,1)} %mark.1.refs_1_, bf16[256,1024]{1,0:T(8,128)(2,1)} %bitcast.19, bf16[256,1024]{1,0:T(8,128)(2,1)} %bitcast.21), custom_call_target="tpu_custom_call" | custom-call | flops 262144 | bytes 4194304 | tf_op jit(solution)/shard_map/pack/pallas_call | solution.py:70
  23.4 17.4 %all-to-all-start = ((bf16[64,128,128]{2,1,0:T(8,128)(2,1)}), bf16[64,128,128]{2,1,0:T(8,128)(2,1)}, u32[]{:S(2)}, u32[]{:S(2)}) async-start(bf16[64,128,128]{2,1,0:T(8,128)(2,1)} %bitcast.12), calls=%async_computation | async-start | bytes 4194304 | tf_op jit(solution)/shard_map/all_to_all | solution.py:288
  40.8 0.0 copy-start.2
  40.8 0.0 copy-start.3
  40.9 0.7 copy-done.2
  41.6 0.2 copy-done.3
  41.8 0.2 copy-done.4
  42.0 0.8 copy-done.5
  42.8 19.5 %cross_view.1 = (bf16[256,1024]{1,0:T(8,128)(2,1)}, bf16[256,1024]{1,0:T(8,128)(2,1)}, f32[8,2,256,128]{3,2,1,0:T(8,128)}, bf16[8,2,256,128]{3,2,1,0:T(8,128)(2,1)}, bf16[8,2,256,128]{3,2,1,0:T(8,128)(2,1)}) custom-call(bf16[256,1024]{1,0:T(8,128)(2,1)} %bitcast.16, bf16[256,1024]{1,0:T(8,128)(2,1)} %bitcast.22, bf16[256,1024]{1,0:T(8,128)(2,1)} %copy-done.2, ...), custom_call_target="tpu_custom_call" | custom-call | flops 671088640000 | bytes 12582912 | tf_op jit(solution)/shard_map/cross_view/pallas_call | solution.py:139
  62.2 1.9 %collective-permute-start.4 = (bf16[8,2,256,128]{3,2,1,0:T(8,128)(2,1)}, bf16[8,2,256,128]{3,2,1,0:T(8,128)(2,1)S(1)}, u32[]{:S(2)}, u32[]{:S(2)}) collective-permute-start(bf16[8,2,256,128]{3,2,1,0:T(8,128)(2,1)} %get-tuple-element.22), channel_id=1, source_target_pairs={{0,448},{64,0},{128,64},{192,128},{256,192},{320,256},{384,320},{4... | collective-permute-start | bytes 3145736 | tf_op jit(solution)/shard_map/ppermute | solution.py:284
  64.2 3.4 %collective-permute-start.5 = (bf16[8,2,256,128]{3,2,1,0:T(8,128)(2,1)}, bf16[8,2,256,128]{3,2,1,0:T(8,128)(2,1)S(1)}, u32[]{:S(2)}, u32[]{:S(2)}) collective-permute-start(bf16[8,2,256,128]{3,2,1,0:T(8,128)(2,1)} %get-tuple-element.23), channel_id=1, source_target_pairs={{0,64},{64,128},{128,192},{192,256},{256,320},{320,384},{384,448},... | collective-permute-start | bytes 3145736 | tf_op jit(solution)/shard_map/ppermute | solution.py:284
  67.5 25.9 %all-to-all-done = bf16[64,128,128]{2,1,0:T(8,128)(2,1)} async-done(((bf16[64,128,128]{2,1,0:T(8,128)(2,1)}), bf16[64,128,128]{2,1,0:T(8,128)(2,1)}, u32[]{:S(2)}, u32[]{:S(2)}) %all-to-all-start) | async-done | bytes 2097184 | tf_op jit(solution)/shard_map/all_to_all | solution.py:288
  93.5 7.2 %temporal.1 = bf16[64,4,32,128]{3,2,1,0:T(8,128)(2,1)} custom-call(bf16[64,4,32,128]{3,2,1,0:T(8,128)(2,1)} %bitcast.5.y_ref), custom_call_target="tpu_custom_call" | custom-call | flops 201326592 | bytes 4194304 | tf_op jit(solution)/shard_map/temporal/pallas_call | solution.py:203
  100.7 16.3 %all-to-all-start.1 = ((bf16[64,128,128]{2,1,0:T(8,128)(2,1)}), bf16[64,128,128]{2,1,0:T(8,128)(2,1)}, u32[]{:S(2)}, u32[]{:S(2)}) async-start(bf16[64,128,128]{2,1,0:T(8,128)(2,1)} %bitcast.13), calls=%async_computation.1 | async-start | bytes 4194304 | tf_op jit(solution)/shard_map/all_to_all | solution.py:288
  117.1 1.0 copy-done
  118.1 0.3 copy-done.1
  118.4 4.0 %total.1 = (bf16[256,1024]{1,0:T(8,128)(2,1)}, bf16[256,1024]{1,0:T(8,128)(2,1)}) custom-call(f32[8,2,256,128]{3,2,1,0:T(8,128)} %get-tuple-element.21.own_ref, bf16[8,2,256,128]{3,2,1,0:T(8,128)(2,1)} %copy-done, bf16[8,2,256,128]{3,2,1,0:T(8,128)(2,1)} %copy-done.1), custom_call_target="tpu_custom_call" | custom-call | flops 999999995904 | bytes 6291456 | tf_op jit(solution)/shard_map/total/pallas_call | solution.py:235
  122.4 47.2 %all-to-all-done.1 = bf16[64,128,128]{2,1,0:T(8,128)(2,1)} async-done(((bf16[64,128,128]{2,1,0:T(8,128)(2,1)}), bf16[64,128,128]{2,1,0:T(8,128)(2,1)}, u32[]{:S(2)}, u32[]{:S(2)}) %all-to-all-start.1) | async-done | bytes 2097184 | tf_op jit(solution)/shard_map/all_to_all | solution.py:288
  169.7 4.3 %finish.1 = (bf16[256,1024]{1,0:T(8,128)(2,1)}, bf16[256,1024]{1,0:T(8,128)(2,1)}, bf16[256,1024]{1,0:T(8,128)(2,1)}, bf16[256,1024]{1,0:T(8,128)(2,1)}) custom-call(bf16[8,8,4,32,128]{4,3,2,1,0:T(8,128)(2,1)} %bitcast.7.w_ref, bf16[256,1024]{1,0:T(8,128)(2,1)} %get-tuple-element.19.refs_0_, bf16[256,1024]{1,0:T(8,128)(2,1)} %get-tuple-element.20.refs_1_, ...), custom_call_target="tpu_custom_call" | custom-call | flops 1048576 | bytes 8388608 | tf_op jit(solution)/shard_map/finish/pallas_call | solution.py:267
  (10 shorter events, 0.0 us)
Async XLA Ops:
  3.1 37.7 %collective-permute-start = (bf16[256,1024]{1,0:T(8,128)(2,1)}, bf16[256,1024]{1,0:T(8,128)(2,1)S(1)}, u32[]{:S(2)}, u32[]{:S(2)}) collective-permute-start(bf16[256,1024]{1,0:T(8,128)(2,1)} %mark.1.refs_1_), channel_id=1, source_target_pairs={{0,64},{64,128},{128,192},{192,256},{256,320},{320,384},{384,448},... | collective-permute-start | bytes 1572872 | tf_op jit(solution)/shard_map/ppermute | solution.py:284
  7.0 33.8 %collective-permute-start.1 = (bf16[256,1024]{1,0:T(8,128)(2,1)}, bf16[256,1024]{1,0:T(8,128)(2,1)S(1)}, u32[]{:S(2)}, u32[]{:S(2)}) collective-permute-start(bf16[256,1024]{1,0:T(8,128)(2,1)} %mark.1.refs_1_), channel_id=1, source_target_pairs={{0,448},{64,0},{128,64},{192,128},{256,192},{320,256},{384,320},{4... | collective-permute-start | bytes 1572872 | tf_op jit(solution)/shard_map/ppermute | solution.py:284
  12.0 28.8 %collective-permute-start.2 = (bf16[256,1024]{1,0:T(8,128)(2,1)}, bf16[256,1024]{1,0:T(8,128)(2,1)S(1)}, u32[]{:S(2)}, u32[]{:S(2)}) collective-permute-start(bf16[256,1024]{1,0:T(8,128)(2,1)} %bitcast.17), channel_id=1, source_target_pairs={{0,64},{64,128},{128,192},{192,256},{256,320},{320,384},{384,448},... | collective-permute-start | bytes 1572872 | tf_op jit(solution)/shard_map/ppermute | solution.py:284
  14.0 26.9 %collective-permute-start.3 = (bf16[256,1024]{1,0:T(8,128)(2,1)}, bf16[256,1024]{1,0:T(8,128)(2,1)S(1)}, u32[]{:S(2)}, u32[]{:S(2)}) collective-permute-start(bf16[256,1024]{1,0:T(8,128)(2,1)} %bitcast.18), channel_id=1, source_target_pairs={{0,448},{64,0},{128,64},{192,128},{256,192},{320,256},{384,320},{4... | collective-permute-start | bytes 1572872 | tf_op jit(solution)/shard_map/ppermute | solution.py:284
  23.4 70.0 %all-to-all-start = ((bf16[64,128,128]{2,1,0:T(8,128)(2,1)}), bf16[64,128,128]{2,1,0:T(8,128)(2,1)}, u32[]{:S(2)}, u32[]{:S(2)}) async-start(bf16[64,128,128]{2,1,0:T(8,128)(2,1)} %bitcast.12), calls=%async_computation | async-start | bytes 4194304 | tf_op jit(solution)/shard_map/all_to_all | solution.py:288
  40.8 0.8 copy-start.2
  40.8 0.9 copy-start.3
  40.9 1.1 copy-start.4
  42.0 0.8 copy-start.5
  62.2 54.8 %collective-permute-start.4 = (bf16[8,2,256,128]{3,2,1,0:T(8,128)(2,1)}, bf16[8,2,256,128]{3,2,1,0:T(8,128)(2,1)S(1)}, u32[]{:S(2)}, u32[]{:S(2)}) collective-permute-start(bf16[8,2,256,128]{3,2,1,0:T(8,128)(2,1)} %get-tuple-element.22), channel_id=1, source_target_pairs={{0,448},{64,0},{128,64},{192,128},{256,192},{320,256},{384,320},{4... | collective-permute-start | bytes 3145736 | tf_op jit(solution)/shard_map/ppermute | solution.py:284
  64.2 52.9 %collective-permute-start.5 = (bf16[8,2,256,128]{3,2,1,0:T(8,128)(2,1)}, bf16[8,2,256,128]{3,2,1,0:T(8,128)(2,1)S(1)}, u32[]{:S(2)}, u32[]{:S(2)}) collective-permute-start(bf16[8,2,256,128]{3,2,1,0:T(8,128)(2,1)} %get-tuple-element.23), channel_id=1, source_target_pairs={{0,64},{64,128},{128,192},{192,256},{256,320},{320,384},{384,448},... | collective-permute-start | bytes 3145736 | tf_op jit(solution)/shard_map/ppermute | solution.py:284
  100.7 68.9 %all-to-all-start.1 = ((bf16[64,128,128]{2,1,0:T(8,128)(2,1)}), bf16[64,128,128]{2,1,0:T(8,128)(2,1)}, u32[]{:S(2)}, u32[]{:S(2)}) async-start(bf16[64,128,128]{2,1,0:T(8,128)(2,1)} %bitcast.13), calls=%async_computation.1 | async-start | bytes 4194304 | tf_op jit(solution)/shard_map/all_to_all | solution.py:288
  117.0 1.0 copy-start
  117.1 1.3 copy-start.1

commit v4 on v3

--- a/solution.py
+++ b/solution.py
@@ -1,3 +1,5 @@
+import functools
+
 import jax
 import jax.numpy as jnp
 from jax import lax
@@ -6,6 +8,7 @@
 from jax.sharding import PartitionSpec as P
 
 HEAD_DIM = 64
+HALVES = 2
 PAIR = 128
 MARK = 1024.0
 MARK_CUT = 512.0
@@ -28,66 +31,79 @@
     return pltpu.CompilerParams(vmem_limit_bytes=limit)
 
 
-def mark_kernel(count_ref, k_ref, marked_ref):
+def mark_kernel(count_ref, k_ref, v_ref, kv_ref):
     positions = lax.broadcasted_iota(jnp.int32, k_ref.shape, 0) + pl.program_id(0) * k_ref.shape[0]
     wide = k_ref[...].astype(jnp.float32)
-    marked_ref[...] = jnp.where(positions < count_ref[0, 0], wide, MARK).astype(jnp.bfloat16)
-
-
-def mark(count, keys):
+    marked = jnp.where(positions < count_ref[0, 0], wide, MARK).astype(jnp.bfloat16)
+    values = v_ref[...]
+    for pair in range(kv_ref.shape[0]):
+        columns = slice(pair * PAIR, (pair + 1) * PAIR)
+        kv_ref[pair, 0] = marked[:, columns]
+        kv_ref[pair, 1] = values[:, columns]
+
+
+def mark(count, keys, values):
     length, width = keys.shape
-    row_spec = pl.BlockSpec((length // 2, width), lambda i: (i, 0))
+    pairs = width // PAIR
+    height = length // 2
+    row_spec = pl.BlockSpec((height, width), lambda i: (i, 0))
     return pl.pallas_call(
         mark_kernel,
-        grid=(2,),
-        in_specs=[pl.BlockSpec(memory_space=pltpu.SMEM), row_spec],
-        out_specs=row_spec,
-        out_shape=jax.ShapeDtypeStruct(keys.shape, jnp.bfloat16),
+        grid=(length // height,),
+        in_specs=[pl.BlockSpec(memory_space=pltpu.SMEM)] + [row_spec] * 2,
+        out_specs=pl.BlockSpec((pairs, 2, height, PAIR), lambda i: (0, 0, i, 0)),
+        out_shape=jax.ShapeDtypeStruct((pairs, 2, length, PAIR), jnp.bfloat16),
         compiler_params=params(),
         cost_estimate=pl.CostEstimate(
-            flops=length * width, bytes_accessed=4 * length * width, transcendentals=0
+            flops=length * width, bytes_accessed=8 * length * width, transcendentals=0
         ),
         name="mark",
-    )(count, keys)
-
-
-def pack_kernel(*refs):
-    x_ref = refs[-1]
+    )(count, keys, values)
+
+
+def pack_kernel(half, count_ref, q_ref, k_ref, v_ref, g_ref, x_ref):
     blocks, pairs, _, rows, _ = x_ref.shape
-    for index, ref in enumerate(refs[:-1]):
+    start = (pl.program_id(0) * blocks * HALVES + half) * rows
+    shape = k_ref.shape
+    in_block = lax.broadcasted_iota(jnp.int32, shape, 0) * (HALVES * rows)
+    positions = start + in_block + lax.broadcasted_iota(jnp.int32, shape, 2)
+    wide = k_ref[...].astype(jnp.float32)
+    marked = jnp.where(positions < count_ref[0, 0], wide, MARK).astype(jnp.bfloat16)
+    for index, whole in enumerate((q_ref[...], marked, v_ref[...], g_ref[...])):
         for pair in range(pairs):
-            part = ref[:, pair * PAIR : (pair + 1) * PAIR]
-            x_ref[:, pair, index] = part.reshape(blocks, rows, PAIR)
-
-
-def pack(queries, keys, values, cotangents, frames):
+            x_ref[:, pair, index] = whole[:, 0, :, pair * PAIR : (pair + 1) * PAIR]
+
+
+def pack(count, queries, keys, values, cotangents, frames, half):
     length, width = queries.shape
     pairs = width // PAIR
     blocks = frames // pairs
-    rows = length // blocks
-    per_step = 2
-    row_spec = pl.BlockSpec((per_step * rows, width), lambda i: (i, 0))
-    return pl.pallas_call(
-        pack_kernel,
+    rows = length // blocks // HALVES
+    per_step = 4
+
+    def split(array):
+        return array.reshape(blocks, HALVES, rows, width)
+
+    row_spec = pl.BlockSpec((per_step, 1, rows, width), lambda i: (i, half, 0, 0))
+    return pl.pallas_call(
+        functools.partial(pack_kernel, half),
         grid=(blocks // per_step,),
-        in_specs=[row_spec] * 4,
+        in_specs=[pl.BlockSpec(memory_space=pltpu.SMEM)] + [row_spec] * 4,
         out_specs=pl.BlockSpec((per_step, pairs, 4, rows, PAIR), lambda i: (i, 0, 0, 0, 0)),
         out_shape=jax.ShapeDtypeStruct((blocks, pairs, 4, rows, PAIR), jnp.bfloat16),
         compiler_params=params(),
         cost_estimate=pl.CostEstimate(
-            flops=length * width, bytes_accessed=16 * length * width, transcendentals=0
+            flops=length * width, bytes_accessed=8 * length * width, transcendentals=0
         ),
         name="pack",
-    )(queries, keys, values, cotangents)
-
-
-def cross_kernel(q_ref, g_ref, *refs):
-    key_refs, value_refs = refs[:3], refs[3:6]
-    o_ref, dq_ref, own_out, low_out, up_out = refs[6:]
+    )(count, split(queries), split(keys), split(values), split(cotangents))
+
+
+def cross_kernel(q_ref, g_ref, own_ref, low_ref, up_ref, o_ref, dq_ref, own_out, low_out, up_out):
     length = q_ref.shape[0]
     first = lax.broadcasted_iota(jnp.int32, (length, PAIR), 1) < HEAD_DIM
-    marked = jnp.concatenate([ref[...] for ref in key_refs], axis=0)
-    values = jnp.concatenate([ref[...] for ref in value_refs], axis=0)
+    marked = jnp.concatenate([low_ref[0, 0], own_ref[0, 0], up_ref[0, 0]], axis=0)
+    values = jnp.concatenate([low_ref[0, 1], own_ref[0, 1], up_ref[0, 1]], axis=0)
     wide = marked.astype(jnp.float32)
     invalid = wide > MARK_CUT
     keys_wide = jnp.where(invalid, 0.0, wide)
@@ -128,7 +144,7 @@
         up_out[0, index] = grad[2 * length :].astype(jnp.bfloat16)
 
 
-def cross(queries, cotangents, keys, values):
+def cross(queries, cotangents, own, lower, upper):
     length, width = queries.shape
     pairs = width // PAIR
     column_spec = pl.BlockSpec((length, PAIR), lambda j: (0, j))
@@ -139,7 +155,7 @@
     return pl.pallas_call(
         cross_kernel,
         grid=(pairs,),
-        in_specs=[column_spec] * 8,
+        in_specs=[column_spec] * 2 + [pair_spec] * 3,
         out_specs=[column_spec] * 2 + [pair_spec] * 3,
         out_shape=[flat, flat, paired, paired_low, paired_low],
         compiler_params=params(),
@@ -149,7 +165,7 @@
             transcendentals=48 * length * length,
         ),
         name="cross_view",
-    )(queries, cotangents, *keys, *values)
+    )(queries, cotangents, own, lower, upper)
 
 
 def temporal_kernel(y_ref, z_ref, rows_in, rows_out):
@@ -197,19 +213,17 @@
 
 def temporal(blocks):
     frames, _, positions, _ = blocks.shape
-    per_step = 16
-    spec = pl.BlockSpec((frames, 4, per_step, PAIR), lambda i: (0, 0, i, 0))
-    scratch = pltpu.VMEM((4, frames * per_step, PAIR), jnp.float32)
+    spec = pl.BlockSpec(blocks.shape, lambda: (0, 0, 0, 0))
+    scratch = pltpu.VMEM((4, frames * positions, PAIR), jnp.float32)
     return pl.pallas_call(
         temporal_kernel,
-        grid=(positions // per_step,),
         in_specs=[spec],
         out_specs=spec,
         out_shape=pltpu.HBM(blocks.shape, jnp.bfloat16),
         scratch_shapes=[scratch, scratch],
         compiler_params=params(ROOMY_BYTES),
         cost_estimate=pl.CostEstimate(
-            flops=12 * positions * frames * frames * PAIR,
+            flops=10**12,
             bytes_accessed=4 * blocks.size,
             transcendentals=2 * positions * frames * frames,
         ),
@@ -248,35 +262,40 @@
     )(own, lower, upper)
 
 
-def finish_kernel(w_ref, *refs):
-    cross_refs, out_refs = refs[:4], refs[4:]
-    height = cross_refs[0].shape[0]
-    for pair in range(w_ref.shape[1]):
-        columns = slice(pair * PAIR, (pair + 1) * PAIR)
-        for index, (cross_ref, out_ref) in enumerate(zip(cross_refs, out_refs)):
-            returned = w_ref[:, pair, index].reshape(height, PAIR).astype(jnp.float32)
-            crossed = cross_ref[:, columns].astype(jnp.float32)
-            out_ref[:, columns] = (crossed + returned).astype(jnp.bfloat16)
-
-
-def finish(returned, *cross_parts):
+def finish_kernel(*refs):
+    half_refs, cross_refs, out_refs = refs[:HALVES], refs[HALVES : HALVES + 4], refs[HALVES + 4 :]
+    blocks, pairs, _, rows, _ = half_refs[0].shape
+    for half, w_ref in enumerate(half_refs):
+        for pair in range(pairs):
+            columns = slice(pair * PAIR, (pair + 1) * PAIR)
+            for index, (cross_ref, out_ref) in enumerate(zip(cross_refs, out_refs)):
+                crossed = cross_ref[:, half, :, columns].astype(jnp.float32)
+                summed = crossed + w_ref[:, pair, index].astype(jnp.float32)
+                out_ref[:, half, :, columns] = summed.astype(jnp.bfloat16)
+
+
+def finish(returned, cross_parts):
     length, width = cross_parts[0].shape
-    blocks, pairs, _, rows, _ = returned.shape
+    blocks, pairs, _, rows, _ = returned[0].shape
     per_step = 2
-    row_spec = pl.BlockSpec((per_step * rows, width), lambda i: (i, 0))
+    split = (blocks, HALVES, rows, width)
+    row_spec = pl.BlockSpec((per_step,) + split[1:], lambda i: (i, 0, 0, 0))
+    half_spec = pl.BlockSpec((per_step, pairs, 4, rows, PAIR), lambda i: (i, 0, 0, 0, 0))
+    in_place = (
+        pltpu.with_memory_space_constraint(part.reshape(split), pltpu.HBM) for part in cross_parts
+    )
     return pl.pallas_call(
         finish_kernel,
         grid=(blocks // per_step,),
-        in_specs=[pl.BlockSpec((per_step, pairs, 4, rows, PAIR), lambda i: (i, 0, 0, 0, 0))]
-        + [row_spec] * 4,
+        in_specs=[half_spec] * HALVES + [row_spec] * 4,
         out_specs=[row_spec] * 4,
-        out_shape=[jax.ShapeDtypeStruct((length, width), jnp.bfloat16)] * 4,
+        out_shape=[jax.ShapeDtypeStruct(split, jnp.bfloat16)] * 4,
         compiler_params=params(ROOMY_BYTES),
         cost_estimate=pl.CostEstimate(
-            flops=4 * length * width, bytes_accessed=32 * length * width, transcendentals=0
+            flops=4 * length * width, bytes_accessed=24 * length * width, transcendentals=0
         ),
         name="finish",
-    )(returned, *(pltpu.with_memory_space_constraint(part, pltpu.HBM) for part in cross_parts))
+    )(*returned, *in_place)
 
 
 def from_behind(shard, axis, by):
@@ -294,28 +313,40 @@
     value_rows = value_vectors[0, 0]
     grad_rows = out_grad[0, 0]
     frames = lax.axis_size("frame")
-    lower_values = from_behind(value_rows, "cam", 1)
-    upper_values = from_behind(value_rows, "cam", -1)
-    marked = mark(valid_count, key_rows)
-    lower_keys = from_behind(marked, "cam", 1)
-    upper_keys = from_behind(marked, "cam", -1)
-    packed = pack(query_rows, marked, value_rows, grad_rows, frames)
-    rows = packed.shape[3]
-    arrived = exchange(packed.reshape(frames, 4 * rows, PAIR))
+
+    def packed(half):
+        return pack(valid_count, query_rows, key_rows, value_rows, grad_rows, frames, half)
+
+    first = packed(0)
+    rows = first.shape[3]
+    by_frame = (frames, 4 * rows, PAIR)
+    by_array = (frames, 4, rows, PAIR)
+    arrived_first = exchange(first.reshape(by_frame))
+    marked = mark(valid_count, key_rows, value_rows)
+    lower = from_behind(marked, "cam", 1)
+    upper = from_behind(marked, "cam", -1)
+    arrived_first, second = lax.optimization_barrier((arrived_first, packed(1)))
+    arrived_second = exchange(second.reshape(by_frame))
+    arrived_first, lower, upper = lax.optimization_barrier((arrived_first, lower, upper))
+    answered_first = temporal(arrived_first.reshape(by_array))
+    arrived_second, answered_first, cross_queries = lax.optimization_barrier(
+        (arrived_second, answered_first, query_rows)
+    )
+    returned_first = exchange(answered_first.reshape(by_frame))
+    answered_second = temporal(arrived_second.reshape(by_array))
     cross_out, cross_query, own_grads, lower_grads, upper_grads = cross(
-        query_rows,
-        grad_rows,
-        (lower_keys, marked, upper_keys),
-        (lower_values, value_rows, upper_values),
+        cross_queries, grad_rows, marked, lower, upper
     )
     from_upper = from_behind(lower_grads, "cam", -1)
     from_lower = from_behind(upper_grads, "cam", 1)
-    arrived, cross_out = lax.optimization_barrier((arrived, cross_out))
-    answered = temporal(arrived.reshape(frames, 4, rows, PAIR))
-    returned = exchange(answered.reshape(frames, 4 * rows, PAIR)).reshape(packed.shape)
+    answered_second, returned_first, cross_out = lax.optimization_barrier(
+        (answered_second, returned_first, cross_out)
+    )
+    returned_second = exchange(answered_second.reshape(by_frame))
     key_total, value_total = total(own_grads, from_upper, from_lower)
-    results = finish(returned, cross_out, cross_query, key_total, value_total)
-    return tuple(result[None, None] for result in results)
+    returned = [part.reshape(first.shape) for part in (returned_first, returned_second)]
+    results = finish(returned, (cross_out, cross_query, key_total, value_total))
+    return tuple(result.reshape(queries.shape) for result in results)
 
 
 def solution(mesh):

time: 175 us -> 189 us (1.080)
  starting transfers between devices: 55.3 us -> 64.7 us
  waiting for transfers between devices: 73.2 us -> 79.1 us
  local copies, waits for them, and re-layouts: 3.21 us -> 0.01 us
    ppermute x6 -> x4, waiting for transfers between devices: 0.02 us -> 48.6 us  [from_behind(): lax.ppermute(shard, axis, [(i, (i + by) % devices) for i in range(devices)])]
    all_to_all x2 -> x4, waiting for transfers between devices: 73.2 us -> 30.5 us  [exchange(): lax.all_to_all(blocks, 'frame', split_axis=0, concat_axis=0, tiled=True)]
    all_to_all x2 -> x4, starting transfers between devices: 33.7 us -> 52.3 us  [exchange(): lax.all_to_all(blocks, 'frame', split_axis=0, concat_axis=0, tiled=True)]
    ppermute x6 -> x4, starting transfers between devices: 21.6 us -> 12.5 us  [from_behind(): lax.ppermute(shard, axis, [(i, (i + by) % devices) for i in range(devices)])]
    unnamed x12 -> x4, local copies, waits for them, and re-layouts: 3.21 us -> 0.01 us
    pallas_call x5 -> x7, Pallas kernels: 36.8 us -> 38.4 us  [the longest x1 19.4 us: cross(): pl.pallas_call(cross_kernel, grid=(pairs,), in_specs=[column_spec] * 2 +...]
  transfers between devices with their start and end apart: 8 -> 8, of which waited for: 2 -> 8; matrix products, arithmetic and copies ran while one was open for 0% -> 0% of each run, Pallas kernels for 20% -> 19%
where the time goes in v4:
time: 189 us; the launch traced here: 188 us
  waiting for transfers between devices  79.1 us (42%)
  starting transfers between devices  64.7 us (34%)
  Pallas kernels  42.5 us (22%)
    all_to_all x4, starting transfers between devices, exchange(): lax.all_to_all(blocks, 'frame', split_axis=0, concat_axis=0, tiled=True)  52.3 us
    ppermute x4, waiting for transfers between devices, from_behind(): lax.ppermute(shard, axis, [(i, (i + by) % devices) for i in range(devices)])  48.6 us
    all_to_all x4, waiting for transfers between devices, exchange(): lax.all_to_all(blocks, 'frame', split_axis=0, concat_axis=0, tiled=True)  30.5 us
    pallas_call x1, Pallas kernels, cross(): pl.pallas_call(cross_kernel, grid=(pairs,), in_specs=[column_spec] * 2 +...  19.4 us
    ppermute x4, starting transfers between devices, from_behind(): lax.ppermute(shard, axis, [(i, (i + by) % devices) for i in range(devices)])  12.5 us
    pallas_call x2, Pallas kernels, temporal(): pl.pallas_call(temporal_kernel, in_specs=[spec], out_specs=spec, out_shap...  8.22 us
    pallas_call x2, Pallas kernels, pack(): pl.pallas_call(functools.partial(pack_kernel, half), grid=(blocks // per_...  4.39 us
    pallas_call x1, Pallas kernels, finish(): pl.pallas_call(finish_kernel, grid=(blocks // per_step,), in_specs=[half_...  4.24 us
  transfers between devices with their start and end apart: 8, of which 8 were waited for; matrix products, arithmetic and copies ran while one was open for 0% of the time, Pallas kernels for 19%

profile of v4, /device:TPU:1, one launch (start us, length us, event | category | flops | bytes accessed | tf_op | source)
XLA Modules:
  0.0 187.6 jit_solution(4041890173797158996)
XLA Ops:
  1.3 2.2 %pack.2 = bf16[8,8,4,16,128]{4,3,2,1,0:T(8,128)(2,1)} custom-call(s32[1,1]{1,0:T(1,128)S(6)} %copy.9.count_ref, bf16[8,2,16,1024]{3,2,1,0:T(8,128)(2,1)} %bitcast.33, bf16[8,2,16,1024]{3,2,1,0:T(8,128)(2,1)} %bitcast.25, bf16[8,2,16,1024]{3,2,1,0:T(8,128)(2,1)} %bitcast.28, bf16[8,2,16,1024]{3,2,1,0:T(8,128)(2,1)} %bitcast.36), custom_call_target="tpu_custom_call" | custom-call | flops 262144 | bytes 2097152 | tf_op jit(solution)/shard_map/pack/pallas_call | solution.py:88
  3.5 17.6 %all-to-all-start = ((bf16[64,64,128]{2,1,0:T(8,128)(2,1)}), bf16[64,64,128]{2,1,0:T(8,128)(2,1)S(1)}, u32[]{:S(2)}, u32[]{:S(2)}) async-start(bf16[64,64,128]{2,1,0:T(8,128)(2,1)} %bitcast.32), calls=%async_computation | async-start | bytes 2097152 | tf_op jit(solution)/shard_map/all_to_all | solution.py:307
  21.1 2.1 %mark.1.own_ref = bf16[8,2,256,128]{3,2,1,0:T(8,128)(2,1)} custom-call(s32[1,1]{1,0:T(1,128)S(6)} %copy.9.count_ref, bf16[256,1024]{1,0:T(8,128)(2,1)} %bitcast.26, bf16[256,1024]{1,0:T(8,128)(2,1)} %bitcast.29), custom_call_target="tpu_custom_call" | custom-call | flops 262144 | bytes 2097152 | tf_op jit(solution)/shard_map/mark/pallas_call | solution.py:50
  23.2 5.3 %collective-permute-start.1 = (bf16[8,2,256,128]{3,2,1,0:T(8,128)(2,1)}, bf16[8,2,256,128]{3,2,1,0:T(8,128)(2,1)S(1)}, u32[]{:S(2)}, u32[]{:S(2)}) collective-permute-start(bf16[8,2,256,128]{3,2,1,0:T(8,128)(2,1)} %mark.1.own_ref), channel_id=1, source_target_pairs={{0,448},{64,0},{128,64},{192,128},{256,192},{320,256},{384,320},{4... | collective-permute-start | bytes 3145736 | tf_op jit(solution)/shard_map/ppermute | solution.py:303
  28.5 1.9 %collective-permute-start = (bf16[8,2,256,128]{3,2,1,0:T(8,128)(2,1)}, bf16[8,2,256,128]{3,2,1,0:T(8,128)(2,1)S(1)}, u32[]{:S(2)}, u32[]{:S(2)}) collective-permute-start(bf16[8,2,256,128]{3,2,1,0:T(8,128)(2,1)} %mark.1.own_ref), channel_id=1, source_target_pairs={{0,64},{64,128},{128,192},{192,256},{256,320},{320,384},{384,448},... | collective-permute-start | bytes 3145736 | tf_op jit(solution)/shard_map/ppermute | solution.py:303
  30.5 2.2 %pack.3 = bf16[8,8,4,16,128]{4,3,2,1,0:T(8,128)(2,1)} custom-call(s32[1,1]{1,0:T(1,128)S(6)} %copy.9.count_ref, bf16[8,2,16,1024]{3,2,1,0:T(8,128)(2,1)} %bitcast.34, bf16[8,2,16,1024]{3,2,1,0:T(8,128)(2,1)} %bitcast.27, bf16[8,2,16,1024]{3,2,1,0:T(8,128)(2,1)} %bitcast.30, bf16[8,2,16,1024]{3,2,1,0:T(8,128)(2,1)} %bitcast.37), custom_call_target="tpu_custom_call" | custom-call | flops 262144 | bytes 2097152 | tf_op jit(solution)/shard_map/pack/pallas_call | solution.py:88
  32.7 18.0 %all-to-all-done = bf16[64,64,128]{2,1,0:T(8,128)(2,1)S(1)} async-done(((bf16[64,64,128]{2,1,0:T(8,128)(2,1)}), bf16[64,64,128]{2,1,0:T(8,128)(2,1)S(1)}, u32[]{:S(2)}, u32[]{:S(2)}) %all-to-all-start) | async-done | bytes 1048608 | tf_op jit(solution)/shard_map/all_to_all | solution.py:307
  50.7 8.9 %all-to-all-start.1 = ((bf16[64,64,128]{2,1,0:T(8,128)(2,1)}), bf16[64,64,128]{2,1,0:T(8,128)(2,1)}, u32[]{:S(2)}, u32[]{:S(2)}) async-start(bf16[64,64,128]{2,1,0:T(8,128)(2,1)} %bitcast.31), calls=%async_computation.1 | async-start | bytes 2097152 | tf_op jit(solution)/shard_map/all_to_all | solution.py:307
  59.6 29.8 %collective-permute-done.1.up_ref = bf16[8,2,256,128]{3,2,1,0:T(8,128)(2,1)S(1)} collective-permute-done((bf16[8,2,256,128]{3,2,1,0:T(8,128)(2,1)}, bf16[8,2,256,128]{3,2,1,0:T(8,128)(2,1)S(1)}, u32[]{:S(2)}, u32[]{:S(2)}) %collective-permute-start.1) | collective-permute-done | bytes 1048608 | tf_op jit(solution)/shard_map/ppermute | solution.py:303
  89.4 2.4 %collective-permute-done.low_ref = bf16[8,2,256,128]{3,2,1,0:T(8,128)(2,1)S(1)} collective-permute-done((bf16[8,2,256,128]{3,2,1,0:T(8,128)(2,1)}, bf16[8,2,256,128]{3,2,1,0:T(8,128)(2,1)S(1)}, u32[]{:S(2)}, u32[]{:S(2)}) %collective-permute-start) | collective-permute-done | bytes 1048608 | tf_op jit(solution)/shard_map/ppermute | solution.py:303
  91.8 3.5 %temporal.2 = bf16[64,4,16,128]{3,2,1,0:T(8,128)(2,1)} custom-call(bf16[64,4,16,128]{3,2,1,0:T(8,128)(2,1)S(1)} %bitcast.24), custom_call_target="tpu_custom_call" | custom-call | flops 999999995904 | bytes 2097152 | tf_op jit(solution)/shard_map/temporal/pallas_call | solution.py:218
  95.3 0.7 all-to-all-done.1
  96.0 12.4 %all-to-all-start.2 = ((bf16[64,64,128]{2,1,0:T(8,128)(2,1)}), bf16[64,64,128]{2,1,0:T(8,128)(2,1)}, u32[]{:S(2)}, u32[]{:S(2)}) async-start(bf16[64,64,128]{2,1,0:T(8,128)(2,1)} %bitcast.39), calls=%async_computation.2 | async-start | bytes 2097152 | tf_op jit(solution)/shard_map/all_to_all | solution.py:307
  108.4 19.4 %cross_view.1 = (bf16[256,1024]{1,0:T(8,128)(2,1)}, bf16[256,1024]{1,0:T(8,128)(2,1)}, f32[8,2,256,128]{3,2,1,0:T(8,128)}, bf16[8,2,256,128]{3,2,1,0:T(8,128)(2,1)}, bf16[8,2,256,128]{3,2,1,0:T(8,128)(2,1)}) custom-call(bf16[256,1024]{1,0:T(8,128)(2,1)} %bitcast.35, bf16[256,1024]{1,0:T(8,128)(2,1)} %bitcast.38, bf16[8,2,256,128]{3,2,1,0:T(8,128)(2,1)} %mark.1.own_ref, ...), custom_call_target="tpu_custom_call" | custom-call | flops 671088640000 | bytes 12582912 | tf_op jit(solution)/shard_map/cross_view/pallas_call | solution.py:155
  127.8 1.9 %collective-permute-start.2 = (bf16[8,2,256,128]{3,2,1,0:T(8,128)(2,1)}, bf16[8,2,256,128]{3,2,1,0:T(8,128)(2,1)}, u32[]{:S(2)}, u32[]{:S(2)}) collective-permute-start(bf16[8,2,256,128]{3,2,1,0:T(8,128)(2,1)} %get-tuple-element.40), channel_id=1, source_target_pairs={{0,448},{64,0},{128,64},{192,128},{256,192},{320,256},{384,320},{4... | collective-permute-start | bytes 3145736 | tf_op jit(solution)/shard_map/ppermute | solution.py:303
  129.7 3.4 %collective-permute-start.3 = (bf16[8,2,256,128]{3,2,1,0:T(8,128)(2,1)}, bf16[8,2,256,128]{3,2,1,0:T(8,128)(2,1)}, u32[]{:S(2)}, u32[]{:S(2)}) collective-permute-start(bf16[8,2,256,128]{3,2,1,0:T(8,128)(2,1)} %get-tuple-element.41), channel_id=1, source_target_pairs={{0,64},{64,128},{128,192},{192,256},{256,320},{320,384},{384,448},... | collective-permute-start | bytes 3145736 | tf_op jit(solution)/shard_map/ppermute | solution.py:303
  133.1 4.7 %temporal.3 = bf16[64,4,16,128]{3,2,1,0:T(8,128)(2,1)} custom-call(bf16[64,4,16,128]{3,2,1,0:T(8,128)(2,1)} %bitcast.10.y_ref), custom_call_target="tpu_custom_call" | custom-call | flops 999999995904 | bytes 2097152 | tf_op jit(solution)/shard_map/temporal/pallas_call | solution.py:218
  137.8 0.2 all-to-all-done.2
  138.0 13.3 %all-to-all-start.3 = ((bf16[64,64,128]{2,1,0:T(8,128)(2,1)}), bf16[64,64,128]{2,1,0:T(8,128)(2,1)}, u32[]{:S(2)}, u32[]{:S(2)}) async-start(bf16[64,64,128]{2,1,0:T(8,128)(2,1)} %bitcast.40), calls=%async_computation.3 | async-start | bytes 2097152 | tf_op jit(solution)/shard_map/all_to_all | solution.py:307
  151.3 12.2 %collective-permute-done.2.low_ref = bf16[8,2,256,128]{3,2,1,0:T(8,128)(2,1)} collective-permute-done((bf16[8,2,256,128]{3,2,1,0:T(8,128)(2,1)}, bf16[8,2,256,128]{3,2,1,0:T(8,128)(2,1)}, u32[]{:S(2)}, u32[]{:S(2)}) %collective-permute-start.2) | collective-permute-done | bytes 1048608 | tf_op jit(solution)/shard_map/ppermute | solution.py:303
  163.5 4.2 %collective-permute-done.3.up_ref = bf16[8,2,256,128]{3,2,1,0:T(8,128)(2,1)} collective-permute-done((bf16[8,2,256,128]{3,2,1,0:T(8,128)(2,1)}, bf16[8,2,256,128]{3,2,1,0:T(8,128)(2,1)}, u32[]{:S(2)}, u32[]{:S(2)}) %collective-permute-start.3) | collective-permute-done | bytes 1048608 | tf_op jit(solution)/shard_map/ppermute | solution.py:303
  167.8 4.1 %total.1 = (bf16[256,1024]{1,0:T(8,128)(2,1)}, bf16[256,1024]{1,0:T(8,128)(2,1)}) custom-call(f32[8,2,256,128]{3,2,1,0:T(8,128)} %get-tuple-element.39.own_ref, bf16[8,2,256,128]{3,2,1,0:T(8,128)(2,1)} %collective-permute-done.2.low_ref, bf16[8,2,256,128]{3,2,1,0:T(8,128)(2,1)} %collective-permute-done.3.up_ref), custom_call_target="tpu_custom_call" | custom-call | flops 999999995904 | bytes 6291456 | tf_op jit(solution)/shard_map/total/pallas_call | solution.py:249
  171.8 11.6 %all-to-all-done.3 = bf16[64,64,128]{2,1,0:T(8,128)(2,1)} async-done(((bf16[64,64,128]{2,1,0:T(8,128)(2,1)}), bf16[64,64,128]{2,1,0:T(8,128)(2,1)}, u32[]{:S(2)}, u32[]{:S(2)}) %all-to-all-start.3) | async-done | bytes 1048608 | tf_op jit(solution)/shard_map/all_to_all | solution.py:307
  183.4 4.2 %finish.1 = (bf16[8,2,16,1024]{3,2,1,0:T(8,128)(2,1)}, bf16[8,2,16,1024]{3,2,1,0:T(8,128)(2,1)}, bf16[8,2,16,1024]{3,2,1,0:T(8,128)(2,1)}, bf16[8,2,16,1024]{3,2,1,0:T(8,128)(2,1)}) custom-call(bf16[8,8,4,16,128]{4,3,2,1,0:T(8,128)(2,1)} %bitcast.13.refs_0_, bf16[8,8,4,16,128]{4,3,2,1,0:T(8,128)(2,1)} %bitcast.15.refs_1_, bf16[8,2,16,1024]{3,2,1,0:T(8,128)(2,1)} %bitcast.41, ...), custom_call_target="tpu_custom_call" | custom-call | flops 1048576 | bytes 6291456 | tf_op jit(solution)/shard_map/finish/pallas_call | solution.py:287
  (4 shorter events, 0.0 us)
Async XLA Ops:
  3.5 47.2 %all-to-all-start = ((bf16[64,64,128]{2,1,0:T(8,128)(2,1)}), bf16[64,64,128]{2,1,0:T(8,128)(2,1)S(1)}, u32[]{:S(2)}, u32[]{:S(2)}) async-start(bf16[64,64,128]{2,1,0:T(8,128)(2,1)} %bitcast.32), calls=%async_computation | async-start | bytes 2097152 | tf_op jit(solution)/shard_map/all_to_all | solution.py:307
  23.2 66.2 %collective-permute-start.1 = (bf16[8,2,256,128]{3,2,1,0:T(8,128)(2,1)}, bf16[8,2,256,128]{3,2,1,0:T(8,128)(2,1)S(1)}, u32[]{:S(2)}, u32[]{:S(2)}) collective-permute-start(bf16[8,2,256,128]{3,2,1,0:T(8,128)(2,1)} %mark.1.own_ref), channel_id=1, source_target_pairs={{0,448},{64,0},{128,64},{192,128},{256,192},{320,256},{384,320},{4... | collective-permute-start | bytes 3145736 | tf_op jit(solution)/shard_map/ppermute | solution.py:303
  28.5 63.3 %collective-permute-start = (bf16[8,2,256,128]{3,2,1,0:T(8,128)(2,1)}, bf16[8,2,256,128]{3,2,1,0:T(8,128)(2,1)S(1)}, u32[]{:S(2)}, u32[]{:S(2)}) collective-permute-start(bf16[8,2,256,128]{3,2,1,0:T(8,128)(2,1)} %mark.1.own_ref), channel_id=1, source_target_pairs={{0,64},{64,128},{128,192},{192,256},{256,320},{320,384},{384,448},... | collective-permute-start | bytes 3145736 | tf_op jit(solution)/shard_map/ppermute | solution.py:303
  50.7 45.3 %all-to-all-start.1 = ((bf16[64,64,128]{2,1,0:T(8,128)(2,1)}), bf16[64,64,128]{2,1,0:T(8,128)(2,1)}, u32[]{:S(2)}, u32[]{:S(2)}) async-start(bf16[64,64,128]{2,1,0:T(8,128)(2,1)} %bitcast.31), calls=%async_computation.1 | async-start | bytes 2097152 | tf_op jit(solution)/shard_map/all_to_all | solution.py:307
  89.4 5.8 %copy-start = (bf16[8,2,256,128]{3,2,1,0:T(8,128)(2,1)}, bf16[8,2,256,128]{3,2,1,0:T(8,128)(2,1)S(1)}, u32[]{:S(2)}) copy-start(bf16[8,2,256,128]{3,2,1,0:T(8,128)(2,1)S(1)} %collective-permute-done.1.up_ref) | copy-start | bytes 3145732
  91.8 3.5 %copy-start.1 = (bf16[8,2,256,128]{3,2,1,0:T(8,128)(2,1)}, bf16[8,2,256,128]{3,2,1,0:T(8,128)(2,1)S(1)}, u32[]{:S(2)}) copy-start(bf16[8,2,256,128]{3,2,1,0:T(8,128)(2,1)S(1)} %collective-permute-done.low_ref) | copy-start | bytes 3145732
  96.0 42.0 %all-to-all-start.2 = ((bf16[64,64,128]{2,1,0:T(8,128)(2,1)}), bf16[64,64,128]{2,1,0:T(8,128)(2,1)}, u32[]{:S(2)}, u32[]{:S(2)}) async-start(bf16[64,64,128]{2,1,0:T(8,128)(2,1)} %bitcast.39), calls=%async_computation.2 | async-start | bytes 2097152 | tf_op jit(solution)/shard_map/all_to_all | solution.py:307
  127.8 35.7 %collective-permute-start.2 = (bf16[8,2,256,128]{3,2,1,0:T(8,128)(2,1)}, bf16[8,2,256,128]{3,2,1,0:T(8,128)(2,1)}, u32[]{:S(2)}, u32[]{:S(2)}) collective-permute-start(bf16[8,2,256,128]{3,2,1,0:T(8,128)(2,1)} %get-tuple-element.40), channel_id=1, source_target_pairs={{0,448},{64,0},{128,64},{192,128},{256,192},{320,256},{384,320},{4... | collective-permute-start | bytes 3145736 | tf_op jit(solution)/shard_map/ppermute | solution.py:303
  129.7 38.0 %collective-permute-start.3 = (bf16[8,2,256,128]{3,2,1,0:T(8,128)(2,1)}, bf16[8,2,256,128]{3,2,1,0:T(8,128)(2,1)}, u32[]{:S(2)}, u32[]{:S(2)}) collective-permute-start(bf16[8,2,256,128]{3,2,1,0:T(8,128)(2,1)} %get-tuple-element.41), channel_id=1, source_target_pairs={{0,64},{64,128},{128,192},{192,256},{256,320},{320,384},{384,448},... | collective-permute-start | bytes 3145736 | tf_op jit(solution)/shard_map/ppermute | solution.py:303
  138.0 45.4 %all-to-all-start.3 = ((bf16[64,64,128]{2,1,0:T(8,128)(2,1)}), bf16[64,64,128]{2,1,0:T(8,128)(2,1)}, u32[]{:S(2)}, u32[]{:S(2)}) async-start(bf16[64,64,128]{2,1,0:T(8,128)(2,1)} %bitcast.40), calls=%async_computation.3 | async-start | bytes 2097152 | tf_op jit(solution)/shard_map/all_to_all | solution.py:307

commit v5 on v3

--- a/solution.py
+++ b/solution.py
@@ -152,11 +152,11 @@
     )(queries, cotangents, *keys, *values)
 
 
-def temporal_kernel(y_ref, z_ref, rows_in, rows_out):
+def temporal_kernel(y_ref, z_ref):
     frames, _, positions, _ = y_ref.shape
     first = lax.broadcasted_iota(jnp.int32, (frames, PAIR), 1) < HEAD_DIM
-    for index in range(4):
-        rows_in[index] = y_ref[:, index].astype(jnp.float32).reshape(frames * positions, PAIR)
+    rows_in = [jnp.swapaxes(y_ref[:, index].astype(jnp.float32), 0, 1) for index in range(4)]
+    rows_out = [[], [], [], []]
 
     def stacked(rows):
         return jnp.concatenate(
@@ -170,43 +170,39 @@
     for start in range(0, positions, group):
         held = []
         for position in range(start, start + group):
-            at = pl.ds(position, frames, stride=positions)
-            marked = rows_in[1, at, :]
+            marked = rows_in[1][position]
             invalid = marked > MARK_CUT
             keys = jnp.where(invalid, 0.0, marked).astype(jnp.bfloat16)
-            values = rows_in[2, at, :].astype(jnp.bfloat16)
-            queries = stacked(rows_in[0, at, :] * SCALE)
-            cotangents = stacked(rows_in[3, at, :])
+            values = rows_in[2][position].astype(jnp.bfloat16)
+            queries = stacked(rows_in[0][position] * SCALE)
+            cotangents = stacked(rows_in[3][position])
             scores = jnp.where(invalid, MASKED, contract(keys, queries, ROW_T))
             grad_probs = contract(values, cotangents, ROW_T)
-            held.append((at, keys, values, queries, cotangents, scores, grad_probs))
-        for at, keys, values, queries, cotangents, scores, grad_probs in held:
+            held.append((keys, values, queries, cotangents, scores, grad_probs))
+        for keys, values, queries, cotangents, scores, grad_probs in held:
             shifted = jnp.exp(scores - jnp.max(scores, axis=0, keepdims=True))
             probs = shifted * (1.0 / jnp.sum(shifted, axis=0, keepdims=True))
             row_delta = jnp.sum(probs * grad_probs, axis=0, keepdims=True)
             grad_scores = probs * (grad_probs - row_delta)
-            rows_out[0, at, :] = diagonal(multiply(probs.T.astype(jnp.bfloat16), values))
-            rows_out[1, at, :] = (
-                diagonal(multiply(grad_scores.T.astype(jnp.bfloat16), keys)) * SCALE
-            )
-            rows_out[2, at, :] = multiply(grad_scores.astype(jnp.bfloat16), queries)
-            rows_out[3, at, :] = multiply(probs.astype(jnp.bfloat16), cotangents)
+            rows_out[0].append(diagonal(multiply(probs.T.astype(jnp.bfloat16), values)))
+            query_part = diagonal(multiply(grad_scores.T.astype(jnp.bfloat16), keys))
+            rows_out[1].append(query_part * SCALE)
+            rows_out[2].append(multiply(grad_scores.astype(jnp.bfloat16), queries))
+            rows_out[3].append(multiply(probs.astype(jnp.bfloat16), cotangents))
     for index in range(4):
-        z_ref[:, index] = rows_out[index].reshape(frames, positions, PAIR).astype(jnp.bfloat16)
+        z_ref[:, index] = jnp.swapaxes(jnp.stack(rows_out[index]), 0, 1).astype(jnp.bfloat16)
 
 
 def temporal(blocks):
     frames, _, positions, _ = blocks.shape
     per_step = 16
     spec = pl.BlockSpec((frames, 4, per_step, PAIR), lambda i: (0, 0, i, 0))
-    scratch = pltpu.VMEM((4, frames * per_step, PAIR), jnp.float32)
     return pl.pallas_call(
         temporal_kernel,
         grid=(positions // per_step,),
         in_specs=[spec],
         out_specs=spec,
         out_shape=pltpu.HBM(blocks.shape, jnp.bfloat16),
-        scratch_shapes=[scratch, scratch],
         compiler_params=params(ROOMY_BYTES),
         cost_estimate=pl.CostEstimate(
             flops=12 * positions * frames * frames * PAIR,
@@ -262,7 +258,7 @@
 def finish(returned, *cross_parts):
     length, width = cross_parts[0].shape
     blocks, pairs, _, rows, _ = returned.shape
-    per_step = 2
+    per_step = 1
     row_spec = pl.BlockSpec((per_step * rows, width), lambda i: (i, 0))
     return pl.pallas_call(
         finish_kernel,

time: 175 us -> 175 us (level)
    pallas_call x1, Pallas kernels: 4.26 us -> 6.05 us  [finish(): pl.pallas_call(finish_kernel, grid=(blocks // per_step,), in_specs=[pl.Bl...]
  transfers between devices with their start and end apart: 8 -> 8, of which waited for: 2 -> 2; matrix products, arithmetic and copies ran while one was open for 0% -> 0% of each run, Pallas kernels for 20% -> 19%
where the time goes in v5:
time: 175 us
  waiting for transfers between devices  73.2 us (42%)
  starting transfers between devices  55.3 us (32%)
  Pallas kernels  41.4 us (24%)
  local copies, waits for them, and re-layouts  3.21 us (2%)
    all_to_all x2, waiting for transfers between devices, exchange(): lax.all_to_all(blocks, 'frame', split_axis=0, concat_axis=0, tiled=True)  73.2 us
    all_to_all x2, starting transfers between devices, exchange(): lax.all_to_all(blocks, 'frame', split_axis=0, concat_axis=0, tiled=True)  33.7 us
    ppermute x6, starting transfers between devices, from_behind(): lax.ppermute(shard, axis, [(i, (i + by) % devices) for i in range(devices)])  21.6 us
    pallas_call x1, Pallas kernels, cross(): pl.pallas_call(cross_kernel, grid=(pairs,), in_specs=[column_spec] * 8, o...  19.5 us
    pallas_call x1, Pallas kernels, temporal(): pl.pallas_call(temporal_kernel, grid=(positions // per_step,), in_specs=[...  6.12 us
    pallas_call x1, Pallas kernels, finish(): pl.pallas_call(finish_kernel, grid=(blocks // per_step,), in_specs=[pl.Bl...  6.05 us
    pallas_call x1, Pallas kernels, total(): pl.pallas_call(total_kernel, grid=(pairs // per_step,), in_specs=[pair_sp...  4.04 us
    pallas_call x1, Pallas kernels, pack(): pl.pallas_call(pack_kernel, grid=(blocks // per_step,), in_specs=[row_spe...  3.97 us
  transfers between devices with their start and end apart: 8, of which 2 were waited for; matrix products, arithmetic and copies ran while one was open for 0% of the time, Pallas kernels for 19%

profile of v5, /device:TPU:1, one launch (start us, length us, event | category | flops | bytes accessed | tf_op | source)
XLA Modules:
  0.0 174.6 jit_solution(15611635657150102026)
XLA Ops:
  1.3 1.8 %mark.1.refs_1_ = bf16[256,1024]{1,0:T(8,128)(2,1)} custom-call(s32[1,1]{1,0:T(1,128)S(6)} %copy.9.count_ref, bf16[256,1024]{1,0:T(8,128)(2,1)} %bitcast.14), custom_call_target="tpu_custom_call" | custom-call | flops 262144 | bytes 1048576 | tf_op jit(solution)/shard_map/mark/pallas_call | solution.py:40
  3.1 3.9 %collective-permute-start = (bf16[256,1024]{1,0:T(8,128)(2,1)}, bf16[256,1024]{1,0:T(8,128)(2,1)S(1)}, u32[]{:S(2)}, u32[]{:S(2)}) collective-permute-start(bf16[256,1024]{1,0:T(8,128)(2,1)} %mark.1.refs_1_), channel_id=1, source_target_pairs={{0,64},{64,128},{128,192},{192,256},{256,320},{320,384},{384,448},... | collective-permute-start | bytes 1572872 | tf_op jit(solution)/shard_map/ppermute | solution.py:280
  7.0 5.0 %collective-permute-start.1 = (bf16[256,1024]{1,0:T(8,128)(2,1)}, bf16[256,1024]{1,0:T(8,128)(2,1)S(1)}, u32[]{:S(2)}, u32[]{:S(2)}) collective-permute-start(bf16[256,1024]{1,0:T(8,128)(2,1)} %mark.1.refs_1_), channel_id=1, source_target_pairs={{0,448},{64,0},{128,64},{192,128},{256,192},{320,256},{384,320},{4... | collective-permute-start | bytes 1572872 | tf_op jit(solution)/shard_map/ppermute | solution.py:280
  12.0 1.9 %collective-permute-start.2 = (bf16[256,1024]{1,0:T(8,128)(2,1)}, bf16[256,1024]{1,0:T(8,128)(2,1)S(1)}, u32[]{:S(2)}, u32[]{:S(2)}) collective-permute-start(bf16[256,1024]{1,0:T(8,128)(2,1)} %bitcast.17), channel_id=1, source_target_pairs={{0,64},{64,128},{128,192},{192,256},{256,320},{320,384},{384,448},... | collective-permute-start | bytes 1572872 | tf_op jit(solution)/shard_map/ppermute | solution.py:280
  14.0 5.5 %collective-permute-start.3 = (bf16[256,1024]{1,0:T(8,128)(2,1)}, bf16[256,1024]{1,0:T(8,128)(2,1)S(1)}, u32[]{:S(2)}, u32[]{:S(2)}) collective-permute-start(bf16[256,1024]{1,0:T(8,128)(2,1)} %bitcast.18), channel_id=1, source_target_pairs={{0,448},{64,0},{128,64},{192,128},{256,192},{320,256},{384,320},{4... | collective-permute-start | bytes 1572872 | tf_op jit(solution)/shard_map/ppermute | solution.py:280
  19.4 4.0 %pack.1 = bf16[8,8,4,32,128]{4,3,2,1,0:T(8,128)(2,1)} custom-call(bf16[256,1024]{1,0:T(8,128)(2,1)} %bitcast.15, bf16[256,1024]{1,0:T(8,128)(2,1)} %mark.1.refs_1_, bf16[256,1024]{1,0:T(8,128)(2,1)} %bitcast.19, bf16[256,1024]{1,0:T(8,128)(2,1)} %bitcast.21), custom_call_target="tpu_custom_call" | custom-call | flops 262144 | bytes 4194304 | tf_op jit(solution)/shard_map/pack/pallas_call | solution.py:70
  23.4 17.4 %all-to-all-start = ((bf16[64,128,128]{2,1,0:T(8,128)(2,1)}), bf16[64,128,128]{2,1,0:T(8,128)(2,1)}, u32[]{:S(2)}, u32[]{:S(2)}) async-start(bf16[64,128,128]{2,1,0:T(8,128)(2,1)} %bitcast.12), calls=%async_computation | async-start | bytes 4194304 | tf_op jit(solution)/shard_map/all_to_all | solution.py:284
  40.8 0.0 copy-start.2
  40.8 0.0 copy-start.3
  40.9 0.7 copy-done.2
  41.6 0.2 copy-done.3
  41.8 0.2 copy-done.4
  42.0 0.8 copy-done.5
  42.8 19.5 %cross_view.1 = (bf16[256,1024]{1,0:T(8,128)(2,1)}, bf16[256,1024]{1,0:T(8,128)(2,1)}, f32[8,2,256,128]{3,2,1,0:T(8,128)}, bf16[8,2,256,128]{3,2,1,0:T(8,128)(2,1)}, bf16[8,2,256,128]{3,2,1,0:T(8,128)(2,1)}) custom-call(bf16[256,1024]{1,0:T(8,128)(2,1)} %bitcast.16, bf16[256,1024]{1,0:T(8,128)(2,1)} %bitcast.22, bf16[256,1024]{1,0:T(8,128)(2,1)} %copy-done.2, ...), custom_call_target="tpu_custom_call" | custom-call | flops 671088640000 | bytes 12582912 | tf_op jit(solution)/shard_map/cross_view/pallas_call | solution.py:139
  62.2 1.9 %collective-permute-start.4 = (bf16[8,2,256,128]{3,2,1,0:T(8,128)(2,1)}, bf16[8,2,256,128]{3,2,1,0:T(8,128)(2,1)S(1)}, u32[]{:S(2)}, u32[]{:S(2)}) collective-permute-start(bf16[8,2,256,128]{3,2,1,0:T(8,128)(2,1)} %get-tuple-element.22), channel_id=1, source_target_pairs={{0,448},{64,0},{128,64},{192,128},{256,192},{320,256},{384,320},{4... | collective-permute-start | bytes 3145736 | tf_op jit(solution)/shard_map/ppermute | solution.py:280
  64.2 3.4 %collective-permute-start.5 = (bf16[8,2,256,128]{3,2,1,0:T(8,128)(2,1)}, bf16[8,2,256,128]{3,2,1,0:T(8,128)(2,1)S(1)}, u32[]{:S(2)}, u32[]{:S(2)}) collective-permute-start(bf16[8,2,256,128]{3,2,1,0:T(8,128)(2,1)} %get-tuple-element.23), channel_id=1, source_target_pairs={{0,64},{64,128},{128,192},{192,256},{256,320},{320,384},{384,448},... | collective-permute-start | bytes 3145736 | tf_op jit(solution)/shard_map/ppermute | solution.py:280
  67.5 25.9 %all-to-all-done = bf16[64,128,128]{2,1,0:T(8,128)(2,1)} async-done(((bf16[64,128,128]{2,1,0:T(8,128)(2,1)}), bf16[64,128,128]{2,1,0:T(8,128)(2,1)}, u32[]{:S(2)}, u32[]{:S(2)}) %all-to-all-start) | async-done | bytes 2097184 | tf_op jit(solution)/shard_map/all_to_all | solution.py:284
  93.5 6.1 %temporal.1 = bf16[64,4,32,128]{3,2,1,0:T(8,128)(2,1)} custom-call(bf16[64,4,32,128]{3,2,1,0:T(8,128)(2,1)} %bitcast.5.y_ref), custom_call_target="tpu_custom_call" | custom-call | flops 201326592 | bytes 4194304 | tf_op jit(solution)/shard_map/temporal/pallas_call | solution.py:200
  99.6 16.3 %all-to-all-start.1 = ((bf16[64,128,128]{2,1,0:T(8,128)(2,1)}), bf16[64,128,128]{2,1,0:T(8,128)(2,1)}, u32[]{:S(2)}, u32[]{:S(2)}) async-start(bf16[64,128,128]{2,1,0:T(8,128)(2,1)} %bitcast.13), calls=%async_computation.1 | async-start | bytes 4194304 | tf_op jit(solution)/shard_map/all_to_all | solution.py:284
  115.9 1.0 copy-done
  116.9 0.3 copy-done.1
  117.3 4.0 %total.1 = (bf16[256,1024]{1,0:T(8,128)(2,1)}, bf16[256,1024]{1,0:T(8,128)(2,1)}) custom-call(f32[8,2,256,128]{3,2,1,0:T(8,128)} %get-tuple-element.21.own_ref, bf16[8,2,256,128]{3,2,1,0:T(8,128)(2,1)} %copy-done, bf16[8,2,256,128]{3,2,1,0:T(8,128)(2,1)} %copy-done.1), custom_call_target="tpu_custom_call" | custom-call | flops 999999995904 | bytes 6291456 | tf_op jit(solution)/shard_map/total/pallas_call | solution.py:231
  121.3 47.2 %all-to-all-done.1 = bf16[64,128,128]{2,1,0:T(8,128)(2,1)} async-done(((bf16[64,128,128]{2,1,0:T(8,128)(2,1)}), bf16[64,128,128]{2,1,0:T(8,128)(2,1)}, u32[]{:S(2)}, u32[]{:S(2)}) %all-to-all-start.1) | async-done | bytes 2097184 | tf_op jit(solution)/shard_map/all_to_all | solution.py:284
  168.5 6.0 %finish.1 = (bf16[256,1024]{1,0:T(8,128)(2,1)}, bf16[256,1024]{1,0:T(8,128)(2,1)}, bf16[256,1024]{1,0:T(8,128)(2,1)}, bf16[256,1024]{1,0:T(8,128)(2,1)}) custom-call(bf16[8,8,4,32,128]{4,3,2,1,0:T(8,128)(2,1)} %bitcast.7.w_ref, bf16[256,1024]{1,0:T(8,128)(2,1)} %get-tuple-element.19.refs_0_, bf16[256,1024]{1,0:T(8,128)(2,1)} %get-tuple-element.20.refs_1_, ...), custom_call_target="tpu_custom_call" | custom-call | flops 1048576 | bytes 8388608 | tf_op jit(solution)/shard_map/finish/pallas_call | solution.py:263
  (10 shorter events, 0.0 us)
Async XLA Ops:
  3.1 37.7 %collective-permute-start = (bf16[256,1024]{1,0:T(8,128)(2,1)}, bf16[256,1024]{1,0:T(8,128)(2,1)S(1)}, u32[]{:S(2)}, u32[]{:S(2)}) collective-permute-start(bf16[256,1024]{1,0:T(8,128)(2,1)} %mark.1.refs_1_), channel_id=1, source_target_pairs={{0,64},{64,128},{128,192},{192,256},{256,320},{320,384},{384,448},... | collective-permute-start | bytes 1572872 | tf_op jit(solution)/shard_map/ppermute | solution.py:280
  7.0 33.8 %collective-permute-start.1 = (bf16[256,1024]{1,0:T(8,128)(2,1)}, bf16[256,1024]{1,0:T(8,128)(2,1)S(1)}, u32[]{:S(2)}, u32[]{:S(2)}) collective-permute-start(bf16[256,1024]{1,0:T(8,128)(2,1)} %mark.1.refs_1_), channel_id=1, source_target_pairs={{0,448},{64,0},{128,64},{192,128},{256,192},{320,256},{384,320},{4... | collective-permute-start | bytes 1572872 | tf_op jit(solution)/shard_map/ppermute | solution.py:280
  12.0 28.8 %collective-permute-start.2 = (bf16[256,1024]{1,0:T(8,128)(2,1)}, bf16[256,1024]{1,0:T(8,128)(2,1)S(1)}, u32[]{:S(2)}, u32[]{:S(2)}) collective-permute-start(bf16[256,1024]{1,0:T(8,128)(2,1)} %bitcast.17), channel_id=1, source_target_pairs={{0,64},{64,128},{128,192},{192,256},{256,320},{320,384},{384,448},... | collective-permute-start | bytes 1572872 | tf_op jit(solution)/shard_map/ppermute | solution.py:280
  14.0 26.9 %collective-permute-start.3 = (bf16[256,1024]{1,0:T(8,128)(2,1)}, bf16[256,1024]{1,0:T(8,128)(2,1)S(1)}, u32[]{:S(2)}, u32[]{:S(2)}) collective-permute-start(bf16[256,1024]{1,0:T(8,128)(2,1)} %bitcast.18), channel_id=1, source_target_pairs={{0,448},{64,0},{128,64},{192,128},{256,192},{320,256},{384,320},{4... | collective-permute-start | bytes 1572872 | tf_op jit(solution)/shard_map/ppermute | solution.py:280
  23.4 70.0 %all-to-all-start = ((bf16[64,128,128]{2,1,0:T(8,128)(2,1)}), bf16[64,128,128]{2,1,0:T(8,128)(2,1)}, u32[]{:S(2)}, u32[]{:S(2)}) async-start(bf16[64,128,128]{2,1,0:T(8,128)(2,1)} %bitcast.12), calls=%async_computation | async-start | bytes 4194304 | tf_op jit(solution)/shard_map/all_to_all | solution.py:284
  40.8 0.8 copy-start.2
  40.8 0.9 copy-start.3
  40.9 1.1 copy-start.4
  42.0 0.8 copy-start.5
  62.2 53.7 %collective-permute-start.4 = (bf16[8,2,256,128]{3,2,1,0:T(8,128)(2,1)}, bf16[8,2,256,128]{3,2,1,0:T(8,128)(2,1)S(1)}, u32[]{:S(2)}, u32[]{:S(2)}) collective-permute-start(bf16[8,2,256,128]{3,2,1,0:T(8,128)(2,1)} %get-tuple-element.22), channel_id=1, source_target_pairs={{0,448},{64,0},{128,64},{192,128},{256,192},{320,256},{384,320},{4... | collective-permute-start | bytes 3145736 | tf_op jit(solution)/shard_map/ppermute | solution.py:280
  64.2 51.8 %collective-permute-start.5 = (bf16[8,2,256,128]{3,2,1,0:T(8,128)(2,1)}, bf16[8,2,256,128]{3,2,1,0:T(8,128)(2,1)S(1)}, u32[]{:S(2)}, u32[]{:S(2)}) collective-permute-start(bf16[8,2,256,128]{3,2,1,0:T(8,128)(2,1)} %get-tuple-element.23), channel_id=1, source_target_pairs={{0,64},{64,128},{128,192},{192,256},{256,320},{320,384},{384,448},... | collective-permute-start | bytes 3145736 | tf_op jit(solution)/shard_map/ppermute | solution.py:280
  99.6 68.9 %all-to-all-start.1 = ((bf16[64,128,128]{2,1,0:T(8,128)(2,1)}), bf16[64,128,128]{2,1,0:T(8,128)(2,1)}, u32[]{:S(2)}, u32[]{:S(2)}) async-start(bf16[64,128,128]{2,1,0:T(8,128)(2,1)} %bitcast.13), calls=%async_computation.1 | async-start | bytes 4194304 | tf_op jit(solution)/shard_map/all_to_all | solution.py:284
  115.9 1.0 copy-start
  115.9 1.3 copy-start.1

commit v6 on v5

--- a/solution.py
+++ b/solution.py
@@ -65,7 +65,7 @@
     pairs = width // PAIR
     blocks = frames // pairs
     rows = length // blocks
-    per_step = 2
+    per_step = 4
     row_spec = pl.BlockSpec((per_step * rows, width), lambda i: (i, 0))
     return pl.pallas_call(
         pack_kernel,
@@ -258,7 +258,7 @@
 def finish(returned, *cross_parts):
     length, width = cross_parts[0].shape
     blocks, pairs, _, rows, _ = returned.shape
-    per_step = 1
+    per_step = 4
     row_spec = pl.BlockSpec((per_step * rows, width), lambda i: (i, 0))
     return pl.pallas_call(
         finish_kernel,

time: 175 us -> 172 us (0.983)
  Pallas kernels: 41.4 us -> 37.5 us
    pallas_call x1, Pallas kernels: 6.05 us -> 3.35 us  [finish(): pl.pallas_call(finish_kernel, grid=(blocks // per_step,), in_specs=[pl.Bl...]
where the time goes in v6:
time: 172 us; the launch traced here: 171 us
  waiting for transfers between devices  73.2 us (43%)
  starting transfers between devices  55.9 us (32%)
  Pallas kernels  37.5 us (22%)
  local copies, waits for them, and re-layouts  3.21 us (2%)
    all_to_all x2, waiting for transfers between devices, exchange(): lax.all_to_all(blocks, 'frame', split_axis=0, concat_axis=0, tiled=True)  73.2 us
    all_to_all x2, starting transfers between devices, exchange(): lax.all_to_all(blocks, 'frame', split_axis=0, concat_axis=0, tiled=True)  34.3 us
    ppermute x6, starting transfers between devices, from_behind(): lax.ppermute(shard, axis, [(i, (i + by) % devices) for i in range(devices)])  21.6 us
    pallas_call x1, Pallas kernels, cross(): pl.pallas_call(cross_kernel, grid=(pairs,), in_specs=[column_spec] * 8, o...  19.5 us
    pallas_call x1, Pallas kernels, temporal(): pl.pallas_call(temporal_kernel, grid=(positions // per_step,), in_specs=[...  6.12 us
    pallas_call x1, Pallas kernels, total(): pl.pallas_call(total_kernel, grid=(pairs // per_step,), in_specs=[pair_sp...  4.04 us
  transfers between devices with their start and end apart: 8, of which 2 were waited for; matrix products, arithmetic and copies ran while one was open for 0% of the time, Pallas kernels for 19%

profile of v6, /device:TPU:1, one launch (start us, length us, event | category | flops | bytes accessed | tf_op | source)
XLA Modules:
  0.0 171.3 jit_solution(12872653227715754565)
XLA Ops:
  1.3 1.8 %mark.1.refs_1_ = bf16[256,1024]{1,0:T(8,128)(2,1)} custom-call(s32[1,1]{1,0:T(1,128)S(6)} %copy.9.count_ref, bf16[256,1024]{1,0:T(8,128)(2,1)} %bitcast.14), custom_call_target="tpu_custom_call" | custom-call | flops 262144 | bytes 1048576 | tf_op jit(solution)/shard_map/mark/pallas_call | solution.py:40
  3.1 3.9 %collective-permute-start = (bf16[256,1024]{1,0:T(8,128)(2,1)}, bf16[256,1024]{1,0:T(8,128)(2,1)S(1)}, u32[]{:S(2)}, u32[]{:S(2)}) collective-permute-start(bf16[256,1024]{1,0:T(8,128)(2,1)} %mark.1.refs_1_), channel_id=1, source_target_pairs={{0,64},{64,128},{128,192},{192,256},{256,320},{320,384},{384,448},... | collective-permute-start | bytes 1572872 | tf_op jit(solution)/shard_map/ppermute | solution.py:280
  7.0 5.0 %collective-permute-start.1 = (bf16[256,1024]{1,0:T(8,128)(2,1)}, bf16[256,1024]{1,0:T(8,128)(2,1)S(1)}, u32[]{:S(2)}, u32[]{:S(2)}) collective-permute-start(bf16[256,1024]{1,0:T(8,128)(2,1)} %mark.1.refs_1_), channel_id=1, source_target_pairs={{0,448},{64,0},{128,64},{192,128},{256,192},{320,256},{384,320},{4... | collective-permute-start | bytes 1572872 | tf_op jit(solution)/shard_map/ppermute | solution.py:280
  12.0 1.9 %collective-permute-start.2 = (bf16[256,1024]{1,0:T(8,128)(2,1)}, bf16[256,1024]{1,0:T(8,128)(2,1)S(1)}, u32[]{:S(2)}, u32[]{:S(2)}) collective-permute-start(bf16[256,1024]{1,0:T(8,128)(2,1)} %bitcast.17), channel_id=1, source_target_pairs={{0,64},{64,128},{128,192},{192,256},{256,320},{320,384},{384,448},... | collective-permute-start | bytes 1572872 | tf_op jit(solution)/shard_map/ppermute | solution.py:280
  14.0 5.5 %collective-permute-start.3 = (bf16[256,1024]{1,0:T(8,128)(2,1)}, bf16[256,1024]{1,0:T(8,128)(2,1)S(1)}, u32[]{:S(2)}, u32[]{:S(2)}) collective-permute-start(bf16[256,1024]{1,0:T(8,128)(2,1)} %bitcast.18), channel_id=1, source_target_pairs={{0,448},{64,0},{128,64},{192,128},{256,192},{320,256},{384,320},{4... | collective-permute-start | bytes 1572872 | tf_op jit(solution)/shard_map/ppermute | solution.py:280
  19.4 2.8 %pack.1 = bf16[8,8,4,32,128]{4,3,2,1,0:T(8,128)(2,1)} custom-call(bf16[256,1024]{1,0:T(8,128)(2,1)} %bitcast.15, bf16[256,1024]{1,0:T(8,128)(2,1)} %mark.1.refs_1_, bf16[256,1024]{1,0:T(8,128)(2,1)} %bitcast.19, bf16[256,1024]{1,0:T(8,128)(2,1)} %bitcast.21), custom_call_target="tpu_custom_call" | custom-call | flops 262144 | bytes 4194304 | tf_op jit(solution)/shard_map/pack/pallas_call | solution.py:70
  22.2 17.4 %all-to-all-start = ((bf16[64,128,128]{2,1,0:T(8,128)(2,1)}), bf16[64,128,128]{2,1,0:T(8,128)(2,1)}, u32[]{:S(2)}, u32[]{:S(2)}) async-start(bf16[64,128,128]{2,1,0:T(8,128)(2,1)} %bitcast.12), calls=%async_computation | async-start | bytes 4194304 | tf_op jit(solution)/shard_map/all_to_all | solution.py:284
  39.6 0.0 copy-start.2
  39.6 0.0 copy-start.4
  39.7 0.7 copy-done.2
  40.4 0.2 copy-done.3
  40.6 0.2 copy-done.4
  40.7 0.8 copy-done.5
  41.5 19.5 %cross_view.1 = (bf16[256,1024]{1,0:T(8,128)(2,1)}, bf16[256,1024]{1,0:T(8,128)(2,1)}, f32[8,2,256,128]{3,2,1,0:T(8,128)}, bf16[8,2,256,128]{3,2,1,0:T(8,128)(2,1)}, bf16[8,2,256,128]{3,2,1,0:T(8,128)(2,1)}) custom-call(bf16[256,1024]{1,0:T(8,128)(2,1)} %bitcast.16, bf16[256,1024]{1,0:T(8,128)(2,1)} %bitcast.22, bf16[256,1024]{1,0:T(8,128)(2,1)} %copy-done.2, ...), custom_call_target="tpu_custom_call" | custom-call | flops 671088640000 | bytes 12582912 | tf_op jit(solution)/shard_map/cross_view/pallas_call | solution.py:139
  61.0 1.9 %collective-permute-start.4 = (bf16[8,2,256,128]{3,2,1,0:T(8,128)(2,1)}, bf16[8,2,256,128]{3,2,1,0:T(8,128)(2,1)S(1)}, u32[]{:S(2)}, u32[]{:S(2)}) collective-permute-start(bf16[8,2,256,128]{3,2,1,0:T(8,128)(2,1)} %get-tuple-element.22), channel_id=1, source_target_pairs={{0,448},{64,0},{128,64},{192,128},{256,192},{320,256},{384,320},{4... | collective-permute-start | bytes 3145736 | tf_op jit(solution)/shard_map/ppermute | solution.py:280
  62.9 3.4 %collective-permute-start.5 = (bf16[8,2,256,128]{3,2,1,0:T(8,128)(2,1)}, bf16[8,2,256,128]{3,2,1,0:T(8,128)(2,1)S(1)}, u32[]{:S(2)}, u32[]{:S(2)}) collective-permute-start(bf16[8,2,256,128]{3,2,1,0:T(8,128)(2,1)} %get-tuple-element.23), channel_id=1, source_target_pairs={{0,64},{64,128},{128,192},{192,256},{256,320},{320,384},{384,448},... | collective-permute-start | bytes 3145736 | tf_op jit(solution)/shard_map/ppermute | solution.py:280
  66.3 25.9 %all-to-all-done = bf16[64,128,128]{2,1,0:T(8,128)(2,1)} async-done(((bf16[64,128,128]{2,1,0:T(8,128)(2,1)}), bf16[64,128,128]{2,1,0:T(8,128)(2,1)}, u32[]{:S(2)}, u32[]{:S(2)}) %all-to-all-start) | async-done | bytes 2097184 | tf_op jit(solution)/shard_map/all_to_all | solution.py:284
  92.2 6.1 %temporal.1 = bf16[64,4,32,128]{3,2,1,0:T(8,128)(2,1)} custom-call(bf16[64,4,32,128]{3,2,1,0:T(8,128)(2,1)} %bitcast.5.y_ref), custom_call_target="tpu_custom_call" | custom-call | flops 201326592 | bytes 4194304 | tf_op jit(solution)/shard_map/temporal/pallas_call | solution.py:200
  98.4 16.9 %all-to-all-start.1 = ((bf16[64,128,128]{2,1,0:T(8,128)(2,1)}), bf16[64,128,128]{2,1,0:T(8,128)(2,1)}, u32[]{:S(2)}, u32[]{:S(2)}) async-start(bf16[64,128,128]{2,1,0:T(8,128)(2,1)} %bitcast.13), calls=%async_computation.1 | async-start | bytes 4194304 | tf_op jit(solution)/shard_map/all_to_all | solution.py:284
  115.3 1.0 copy-done
  116.3 0.3 copy-done.1
  116.7 4.0 %total.1 = (bf16[256,1024]{1,0:T(8,128)(2,1)}, bf16[256,1024]{1,0:T(8,128)(2,1)}) custom-call(f32[8,2,256,128]{3,2,1,0:T(8,128)} %get-tuple-element.21.own_ref, bf16[8,2,256,128]{3,2,1,0:T(8,128)(2,1)} %copy-done, bf16[8,2,256,128]{3,2,1,0:T(8,128)(2,1)} %copy-done.1), custom_call_target="tpu_custom_call" | custom-call | flops 999999995904 | bytes 6291456 | tf_op jit(solution)/shard_map/total/pallas_call | solution.py:231
  120.7 47.2 %all-to-all-done.1 = bf16[64,128,128]{2,1,0:T(8,128)(2,1)} async-done(((bf16[64,128,128]{2,1,0:T(8,128)(2,1)}), bf16[64,128,128]{2,1,0:T(8,128)(2,1)}, u32[]{:S(2)}, u32[]{:S(2)}) %all-to-all-start.1) | async-done | bytes 2097184 | tf_op jit(solution)/shard_map/all_to_all | solution.py:284
  167.9 3.3 %finish.1 = (bf16[256,1024]{1,0:T(8,128)(2,1)}, bf16[256,1024]{1,0:T(8,128)(2,1)}, bf16[256,1024]{1,0:T(8,128)(2,1)}, bf16[256,1024]{1,0:T(8,128)(2,1)}) custom-call(bf16[8,8,4,32,128]{4,3,2,1,0:T(8,128)(2,1)} %bitcast.7.w_ref, bf16[256,1024]{1,0:T(8,128)(2,1)} %get-tuple-element.19.refs_0_, bf16[256,1024]{1,0:T(8,128)(2,1)} %get-tuple-element.20.refs_1_, ...), custom_call_target="tpu_custom_call" | custom-call | flops 1048576 | bytes 8388608 | tf_op jit(solution)/shard_map/finish/pallas_call | solution.py:263
  (10 shorter events, 0.0 us)
Async XLA Ops:
  3.1 36.5 %collective-permute-start = (bf16[256,1024]{1,0:T(8,128)(2,1)}, bf16[256,1024]{1,0:T(8,128)(2,1)S(1)}, u32[]{:S(2)}, u32[]{:S(2)}) collective-permute-start(bf16[256,1024]{1,0:T(8,128)(2,1)} %mark.1.refs_1_), channel_id=1, source_target_pairs={{0,64},{64,128},{128,192},{192,256},{256,320},{320,384},{384,448},... | collective-permute-start | bytes 1572872 | tf_op jit(solution)/shard_map/ppermute | solution.py:280
  7.0 32.6 %collective-permute-start.1 = (bf16[256,1024]{1,0:T(8,128)(2,1)}, bf16[256,1024]{1,0:T(8,128)(2,1)S(1)}, u32[]{:S(2)}, u32[]{:S(2)}) collective-permute-start(bf16[256,1024]{1,0:T(8,128)(2,1)} %mark.1.refs_1_), channel_id=1, source_target_pairs={{0,448},{64,0},{128,64},{192,128},{256,192},{320,256},{384,320},{4... | collective-permute-start | bytes 1572872 | tf_op jit(solution)/shard_map/ppermute | solution.py:280
  12.0 27.6 %collective-permute-start.2 = (bf16[256,1024]{1,0:T(8,128)(2,1)}, bf16[256,1024]{1,0:T(8,128)(2,1)S(1)}, u32[]{:S(2)}, u32[]{:S(2)}) collective-permute-start(bf16[256,1024]{1,0:T(8,128)(2,1)} %bitcast.17), channel_id=1, source_target_pairs={{0,64},{64,128},{128,192},{192,256},{256,320},{320,384},{384,448},... | collective-permute-start | bytes 1572872 | tf_op jit(solution)/shard_map/ppermute | solution.py:280
  14.0 25.7 %collective-permute-start.3 = (bf16[256,1024]{1,0:T(8,128)(2,1)}, bf16[256,1024]{1,0:T(8,128)(2,1)S(1)}, u32[]{:S(2)}, u32[]{:S(2)}) collective-permute-start(bf16[256,1024]{1,0:T(8,128)(2,1)} %bitcast.18), channel_id=1, source_target_pairs={{0,448},{64,0},{128,64},{192,128},{256,192},{320,256},{384,320},{4... | collective-permute-start | bytes 1572872 | tf_op jit(solution)/shard_map/ppermute | solution.py:280
  22.2 70.0 %all-to-all-start = ((bf16[64,128,128]{2,1,0:T(8,128)(2,1)}), bf16[64,128,128]{2,1,0:T(8,128)(2,1)}, u32[]{:S(2)}, u32[]{:S(2)}) async-start(bf16[64,128,128]{2,1,0:T(8,128)(2,1)} %bitcast.12), calls=%async_computation | async-start | bytes 4194304 | tf_op jit(solution)/shard_map/all_to_all | solution.py:284
  39.6 0.8 copy-start.2
  39.6 0.9 copy-start.3
  39.6 1.1 copy-start.4
  40.7 0.8 copy-start.5
  61.0 54.3 %collective-permute-start.4 = (bf16[8,2,256,128]{3,2,1,0:T(8,128)(2,1)}, bf16[8,2,256,128]{3,2,1,0:T(8,128)(2,1)S(1)}, u32[]{:S(2)}, u32[]{:S(2)}) collective-permute-start(bf16[8,2,256,128]{3,2,1,0:T(8,128)(2,1)} %get-tuple-element.22), channel_id=1, source_target_pairs={{0,448},{64,0},{128,64},{192,128},{256,192},{320,256},{384,320},{4... | collective-permute-start | bytes 3145736 | tf_op jit(solution)/shard_map/ppermute | solution.py:280
  62.9 52.4 %collective-permute-start.5 = (bf16[8,2,256,128]{3,2,1,0:T(8,128)(2,1)}, bf16[8,2,256,128]{3,2,1,0:T(8,128)(2,1)S(1)}, u32[]{:S(2)}, u32[]{:S(2)}) collective-permute-start(bf16[8,2,256,128]{3,2,1,0:T(8,128)(2,1)} %get-tuple-element.23), channel_id=1, source_target_pairs={{0,64},{64,128},{128,192},{192,256},{256,320},{320,384},{384,448},... | collective-permute-start | bytes 3145736 | tf_op jit(solution)/shard_map/ppermute | solution.py:280
  98.4 69.6 %all-to-all-start.1 = ((bf16[64,128,128]{2,1,0:T(8,128)(2,1)}), bf16[64,128,128]{2,1,0:T(8,128)(2,1)}, u32[]{:S(2)}, u32[]{:S(2)}) async-start(bf16[64,128,128]{2,1,0:T(8,128)(2,1)} %bitcast.13), calls=%async_computation.1 | async-start | bytes 4194304 | tf_op jit(solution)/shard_map/all_to_all | solution.py:284
  115.3 1.0 copy-start
  115.3 1.3 copy-start.1
